TPU v7x, 32 devices: a whole 2x2x4 slice. The times are simulated.
32 devices in a mesh: stream: 2 (over x), dp: 16 (over z, y, core).
Axes of the slice: x: 2, y: 2, z: 4, core: 2. Of those that a mesh axis runs over, the one named last changes fastest.
Arguments:
- text_in: bfloat16 [32768, 768], P(('stream', 'dp')), may hold values from -6 to 6
- image_in: bfloat16 [9216, 1024], P(('stream', 'dp')), may hold values from -6 to 6
- lengths: int32 [256], P(('stream', 'dp')), may hold values from 16 to 128, as said below
- t_proj: bfloat16 [768, 8448], P(('stream', 'dp')), may hold values from -0.21875 to 0.21875
- t_out: bfloat16 [4864, 768], P(('stream', 'dp'))
- t_bias_wide: bfloat16 [5120], P(('stream', 'dp')), may hold values from -3 to 3
- t_bias: bfloat16 [8, 768], P(None, ('stream', 'dp')), may hold values from -3 to 3
- t_gain: bfloat16 [3, 768], P(None, ('stream', 'dp')), may hold values from 0.25 to 1.75
- i_proj: bfloat16 [1024, 7168], P(('stream', 'dp')), may hold values from -0.1875 to 0.1875
- i_out: bfloat16 [3072, 1024], P(('stream', 'dp'))
- i_bias_wide: bfloat16 [3072], P(('stream', 'dp')), may hold values from -3 to 3
- i_bias: bfloat16 [8, 1024], P(None, ('stream', 'dp')), may hold values from -3 to 3
- i_gain: bfloat16 [3, 1024], P(None, ('stream', 'dp')), may hold values from 0.25 to 1.75
- text_cot: bfloat16 [32768, 768], P(('stream', 'dp')), may hold values from -6 to 6
- image_cot: bfloat16 [9216, 1024], P(('stream', 'dp')), may hold values from -6 to 6
Outputs:
- text_out: float32 [32768, 768], P(('stream', 'dp'))
- image_out: float32 [9216, 1024], P(('stream', 'dp'))
- text_grad: float32 [32768, 768], P(('stream', 'dp'))
- image_grad: float32 [9216, 1024], P(('stream', 'dp'))
- t_proj_grad: float32 [768, 8448], P(('stream', 'dp'))
- t_out_grad: float32 [4864, 768], P(('stream', 'dp'))
- t_bias_wide_grad: float32 [5120], P(('stream', 'dp'))
- t_bias_grad: float32 [8, 768], P(None, ('stream', 'dp'))
- t_gain_grad: float32 [3, 768], P(None, ('stream', 'dp'))
- i_proj_grad: float32 [1024, 7168], P(('stream', 'dp'))
- i_out_grad: float32 [3072, 1024], P(('stream', 'dp'))
- i_bias_wide_grad: float32 [3072], P(('stream', 'dp'))
- i_bias_grad: float32 [8, 1024], P(None, ('stream', 'dp'))
- i_gain_grad: float32 [3, 1024], P(None, ('stream', 'dp'))
Inputs may be any that keep to these rules, and one draw needn't show every extreme that they name: `lengths`: some caption has 128 tokens and some has 16.
All inputs are finite; a program needn't handle non-finite values.
Results may differ from a plain program's by a relative error of at most 0.019.
Values may be sent and summed in bfloat16 or wider, within the bound.
No kernel may reach another device: no remote copies, remote signals or barrier semaphores. Data moves between devices by JAX's collectives and lax.ppermute only.
A program may use at most 320 MiB of HBM per device.

v0:
```python
import functools

import jax
import jax.numpy as jnp
from jax import lax
from jax.sharding import PartitionSpec as P

CO_W = 1024
HEADS_T = 12
HEADS_I = 8
CO_HEADS = 8
CAP = 128
REGIONS = 36


epsilon = 1e-05
negative = -1e30


def partner(block, axis, distance):
    count = lax.axis_size(axis)
    route = []
    for low in range(count):
        high = low | 1 << distance
        if high != low and high < count:
            route += [(low, high), (high, low)]
    return lax.ppermute(block, axis, route)


def forward_dot(left_side, right_side):
    return jnp.dot(left_side, right_side, preferred_element_type=jnp.float32)


def weight_grad(inputs, upstream):
    return jnp.einsum("rk,rn->kn", inputs, upstream, preferred_element_type=jnp.float32)


def input_grad(upstream, weight):
    return jnp.einsum("rn,kn->rk", upstream, weight, preferred_element_type=jnp.float32)


def layer_norm(pre_norm, gain_row, beta_row):
    average = jnp.mean(pre_norm, -1, keepdims=True)
    centered = pre_norm - average
    inverse = lax.rsqrt(jnp.mean(centered * centered, -1, keepdims=True) + epsilon)
    normed = centered * inverse
    return (normed * gain_row + beta_row, normed, inverse)


def norm_back(upstream, gain_row, normed, inverse):
    scaled = upstream * gain_row
    bracket = (
        scaled
        - jnp.mean(scaled, -1, keepdims=True)
        - normed * jnp.mean(scaled * normed, -1, keepdims=True)
    )
    return (inverse * bracket, jnp.sum(upstream * normed, 0), jnp.sum(upstream, 0))


def split_heads(flat_rows, groups, head_count):
    return flat_rows.reshape(
        groups, flat_rows.shape[0] // groups, head_count, flat_rows.shape[1] // head_count
    )


def head_scores(queries, key_rows, mask_add, head_count):
    groups = mask_add.shape[0]
    query_heads = split_heads(queries, groups, head_count)
    key_heads = split_heads(key_rows, groups, head_count)
    factor = query_heads.shape[-1] ** (-0.5)
    scores = (
        jnp.einsum("gqhd,gkhd->ghqk", query_heads, key_heads, preferred_element_type=jnp.float32)
        * factor
        + mask_add[:, None, None, :]
    )
    return (scores, query_heads, key_heads, factor)


def attend_forward(queries, key_rows, values, mask_add, head_count):
    scores, query_heads, key_heads, factor = head_scores(queries, key_rows, mask_add, head_count)
    value_heads = split_heads(values, mask_add.shape[0], head_count)
    highest = jnp.max(scores, -1, keepdims=True)
    exponent = jnp.exp(scores - highest)
    totals = jnp.sum(exponent, -1, keepdims=True)
    weights = (exponent / totals).astype(jnp.bfloat16)
    context = jnp.einsum(
        "ghqk,gkhd->gqhd", weights, value_heads, preferred_element_type=jnp.float32
    )
    return (context.reshape(queries.shape[0], -1).astype(jnp.bfloat16), highest + jnp.log(totals))


def attend_backward(queries, key_rows, values, mask_add, head_count, log_total, context_grad):
    groups = mask_add.shape[0]
    scores, query_heads, key_heads, factor = head_scores(queries, key_rows, mask_add, head_count)
    value_heads = split_heads(values, groups, head_count)
    weights = jnp.exp(scores - log_total)
    upstream = split_heads(context_grad.astype(jnp.bfloat16), groups, head_count)
    values_grad = jnp.einsum(
        "ghqk,gqhd->gkhd",
        weights.astype(jnp.bfloat16),
        upstream,
        preferred_element_type=jnp.float32,
    )
    weights_grad = jnp.einsum(
        "gqhd,gkhd->ghqk", upstream, value_heads, preferred_element_type=jnp.float32
    )
    scores_grad = weights * (weights_grad - jnp.sum(weights * weights_grad, -1, keepdims=True))
    rounded = (scores_grad * factor).astype(jnp.bfloat16)
    queries_grad = jnp.einsum(
        "ghqk,gkhd->gqhd", rounded, key_heads, preferred_element_type=jnp.float32
    )
    keys_grad = jnp.einsum(
        "ghqk,gqhd->gkhd", rounded, query_heads, preferred_element_type=jnp.float32
    )
    return (
        queries_grad.reshape(queries.shape[0], -1),
        keys_grad.reshape(key_rows.shape[0], -1),
        values_grad.reshape(values.shape[0], -1),
    )


def co_inputs(inputs, proj_weight, wide_bias):
    bias_float = wide_bias.astype(jnp.float32)
    queries = (forward_dot(inputs, proj_weight[:, :CO_W]) + bias_float[:CO_W]).astype(jnp.bfloat16)
    pair_bias = jnp.concatenate([jnp.zeros((CO_W,), jnp.float32), bias_float[CO_W : 2 * CO_W]])
    pair_kv = (forward_dot(inputs, proj_weight[:, CO_W : 3 * CO_W]) + pair_bias).astype(
        jnp.bfloat16
    )
    return (queries, pair_kv)


def stream_forward(
    context,
    residual,
    proj_weight,
    out_weight,
    wide_bias,
    bias_rows,
    gain_rows,
    mask_add,
    head_count,
):
    features = residual.shape[1]
    bias_float = bias_rows.astype(jnp.float32)
    gain_float = gain_rows.astype(jnp.float32)
    first_norm, normed_one, inverse_one = layer_norm(
        residual + forward_dot(context, out_weight[:CO_W]) + bias_float[0],
        gain_float[0],
        bias_float[1],
    )
    first_low = first_norm.astype(jnp.bfloat16)
    triple_bias = jnp.concatenate(
        [bias_float[2], jnp.zeros((features,), jnp.float32), bias_float[3]]
    )
    triple = (
        forward_dot(first_low, proj_weight[:, 3 * CO_W : 3 * CO_W + 3 * features]) + triple_bias
    ).astype(jnp.bfloat16)
    attended, attend_total = attend_forward(
        triple[:, :features],
        triple[:, features : 2 * features],
        triple[:, 2 * features :],
        mask_add,
        head_count,
    )
    second_norm, normed_two, inverse_two = layer_norm(
        first_norm + forward_dot(attended, out_weight[CO_W : CO_W + features]) + bias_float[4],
        gain_float[1],
        bias_float[5],
    )
    second_low = second_norm.astype(jnp.bfloat16)
    hidden = (
        forward_dot(second_low, proj_weight[:, 3 * CO_W + 3 * features :])
        + wide_bias.astype(jnp.float32)[2 * CO_W :]
    )
    active_low = jax.nn.gelu(hidden, approximate=False).astype(jnp.bfloat16)
    output, normed_three, inverse_three = layer_norm(
        second_norm + forward_dot(active_low, out_weight[CO_W + features :]) + bias_float[6],
        gain_float[2],
        bias_float[7],
    )
    saved = (
        first_low,
        triple,
        attended,
        attend_total,
        second_low,
        hidden,
        active_low,
        normed_one,
        inverse_one,
        normed_two,
        inverse_two,
        normed_three,
        inverse_three,
    )
    return (output, saved)


def stream_backward(
    upstream, context, saved, proj_weight, out_weight, gain_rows, mask_add, head_count
):
    (
        first_low,
        triple,
        attended,
        attend_total,
        second_low,
        hidden,
        active_low,
        normed_one,
        inverse_one,
        normed_two,
        inverse_two,
        normed_three,
        inverse_three,
    ) = saved
    features = first_low.shape[1]
    gain_float = gain_rows.astype(jnp.float32)
    third_grad, gain_three, beta_three = norm_back(
        upstream, gain_float[2], normed_three, inverse_three
    )
    third_low = third_grad.astype(jnp.bfloat16)
    down_grad = weight_grad(active_low, third_low)
    active_grad = input_grad(third_low, out_weight[CO_W + features :])
    unused, gelu_pull = jax.vjp(functools.partial(jax.nn.gelu, approximate=False), hidden)
    hidden_grad = gelu_pull(active_grad)[0]
    hidden_low = hidden_grad.astype(jnp.bfloat16)
    up_grad = weight_grad(second_low, hidden_low)
    second_in = third_grad + input_grad(hidden_low, proj_weight[:, 3 * CO_W + 3 * features :])
    second_grad, gain_two, beta_two = norm_back(second_in, gain_float[1], normed_two, inverse_two)
    second_round = second_grad.astype(jnp.bfloat16)
    self_out_grad = weight_grad(attended, second_round)
    attended_grad = input_grad(second_round, out_weight[CO_W : CO_W + features])
    query_grad, key_grad, value_grad = attend_backward(
        triple[:, :features],
        triple[:, features : 2 * features],
        triple[:, 2 * features :],
        mask_add,
        head_count,
        attend_total,
        attended_grad,
    )
    triple_low = jnp.concatenate([query_grad, key_grad, value_grad], 1).astype(jnp.bfloat16)
    triple_grad = weight_grad(first_low, triple_low)
    triple_sums = jnp.sum(triple_low.astype(jnp.float32), 0)
    first_in = second_grad + input_grad(
        triple_low, proj_weight[:, 3 * CO_W : 3 * CO_W + 3 * features]
    )
    first_grad, gain_one, beta_one = norm_back(first_in, gain_float[0], normed_one, inverse_one)
    first_round = first_grad.astype(jnp.bfloat16)
    co_out_grad = weight_grad(context, first_round)
    context_grad = input_grad(first_round, out_weight[:CO_W])
    bias_parts = (
        jnp.sum(first_grad, 0),
        beta_one,
        triple_sums[:features],
        triple_sums[2 * features :],
        jnp.sum(second_grad, 0),
        beta_two,
        jnp.sum(third_grad, 0),
        beta_three,
    )
    return (
        first_grad,
        context_grad,
        (
            (triple_grad, up_grad),
            (co_out_grad, self_out_grad, down_grad),
            jnp.sum(hidden_grad, 0),
            bias_parts,
            (gain_one, gain_two, gain_three),
        ),
    )


def co_backward(inputs, proj_weight, queries_grad, pair_grad, residual_grad):
    query_round = queries_grad.astype(jnp.bfloat16)
    rows_grad = (
        residual_grad
        + input_grad(query_round, proj_weight[:, :CO_W])
        + input_grad(pair_grad, proj_weight[:, CO_W : 3 * CO_W])
    )
    parts = (
        weight_grad(inputs, query_round),
        weight_grad(inputs, pair_grad),
        jnp.sum(query_round.astype(jnp.float32), 0),
        jnp.sum(pair_grad[:, CO_W:].astype(jnp.float32), 0),
    )
    return (rows_grad, parts)


def pack_grads(co_parts, stream_parts):
    query_weight, pair_weight, query_bias, value_bias = co_parts
    (
        (triple_grad, up_grad),
        (co_out_grad, self_out_grad, down_grad),
        up_bias,
        bias_parts,
        gain_parts,
    ) = stream_parts
    return (
        jnp.concatenate([query_weight, pair_weight, triple_grad, up_grad], 1),
        jnp.concatenate([co_out_grad, self_out_grad, down_grad], 0),
        jnp.concatenate([query_bias, value_bias, up_bias]),
        jnp.stack(bias_parts),
        jnp.stack(gain_parts),
    )


def shards(
    text_in,
    image_in,
    lengths,
    t_proj,
    t_out,
    t_bias_wide,
    t_bias,
    t_gain,
    i_proj,
    i_out,
    i_bias_wide,
    i_bias,
    i_gain,
    text_cot,
    image_cot,
):
    gathered = (
        lax.all_gather(t_proj, ("stream", "dp"), axis=0, tiled=True),
        lax.all_gather(t_out, ("stream", "dp"), axis=0, tiled=True),
        lax.all_gather(t_bias_wide, ("stream", "dp"), axis=0, tiled=True),
        lax.all_gather(t_bias, ("stream", "dp"), axis=1, tiled=True),
        lax.all_gather(t_gain, ("stream", "dp"), axis=1, tiled=True),
        lax.all_gather(i_proj, ("stream", "dp"), axis=0, tiled=True),
        lax.all_gather(i_out, ("stream", "dp"), axis=0, tiled=True),
        lax.all_gather(i_bias_wide, ("stream", "dp"), axis=0, tiled=True),
        lax.all_gather(i_bias, ("stream", "dp"), axis=1, tiled=True),
        lax.all_gather(i_gain, ("stream", "dp"), axis=1, tiled=True),
    )
    pair_count = lengths.shape[0]
    present = lax.broadcasted_iota(jnp.int32, (pair_count, CAP), 1) < lengths[:, None]
    text_mask = jnp.where(present, 0.0, negative).astype(jnp.float32)
    image_mask = jnp.zeros((pair_count, REGIONS), jnp.float32)
    text_query, text_kv = co_inputs(text_in, gathered[0], gathered[2])
    image_query, image_kv = co_inputs(image_in, gathered[5], gathered[7])
    far_text_kv, far_image_kv, far_present = partner(
        (text_kv, image_kv, present.astype(jnp.bfloat16)), "stream", 0
    )
    far_mask = jnp.where(far_present > 0.5, 0.0, negative).astype(jnp.float32)
    text_context, text_total = attend_forward(
        text_query, far_image_kv[:, :CO_W], far_image_kv[:, CO_W:], image_mask, CO_HEADS
    )
    image_context, image_total = attend_forward(
        image_query, far_text_kv[:, :CO_W], far_text_kv[:, CO_W:], far_mask, CO_HEADS
    )
    text_final, text_saved = stream_forward(
        text_context,
        text_in.astype(jnp.float32),
        gathered[0],
        gathered[1],
        gathered[2],
        gathered[3],
        gathered[4],
        text_mask,
        HEADS_T,
    )
    image_final, image_saved = stream_forward(
        image_context,
        image_in.astype(jnp.float32),
        gathered[5],
        gathered[6],
        gathered[7],
        gathered[8],
        gathered[9],
        image_mask,
        HEADS_I,
    )
    params_back = (
        lax.all_gather(t_proj, ("stream", "dp"), axis=0, tiled=True),
        lax.all_gather(t_out, ("stream", "dp"), axis=0, tiled=True),
        lax.all_gather(t_bias_wide, ("stream", "dp"), axis=0, tiled=True),
        lax.all_gather(t_bias, ("stream", "dp"), axis=1, tiled=True),
        lax.all_gather(t_gain, ("stream", "dp"), axis=1, tiled=True),
        lax.all_gather(i_proj, ("stream", "dp"), axis=0, tiled=True),
        lax.all_gather(i_out, ("stream", "dp"), axis=0, tiled=True),
        lax.all_gather(i_bias_wide, ("stream", "dp"), axis=0, tiled=True),
        lax.all_gather(i_bias, ("stream", "dp"), axis=1, tiled=True),
        lax.all_gather(i_gain, ("stream", "dp"), axis=1, tiled=True),
    )
    text_residual, text_context_grad, text_parts = stream_backward(
        text_cot.astype(jnp.float32),
        text_context,
        text_saved,
        params_back[0],
        params_back[1],
        params_back[4],
        text_mask,
        HEADS_T,
    )
    image_residual, image_context_grad, image_parts = stream_backward(
        image_cot.astype(jnp.float32),
        image_context,
        image_saved,
        params_back[5],
        params_back[6],
        params_back[9],
        image_mask,
        HEADS_I,
    )
    text_query_grad, far_image_key_grad, far_image_value_grad = attend_backward(
        text_query,
        far_image_kv[:, :CO_W],
        far_image_kv[:, CO_W:],
        image_mask,
        CO_HEADS,
        text_total,
        text_context_grad,
    )
    image_query_grad, far_text_key_grad, far_text_value_grad = attend_backward(
        image_query,
        far_text_kv[:, :CO_W],
        far_text_kv[:, CO_W:],
        far_mask,
        CO_HEADS,
        image_total,
        image_context_grad,
    )
    far_text_grad = jnp.concatenate([far_text_key_grad, far_text_value_grad], 1).astype(
        jnp.bfloat16
    )
    far_image_grad = jnp.concatenate([far_image_key_grad, far_image_value_grad], 1).astype(
        jnp.bfloat16
    )
    own_text_grad, own_image_grad = partner((far_text_grad, far_image_grad), "stream", 0)
    text_grad, text_co = co_backward(
        text_in, params_back[0], text_query_grad, own_text_grad, text_residual
    )
    image_grad, image_co = co_backward(
        image_in, params_back[5], image_query_grad, own_image_grad, image_residual
    )
    text_pack = pack_grads(text_co, text_parts)
    image_pack = pack_grads(image_co, image_parts)
    summed = (
        lax.psum_scatter(text_pack[0], ("stream", "dp"), scatter_dimension=0, tiled=True),
        lax.psum_scatter(text_pack[1], ("stream", "dp"), scatter_dimension=0, tiled=True),
        lax.psum_scatter(text_pack[2], ("stream", "dp"), scatter_dimension=0, tiled=True),
        lax.psum_scatter(text_pack[3], ("stream", "dp"), scatter_dimension=1, tiled=True),
        lax.psum_scatter(text_pack[4], ("stream", "dp"), scatter_dimension=1, tiled=True),
        lax.psum_scatter(image_pack[0], ("stream", "dp"), scatter_dimension=0, tiled=True),
        lax.psum_scatter(image_pack[1], ("stream", "dp"), scatter_dimension=0, tiled=True),
        lax.psum_scatter(image_pack[2], ("stream", "dp"), scatter_dimension=0, tiled=True),
        lax.psum_scatter(image_pack[3], ("stream", "dp"), scatter_dimension=1, tiled=True),
        lax.psum_scatter(image_pack[4], ("stream", "dp"), scatter_dimension=1, tiled=True),
    )
    return (text_final, image_final, text_grad, image_grad) + tuple(summed)


def solution(mesh):
    in_specs = (
        P(("stream", "dp"), None),
        P(("stream", "dp"), None),
        P(("stream", "dp")),
        P(("stream", "dp"), None),
        P(("stream", "dp"), None),
        P(("stream", "dp")),
        P(None, ("stream", "dp")),
        P(None, ("stream", "dp")),
        P(("stream", "dp"), None),
        P(("stream", "dp"), None),
        P(("stream", "dp")),
        P(None, ("stream", "dp")),
        P(None, ("stream", "dp")),
        P(("stream", "dp"), None),
        P(("stream", "dp"), None),
    )
    out_specs = (
        P(("stream", "dp"), None),
        P(("stream", "dp"), None),
        P(("stream", "dp"), None),
        P(("stream", "dp"), None),
        P(("stream", "dp"), None),
        P(("stream", "dp"), None),
        P(("stream", "dp")),
        P(None, ("stream", "dp")),
        P(None, ("stream", "dp")),
        P(("stream", "dp"), None),
        P(("stream", "dp"), None),
        P(("stream", "dp")),
        P(None, ("stream", "dp")),
        P(None, ("stream", "dp")),
    )
    return jax.shard_map(shards, mesh=mesh, in_specs=in_specs, out_specs=out_specs, check_vma=False)
```

profile of v0, /device:TPU:0, one launch (start us, length us, event | category | flops | bytes accessed | tf_op | source)
XLA Modules:
  0.0 1766.7 jit_solution(16024742242123231918)
XLA Ops:
  11.2 42.7 %all-reduce.9 = (bf16[3072]{0:T(1024)(128)(2,1)S(1)}, bf16[5120]{0:T(1024)(128)(2,1)S(1)}) all-reduce(bf16[3072]{0:T(1024)(128)(2,1)S(1)} %dynamic-update-slice, bf16[5120]{0:T(1024)(128)(2,1)S(1)} %dynamic-update-slice.1), channel_id=1, replica_groups=mesh['stream'=2,'dp'=16] {'stream','dp'}, use_global_device_ids=true, to_apply=%add.2 | all-reduce | flops 8192 | bytes 32768
  53.9 58.5 %all-gather.11.cloned.1.call-done = bf16[768,8448]{1,0:T(8,128)(2,1)} async-done(((bf16[24,8448]{1,0:T(8,128)(2,1)}), bf16[768,8448]{1,0:T(8,128)(2,1)}) %all-gather.11.cloned.1.call-update) | async-done | bytes 12976144 | tf_op jit(solution)/shard_map/all_gather | solution.py:328
  122.5 39.7 %all-gather = bf16[32,24,8]{1,2,0:T(8,128)(2,1)S(1)} all-gather(bf16[1,24,8]{1,2,0:T(8,128)(2,1)S(1)} %bitcast.401), channel_id=1, replica_groups=mesh['stream'=2,'dp'=16] {'stream','dp'}, dimensions={0}, use_global_device_ids=true | all-gather | bytes 12672 | tf_op jit(solution)/shard_map/all_gather | solution.py:331
  162.5 37.0 %all-gather.1 = bf16[32,24,3]{1,2,0:T(4,128)(2,1)S(1)} all-gather(bf16[1,24,3]{1,2,0:T(4,128)(2,1)S(1)} %bitcast.403), channel_id=1, replica_groups=mesh['stream'=2,'dp'=16] {'stream','dp'}, dimensions={0}, use_global_device_ids=true | all-gather | bytes 4752 | tf_op jit(solution)/shard_map/all_gather | solution.py:332
  199.8 39.3 %all-gather.2 = bf16[32,32,8]{1,2,0:T(8,128)(2,1)S(1)} all-gather(bf16[1,32,8]{1,2,0:T(8,128)(2,1)S(1)} %bitcast.402), channel_id=1, replica_groups=mesh['stream'=2,'dp'=16] {'stream','dp'}, dimensions={0}, use_global_device_ids=true | all-gather | bytes 16896 | tf_op jit(solution)/shard_map/all_gather | solution.py:336
  239.2 37.2 %all-gather.3 = bf16[32,32,3]{1,2,0:T(4,128)(2,1)S(1)} all-gather(bf16[1,32,3]{1,2,0:T(4,128)(2,1)S(1)} %bitcast.404), channel_id=1, replica_groups=mesh['stream'=2,'dp'=16] {'stream','dp'}, dimensions={0}, use_global_device_ids=true | all-gather | bytes 6336 | tf_op jit(solution)/shard_map/all_gather | solution.py:337
  302.8 38.7 %all-gather.15.cloned.1.call-done = bf16[3072,1024]{1,0:T(8,128)(2,1)} async-done(((bf16[96,1024]{1,0:T(8,128)(2,1)}), bf16[3072,1024]{1,0:T(8,128)(2,1)}) %all-gather.15.cloned.1.call-update) | async-done | bytes 6291472 | tf_op jit(solution)/shard_map/all_gather | solution.py:334
  408.5 18.2 %convert_bitcast_fusion.1 = bf16[8,128,8,128]{1,3,2,0:T(8,128)(2,1)} fusion(f32[8,8,36,128]{3,2,1,0:T(8,128)} %fusion.116, f32[8,8,36,128]{3,2,1,0:T(8,128)S(1)} %get-tuple-element.170, f32[8,8,36]{2,1,0:T(8,128)S(1)} %log_add_fusion.2, bf16[8,36,8,128]{3,2,1,0:T(8,128)(2,1)S(1)} %bitcast.320), kind=kOutput, calls=%fused_computation.129 | convolution fusion | flops 78612864 | bytes 5055488 | tf_op jit(solution)/shard_map/ghqk,gqhd->gkhd/dot_general | solution.py:112
  439.7 17.9 %convert_reduce_fusion.6 = (f32[8,128]{1,0:T(8,128)}, bf16[8,8,128,36]{2,3,1,0:T(8,128)(2,1)}) fusion(f32[8,8,36,128]{3,2,1,0:T(8,128)} %fusion.116, f32[8,8,36,128]{3,2,1,0:T(8,128)S(1)} %get-tuple-element.170, f32[8,8,36]{2,1,0:T(8,128)S(1)} %log_add_fusion.2, bf16[8,128,8,128]{3,2,1,0:T(8,128)(2,1)} %bitcast.297), kind=kOutput, calls=%fused_computation.252 | convolution fusion | flops 78448000 | bytes 5059584 | tf_op jit(solution)/shard_map/ghqk,gkhd->gqhd/dot_general | solution.py:109
  519.9 38.7 %multiply_convert_fusion = (bf16[1024,3072]{1,0:T(8,128)(2,1)}, f32[1024,3072]{1,0:T(8,128)}, f32[1024,3072]{1,0:T(8,128)}) fusion(f32[3072]{0:T(1024)S(1)} %slice.283, bf16[768,8448]{1,0:T(8,128)(2,1)} %all-gather.11.cloned.1.call-done, f32[1024,768]{0,1:T(8,128)S(1)} %get-tuple-element.165, f32[768]{0:T(1024)S(1)} %get-tuple-element.97, ...), kind=kOutput, calls=%fused_computation.11 | convolution fusion | flops 5043388416 | bytes 39348224 | tf_op jit(solution)/shard_map/dot_general | solution.py:31
  569.5 19.3 %fusion.454 = (f32[3072]{0:T(1024)S(1)}, bf16[1024,3072]{1,0:T(8,128)(2,1)}) fusion(f32[1024,3072]{1,0:T(8,128)} %get-tuple-element.125, bf16[4864,768]{1,0:T(8,128)(2,1)} %all-gather.13.cloned.1.call-done, f32[1024]{0:T(1024)S(1)} %broadcast_multiply_fusion.4, f32[1024,768]{0,1:T(8,128)S(1)} %get-tuple-element.168, ...), kind=kOutput, calls=%fused_computation.499 | convolution fusion | flops 4889244672 | bytes 40938496 | tf_op jit(solution)/shard_map/rn,kn->rk/dot_general | solution.py:39
  588.8 11.8 multiply_reduce_fusion.1
  617.1 12.6 fusion.162
  629.7 12.6 fusion.159
  698.2 13.7 collective-permute-done.4
  716.3 9.4 pad_maximum_fusion.3
  754.2 10.3 fusion.423
  764.5 10.7 fusion.56
  790.2 16.3 pad_maximum_fusion.1
  843.7 20.8 %pad_maximum_fusion = f32[1024,7168]{1,0:T(8,128)} fusion(f32[1024,1024]{1,0:T(8,128)} %fusion.392, f32[1024,3072]{1,0:T(8,128)} %fusion.418, f32[1024,2048]{1,0:T(8,128)} %copy.307, f32[1024,1024]{1,0:T(8,128)} %copy.306), kind=kLoop, calls=%fused_computation.4 | loop fusion | flops 22020096 | bytes 58720256 | tf_op jit(solution)/shard_map/concatenate | solution.py:302
  897.8 116.4 %reduce-scatter.19.cloned.1.call-done = f32[96,1024]{1,0:T(8,128)} async-done(((f32[3072,1024]{1,0:T(8,128)}), f32[96,1024]{1,0:T(8,128)}) %reduce-scatter.19.cloned.1.call-update) | async-done | bytes 393232 | tf_op jit(solution)/shard_map/reduce_scatter | solution.py:449
  1014.2 173.6 %reduce-scatter.15.cloned.1.call-done = f32[152,768]{1,0:T(8,128)} async-done(((f32[4864,768]{1,0:T(8,128)}), f32[152,768]{1,0:T(8,128)}) %reduce-scatter.15.cloned.1.call-update) | async-done | bytes 466960 | tf_op jit(solution)/shard_map/reduce_scatter | solution.py:444
  1187.7 258.1 %reduce-scatter.13.cloned.1.call-done = f32[24,8448]{1,0:T(8,128)} async-done(((f32[768,8448]{1,0:T(8,128)}), f32[24,8448]{1,0:T(8,128)}) %reduce-scatter.13.cloned.1.call-update) | async-done | bytes 811024 | tf_op jit(solution)/shard_map/reduce_scatter | solution.py:443
  1445.8 314.1 %reduce-scatter.17.cloned.1.call-done = f32[32,7168]{1,0:T(8,128)} async-done(((f32[1024,7168]{1,0:T(8,128)}), f32[32,7168]{1,0:T(8,128)}) %reduce-scatter.17.cloned.1.call-update) | async-done | bytes 917520 | tf_op jit(solution)/shard_map/reduce_scatter | solution.py:448
  (502 shorter events, 383.2 us)
Async XLA Ops:
  7.2 105.3 %all-gather.11.cloned.1.call-start = ((), (), s32[]{:S(2)}) async-start(), calls=%async_computation.7 | async-start | bytes 13381632 | tf_op jit(solution)/shard_map/all_gather | solution.py:328
  7.9 278.0 %all-gather.9.cloned.1.call-start = ((), (), s32[]{:S(2)}) async-start(), calls=%async_computation.6 | async-start | bytes 15138816 | tf_op jit(solution)/shard_map/all_gather | solution.py:333
  8.7 332.9 %all-gather.15.cloned.1.call-start = ((), (), s32[]{:S(2)}) async-start(), calls=%async_computation.9 | async-start | bytes 6488064 | tf_op jit(solution)/shard_map/all_gather | solution.py:334
  9.4 469.7 %all-gather.13.cloned.1.call-start = ((), (), s32[]{:S(2)}) async-start(), calls=%async_computation.8 | async-start | bytes 7704576 | tf_op jit(solution)/shard_map/all_gather | solution.py:329
  53.9 108.7 %copy-start.112 = (bf16[3,24]{1,0:T(4,128)(2,1)S(1)}, bf16[3,24]{1,0:T(4,128)(2,1)}, u32[]{:S(2)}) copy-start(bf16[3,24]{1,0:T(4,128)(2,1)} %param.22) | copy-start | bytes 436
  53.9 145.9 %copy-start.110 = (bf16[8,32]{1,0:T(8,128)(2,1)S(1)}, bf16[8,32]{1,0:T(8,128)(2,1)}, u32[]{:S(2)}) copy-start(bf16[8,32]{1,0:T(8,128)(2,1)} %param.26) | copy-start | bytes 1540
  53.9 185.3 %copy-start.113 = (bf16[3,32]{1,0:T(4,128)(2,1)S(1)}, bf16[3,32]{1,0:T(4,128)(2,1)}, u32[]{:S(2)}) copy-start(bf16[3,32]{1,0:T(4,128)(2,1)} %param.27) | copy-start | bytes 580
  120.3 157.1 %copy-start.61 = (bf16[1024,768]{1,0:T(8,128)(2,1)S(1)}, bf16[1024,768]{1,0:T(8,128)(2,1)}, u32[]{:S(2)}) copy-start(bf16[1024,768]{1,0:T(8,128)(2,1)} %param.15) | copy-start | bytes 4718596
  120.3 174.2 %collective-permute-start.1 = (bf16[1024,2048]{1,0:T(8,128)(2,1)}, bf16[1024,2048]{1,0:T(8,128)(2,1)}, u32[]{:S(2)}, u32[]{:S(2)}) collective-permute-start(bf16[1024,2048]{1,0:T(8,128)(2,1)} %add_convert_fusion.1), channel_id=1, source_target_pairs={{0,16},{16,0},{1,17},{17,1},{2,18},{18,2},{3,19},{19,3},{4,20},{20... | collective-permute-start | bytes 12582920 | tf_op jit(solution)/shard_map/ppermute | solution.py:27
  121.8 158.9 %collective-permute-start.2 = (bf16[8,128]{1,0:T(8,128)(2,1)S(1)}, bf16[8,128]{1,0:T(8,128)(2,1)S(1)}, u32[]{:S(2)}, u32[]{:S(2)}) collective-permute-start(bf16[8,128]{1,0:T(8,128)(2,1)S(1)} %fusion.398), channel_id=1, source_target_pairs={{0,16},{16,0},{1,17},{17,1},{2,18},{18,2},{3,19},{19,3},{4,20},{20... | collective-permute-start | bytes 6152 | tf_op jit(solution)/shard_map/ppermute | solution.py:27
  122.4 746.4 %reduce-scatter.23.cloned.1.call-start = ((), (), s32[]{:S(2)}) async-start(), calls=%async_computation.15 | async-start | bytes 540672
  277.2 240.2 %copy-start.98 = (f32[768]{0:T(1024)}, f32[768]{0:T(1024)S(1)}, u32[]{:S(2)}) copy-start(f32[768]{0:T(1024)S(1)} %get-tuple-element.192) | copy-start | bytes 9220
  277.2 240.2 %copy-start.104 = (f32[768]{0:T(1024)}, f32[768]{0:T(1024)S(1)}, u32[]{:S(2)}) copy-start(f32[768]{0:T(1024)S(1)} %get-tuple-element.101) | copy-start | bytes 9220
  277.2 281.4 %copy-start.102 = (f32[768]{0:T(1024)}, f32[768]{0:T(1024)S(1)}, u32[]{:S(2)}) copy-start(f32[768]{0:T(1024)S(1)} %get-tuple-element.97) | copy-start | bytes 9220
  277.3 114.0 %copy-start.73 = (f32[1,1024]{1,0:T(1,128)}, f32[1,1024]{1,0:T(1,128)S(1)}, u32[]{:S(2)}) copy-start(f32[1,1024]{1,0:T(1,128)S(1)} %get-tuple-element.148) | copy-start | bytes 12292
  290.5 179.9 %collective-permute-start = (bf16[288,2048]{1,0:T(8,128)(2,1)}, bf16[288,2048]{1,0:T(8,128)(2,1)}, u32[]{:S(2)}, u32[]{:S(2)}) collective-permute-start(bf16[288,2048]{1,0:T(8,128)(2,1)} %fusion.73), channel_id=1, source_target_pairs={{0,16},{16,0},{1,17},{17,1},{2,18},{18,2},{3,19},{19,3},{4,20},{20... | collective-permute-start | bytes 3538952 | tf_op jit(solution)/shard_map/ppermute | solution.py:27
  435.5 278.1 %collective-permute-start.3 = (bf16[1024,2048]{1,0:T(8,128)(2,1)}, bf16[1024,2048]{1,0:T(8,128)(2,1)}, u32[]{:S(2)}, u32[]{:S(2)}) collective-permute-start(bf16[1024,2048]{1,0:T(8,128)(2,1)} %pad_maximum_fusion.4), channel_id=1, source_target_pairs={{0,16},{16,0},{1,17},{17,1},{2,18},{18,2},{3,19},{19,3},{4,20},{20... | collective-permute-start | bytes 12582920 | tf_op jit(solution)/shard_map/ppermute | solution.py:27
  457.6 412.6 %reduce-scatter.21.cloned.1.call-start = ((), (), s32[]{:S(2)}) async-start(), calls=%async_computation.14 | async-start | bytes 540672
  458.8 433.7 %all-reduce.12.cloned.1.call-start = ((), (), s32[]{:S(2)}) async-start(), calls=%async_computation.16 | async-start | bytes 139264
  683.7 28.1 %collective-permute-start.4 = (bf16[288,2048]{1,0:T(8,128)(2,1)}, bf16[288,2048]{1,0:T(8,128)(2,1)}, u32[]{:S(2)}, u32[]{:S(2)}) collective-permute-start(bf16[288,2048]{1,0:T(8,128)(2,1)} %pad_maximum_fusion.5), channel_id=1, source_target_pairs={{0,16},{16,0},{1,17},{17,1},{2,18},{18,2},{3,19},{19,3},{4,20},{20... | collective-permute-start | bytes 3538952 | tf_op jit(solution)/shard_map/ppermute | solution.py:27
  716.3 297.9 %reduce-scatter.19.cloned.1.call-start = ((), (), s32[]{:S(2)}) async-start(), calls=%async_computation.13 | async-start | bytes 12976128 | tf_op jit(solution)/shard_map/reduce_scatter | solution.py:449
  725.7 462.0 %reduce-scatter.15.cloned.1.call-start = ((), (), s32[]{:S(2)}) async-start(), calls=%async_computation.11 | async-start | bytes 15409152 | tf_op jit(solution)/shard_map/reduce_scatter | solution.py:444
  743.9 701.9 %reduce-scatter.13.cloned.1.call-start = ((), (), s32[]{:S(2)}) async-start(), calls=%async_computation.10 | async-start | bytes 26763264 | tf_op jit(solution)/shard_map/reduce_scatter | solution.py:443
  806.5 953.4 %reduce-scatter.17.cloned.1.call-start = ((), (), s32[]{:S(2)}) async-start(), calls=%async_computation.12 | async-start | bytes 30277632 | tf_op jit(solution)/shard_map/reduce_scatter | solution.py:448
  (112 other events, 1238.7 us)
Sparse Core Ops, SparseCore 0:
  10.9 101.5 all-gather.10
  115.3 146.3 all-gather.8
  264.6 76.9 all-gather.14
  344.3 74.6 all-gather.12
  457.7 136.5 reduce-scatter.22
  596.5 130.7 reduce-scatter.20
  733.4 115.7 all-reduce.11
  855.9 158.2 reduce-scatter.18
  1021.9 165.7 reduce-scatter.14
  1194.6 251.1 reduce-scatter.12
  1448.7 311.2 reduce-scatter.16
where the time goes:
time: 1780 us; the launch traced here: 1770 us
  waiting for transfers between devices  975 us (55%)
  matrix products  362 us (20%)
  blocking collectives  196 us (11%)
  local copies, waits for them, and re-layouts  130 us (7%)
  other arithmetic  81.1 us (5%)
    reduce_scatter x1, waiting for transfers between devices, shards(): lax.psum_scatter(image_pack[0], ('stream', 'dp'), scatter_dimension=0, ti...  314 us
    reduce_scatter x1, waiting for transfers between devices, shards(): lax.psum_scatter(text_pack[0], ('stream', 'dp'), scatter_dimension=0, til...  258 us
    reduce_scatter x1, waiting for transfers between devices, shards(): lax.psum_scatter(text_pack[1], ('stream', 'dp'), scatter_dimension=0, til...  174 us
    reduce_scatter x1, waiting for transfers between devices, shards(): lax.psum_scatter(image_pack[1], ('stream', 'dp'), scatter_dimension=0, ti...  116 us
    dot_general x14, matrix products, forward_dot(): return jnp.dot(left_side, right_side, preferred_element_type=jnp.float32)  93.3 us
    dot_general x14, matrix products, input_grad(): jnp.einsum('rn,kn->rk', upstream, weight, preferred_element_type=jnp.floa...  83 us
    dot_general x14, matrix products, weight_grad(): jnp.einsum('rk,rn->kn', inputs, upstream, preferred_element_type=jnp.floa...  76.3 us
    unnamed x283, local copies, waits for them, and re-layouts  67.3 us
  transfers between devices with their start and end apart: 16, of which 7 were waited for; matrix products, arithmetic and copies ran while one was open for 31% of the time, Pallas kernels for 0%

commit v1 on v0

v1 whole, which is shorter than its diff:
```python
import functools

import jax
import jax.numpy as jnp
from jax import lax
from jax.experimental import pallas as pl
from jax.experimental.pallas import tpu as pltpu
from jax.sharding import PartitionSpec as P

CO_W = 1024
HEADS_T = 12
HEADS_I = 8
CO_HEADS = 8
CAP = 128
REGIONS = 36
SLOTS = 48

epsilon = 1e-05
negative = -1e30
BF = jnp.bfloat16
F32 = jnp.float32
VMEM_LIMIT = 60 * 1024 * 1024
HALF_ROOT = 0.7071067811865476
INV_ROOT = 0.3989422804014327
ANY = pl.BlockSpec(memory_space=pl.ANY)
SMEM = pl.BlockSpec(memory_space=pltpu.SMEM)


def dot_nn(a, b):
    return lax.dot_general(a, b, (((1,), (0,)), ((), ())), preferred_element_type=F32)


def dot_nt(a, b):
    return lax.dot_general(a, b, (((1,), (1,)), ((), ())), preferred_element_type=F32)


def dot_tn(a, b):
    return lax.dot_general(a, b, (((0,), (0,)), ((), ())), preferred_element_type=F32)


def params():
    return pltpu.CompilerParams(vmem_limit_bytes=VMEM_LIMIT)


def dp_parts():
    total = lax.axis_size("dp")
    index = lax.axis_index("dp")
    return total // 4, index // 4, (index // 2) % 2, index % 2


def over_core(block):
    total = lax.axis_size("dp")
    return lax.ppermute(block, "dp", [(d, d ^ 1) for d in range(total)])


def over_y(block):
    total = lax.axis_size("dp")
    return lax.ppermute(block, "dp", [(d, d ^ 2) for d in range(total)])


def over_x(block):
    total = lax.axis_size("stream")
    return lax.ppermute(block, "stream", [(d, d ^ 1) for d in range(total)])


def over_z(block, shift):
    total = lax.axis_size("dp")
    return lax.ppermute(block, "dp", [(d, (d + 4 * shift) % total) for d in range(total)])


def pick(buffer, position, axis):
    return lax.dynamic_index_in_dim(buffer, position, axis, keepdims=False)


def place_kernel(table_ref, *refs):
    pieces, out_ref = refs[:-1], refs[-1]
    step = pl.program_id(0)
    for number, piece in enumerate(pieces):

        @pl.when(step == number)
        def _(piece=piece):
            out_ref[...] = piece[...]


def place(shape, block_in, grid, steps, block_out, spot, pieces, table):
    def read(number):
        def index(i, j, table_ref):
            return steps(jnp.where(i == number, j, jnp.where(i < number, 0, grid - 1)))

        return pl.BlockSpec(block_in, index)

    return pl.pallas_call(
        place_kernel,
        grid_spec=pltpu.PrefetchScalarGridSpec(
            num_scalar_prefetch=1,
            grid=(len(pieces), grid),
            in_specs=[read(number) for number in range(len(pieces))],
            out_specs=pl.BlockSpec(
                block_out, lambda i, j, table_ref: spot(table_ref[2 * i], table_ref[2 * i + 1], j)
            ),
        ),
        out_shape=jax.ShapeDtypeStruct(shape, pieces[0].dtype),
        compiler_params=params(),
    )(table, *pieces)


def table_of(pairs):
    return jnp.stack([jnp.asarray(v, jnp.int32) for pair in pairs for v in pair])


def gather_rows(own, y_first):
    nz, z, y, c = dp_parts()
    x = lax.axis_index("stream")
    rows, cols = own.shape
    column = place(
        (nz, rows, cols),
        (rows, cols),
        1,
        lambda j: (0, 0),
        (None, rows, cols),
        lambda p, q, j: (p, 0, 0),
        [own] + [over_z(own, shift) for shift in range(1, nz)],
        table_of([((z - shift) % nz, 0) for shift in range(nz)]),
    )

    def pair(first, second):
        return place(
            (nz, 2, rows, cols),
            (nz, rows, cols),
            1,
            lambda j: (0, 0, 0),
            (nz, None, rows, cols),
            lambda p, q, j: (0, p, 0, 0),
            [first, second],
            table_of([(y, 0), (1 - y, 0)]),
        )

    plane = pair(column, over_y(column))
    if y_first:
        far = over_x(plane)
    else:
        over = over_x(column)
        far = pair(over, over_y(over))
    full = place(
        (2, nz, 2, 2, rows, cols),
        (None, 2, rows, cols),
        nz,
        lambda j: (j, 0, 0, 0),
        (None, None, 2, None, rows, cols),
        lambda p, q, j: (p, j, 0, q, 0, 0),
        [plane, far, over_core(plane), over_core(far)],
        table_of([(x, c), (1 - x, c), (x, 1 - c), (1 - x, 1 - c)]),
    )
    return full.reshape(-1, cols)


def add_low(kept, came):
    return (kept.astype(F32) + came.astype(F32)).astype(BF)


def scatter_rows(grad, y_first):
    nz, z, y, c = dp_parts()
    x = lax.axis_index("stream")
    cols = grad.shape[1]
    part = grad.reshape(2, nz, 2, 2, -1, cols)
    part = add_low(pick(part, c, 3), over_core(pick(part, 1 - c, 3)))
    if y_first:
        part = add_low(pick(part, y, 2), over_y(pick(part, 1 - y, 2)))
        part = add_low(pick(part, x, 0), over_x(pick(part, 1 - x, 0)))
    else:
        part = add_low(pick(part, x, 0), over_x(pick(part, 1 - x, 0)))
        part = add_low(pick(part, y, 1), over_y(pick(part, 1 - y, 1)))
    total = pick(part, z, 0).astype(F32)
    for shift in range(1, nz):
        total = total + over_z(pick(part, (z + shift) % nz, 0), shift).astype(F32)
    return total


def softmax_rows(scores):
    high = jnp.max(scores, -1, keepdims=True)
    exponent = jnp.exp(scores - high)
    return exponent * (1.0 / jnp.sum(exponent, -1, keepdims=True))


def norm_rows(pre_norm):
    centered = pre_norm - jnp.mean(pre_norm, -1, keepdims=True)
    inverse = lax.rsqrt(jnp.mean(centered * centered, -1, keepdims=True) + epsilon)
    return centered * inverse, inverse


def norm_back_rows(upstream, gain, normed, inverse):
    scaled = upstream * gain
    return inverse * (
        scaled
        - jnp.mean(scaled, -1, keepdims=True)
        - normed * jnp.mean(scaled * normed, -1, keepdims=True)
    )


def col_sum(block):
    return jnp.sum(block, 0, keepdims=True)


def key_mask(shape, count):
    return jnp.where(lax.broadcasted_iota(jnp.int32, shape, 1) < count, 0.0, negative)


def attend_all(units, factor):
    scores = [dot_nt(q, k) * factor + mask for q, k, _, mask in units]
    probs = [softmax_rows(score).astype(BF) for score in scores]
    return [dot_nn(prob, unit[2]) for prob, unit in zip(probs, units)]


def attend_back_all(units, upstreams, factor):
    scores = [dot_nt(q, k) * factor + mask for q, k, _, mask in units]
    raised = [dot_nt(up, unit[2]) for up, unit in zip(upstreams, units)]
    probs = [softmax_rows(score) for score in scores]
    values_grad = [dot_tn(prob.astype(BF), up) for prob, up in zip(probs, upstreams)]
    rounded = [
        (prob * (grad - jnp.sum(prob * grad, -1, keepdims=True)) * factor).astype(BF)
        for prob, grad in zip(probs, raised)
    ]
    queries_grad = [dot_nn(low, unit[1]) for low, unit in zip(rounded, units)]
    keys_grad = [dot_tn(low, unit[0]) for low, unit in zip(rounded, units)]
    return list(zip(queries_grad, keys_grad, values_grad))


def co_forward_kernel(len_ref, text_ref, image_ref, text_out, image_out):
    step = pl.program_id(0)
    factor = (CO_W // CO_HEADS) ** -0.5
    region_mask = key_mask((1, SLOTS), REGIONS)
    text_mask = key_mask((1, CAP), len_ref[step])
    units, places = [], []
    for head in range(CO_HEADS):
        at = [slice(part * CO_W + head * 128, part * CO_W + head * 128 + 128) for part in range(3)]
        tq, tk, tv = [text_ref[:, where] for where in at]
        iq, ik, iv = [image_ref[:, where] for where in at]
        units += [(tq, ik, iv, region_mask), (iq, tk, tv, text_mask)]
        places += [(text_out, at[0]), (image_out, at[0])]
    for (out_ref, where), context in zip(places, attend_all(units, factor)):
        out_ref[:, where] = context.astype(BF)


def co_forward(lengths, text_co, image_co):
    pairs = lengths.shape[0]
    return pl.pallas_call(
        co_forward_kernel,
        grid=(pairs,),
        in_specs=[
            SMEM,
            pl.BlockSpec((CAP, 3 * CO_W), lambda i: (i, 0)),
            pl.BlockSpec((SLOTS, 3 * CO_W), lambda i: (i, 0)),
        ],
        out_specs=[
            pl.BlockSpec((CAP, CO_W), lambda i: (i, 0)),
            pl.BlockSpec((SLOTS, CO_W), lambda i: (i, 0)),
        ],
        out_shape=[
            jax.ShapeDtypeStruct((pairs * CAP, CO_W), BF),
            jax.ShapeDtypeStruct((pairs * SLOTS, CO_W), BF),
        ],
        compiler_params=params(),
    )(lengths, text_co, image_co)


def co_backward_kernel(
    len_ref, text_ref, image_ref, text_up, image_up, text_out, image_out, text_sum, image_sum
):
    step = pl.program_id(0)
    factor = (CO_W // CO_HEADS) ** -0.5
    region_mask = key_mask((1, SLOTS), REGIONS)
    text_mask = key_mask((1, CAP), len_ref[step])

    @pl.when(step == 0)
    def _():
        text_sum[...] = jnp.zeros_like(text_sum)
        image_sum[...] = jnp.zeros_like(image_sum)

    def store(out_ref, sum_ref, where, grad):
        low = grad.astype(BF)
        out_ref[:, where] = low
        sum_ref[:, where] += col_sum(low.astype(F32))

    units, ups, places = [], [], []
    for head in range(CO_HEADS):
        at = [slice(part * CO_W + head * 128, part * CO_W + head * 128 + 128) for part in range(3)]
        tq, tk, tv = [text_ref[:, where] for where in at]
        iq, ik, iv = [image_ref[:, where] for where in at]
        units += [(tq, ik, iv, region_mask), (iq, tk, tv, text_mask)]
        ups += [text_up[:, at[0]], image_up[:, at[0]]]
        places.append(at)
    grads = attend_back_all(units, ups, factor)
    for head, at in enumerate(places):
        dtq, dik, div = grads[2 * head]
        diq, dtk, dtv = grads[2 * head + 1]
        for where, grad in zip(at, (dtq, dtk, dtv)):
            store(text_out, text_sum, where, grad)
        for where, grad in zip(at, (diq, dik, div)):
            store(image_out, image_sum, where, grad)


def co_backward(lengths, text_co, image_co, text_up, image_up):
    pairs = lengths.shape[0]
    wide = 3 * CO_W
    return pl.pallas_call(
        co_backward_kernel,
        grid=(pairs,),
        in_specs=[
            SMEM,
            pl.BlockSpec((CAP, wide), lambda i: (i, 0)),
            pl.BlockSpec((SLOTS, wide), lambda i: (i, 0)),
            pl.BlockSpec((CAP, CO_W), lambda i: (i, 0)),
            pl.BlockSpec((SLOTS, CO_W), lambda i: (i, 0)),
        ],
        out_specs=[
            pl.BlockSpec((CAP, wide), lambda i: (i, 0)),
            pl.BlockSpec((SLOTS, wide), lambda i: (i, 0)),
            pl.BlockSpec((1, wide), lambda i: (0, 0)),
            pl.BlockSpec((1, wide), lambda i: (0, 0)),
        ],
        out_shape=[
            jax.ShapeDtypeStruct((pairs * CAP, wide), BF),
            jax.ShapeDtypeStruct((pairs * SLOTS, wide), BF),
            jax.ShapeDtypeStruct((1, wide), F32),
            jax.ShapeDtypeStruct((1, wide), F32),
        ],
        compiler_params=params(),
    )(lengths, text_co, image_co, text_up, image_up)


def fetch(step, copies):
    @pl.when(step == 0)
    def _():
        for copy in copies:
            copy.start()
        for copy in copies:
            copy.wait()


def text_units(len_ref, step, pair_count):
    for pair in range(pair_count):
        mask = key_mask((1, CAP), len_ref[step * pair_count + pair])
        for block in range(HEADS_T // 2):
            yield slice(pair * CAP, pair * CAP + CAP), block * 128, mask


def image_mask():
    shape = (2 * SLOTS, 2 * SLOTS)
    row = lax.broadcasted_iota(jnp.int32, shape, 0)
    col = lax.broadcasted_iota(jnp.int32, shape, 1)
    same = (row >= SLOTS) == (col >= SLOTS)
    local = jnp.where(col >= SLOTS, col - SLOTS, col)
    return jnp.where(same & (local < REGIONS), 0.0, negative)


def image_units(rows):
    mask = image_mask()
    return [
        (slice(start, start + 2 * SLOTS), head * 128, mask)
        for start in range(0, rows, 2 * SLOTS)
        for head in range(HEADS_I)
    ]


def halves(block):
    low = lax.broadcasted_iota(jnp.int32, block.shape, 1) < 64
    zero = jnp.zeros_like(block)
    return jnp.concatenate([jnp.where(low, block, zero), jnp.where(low, zero, block)], 0)


def unhalve(stacked):
    rows = stacked.shape[0] // 2
    low = lax.broadcasted_iota(jnp.int32, (rows, stacked.shape[1]), 1) < 64
    return jnp.where(low, stacked[:rows], stacked[rows:])


def attn_forward_kernel(
    is_text,
    down_at,
    len_ref,
    context_ref,
    input_ref,
    proj_ref,
    out_w_ref,
    bias_ref,
    gain_ref,
    zhat1_ref,
    inv1_ref,
    low1_ref,
    triple_ref,
    attended_ref,
    zhat2_ref,
    inv2_ref,
    wco,
    wqkv,
    wo,
    sems,
):
    step = pl.program_id(0)
    width = input_ref.shape[1]
    rows = input_ref.shape[0]
    fetch(
        step,
        [
            pltpu.make_async_copy(out_w_ref.at[pl.ds(0, CO_W)], wco, sems.at[0]),
            pltpu.make_async_copy(proj_ref.at[:, pl.ds(0, 3 * width)], wqkv, sems.at[1]),
            pltpu.make_async_copy(out_w_ref.at[pl.ds(CO_W, width)], wo, sems.at[2]),
        ],
    )
    normed, inverse = norm_rows(
        input_ref[...].astype(F32) + dot_nn(context_ref[...], wco[...]) + bias_ref[0:1]
    )
    zhat1_ref[...] = normed
    inv1_ref[...] = inverse
    first = normed * gain_ref[0:1] + bias_ref[1:2]
    first_low = first.astype(BF)
    low1_ref[...] = first_low
    for part in range(3):
        at = slice(part * width, part * width + width)
        piece = dot_nn(first_low, wqkv[:, at])
        if part == 0:
            piece = piece + bias_ref[2:3]
        if part == 2:
            piece = piece + bias_ref[3:4]
        triple_ref[:, at] = piece.astype(BF)

    def lanes(part, lane):
        return slice(part * width + lane, part * width + lane + 128)

    if is_text:
        places = list(text_units(len_ref, step, rows // CAP))
        factor = (width // HEADS_T) ** -0.5
    else:
        places = image_units(rows)
        factor = (width // HEADS_I) ** -0.5
    units = []
    for where, lane, mask in places:
        q, k, v = [triple_ref[where, lanes(part, lane)] for part in range(3)]
        units.append((halves(q) if is_text else q, k, v, mask))
    for (where, lane, _), context in zip(places, attend_all(units, factor)):
        context = unhalve(context) if is_text else context
        attended_ref[where, lane : lane + 128] = context.astype(BF)
    normed, inverse = norm_rows(first + dot_nn(attended_ref[...], wo[...]) + bias_ref[4:5])
    zhat2_ref[...] = normed
    inv2_ref[...] = inverse


def row_spec(rows, cols):
    return pl.BlockSpec((rows, cols), lambda i: (i, 0))


def whole_spec(rows, cols):
    return pl.BlockSpec((rows, cols), lambda i: (0, 0))


def attn_forward(is_text, block, lengths, context, inputs, proj, out_w, bias, gain):
    rows, width = inputs.shape
    shape = jax.ShapeDtypeStruct
    return pl.pallas_call(
        functools.partial(attn_forward_kernel, is_text, CO_W + width),
        grid=(rows // block,),
        in_specs=[
            SMEM,
            row_spec(block, CO_W),
            row_spec(block, width),
            ANY,
            ANY,
            whole_spec(8, width),
            whole_spec(3, width),
        ],
        out_specs=[
            row_spec(block, width),
            row_spec(block, 1),
            row_spec(block, width),
            row_spec(block, 3 * width),
            row_spec(block, width),
            row_spec(block, width),
            row_spec(block, 1),
        ],
        out_shape=[
            shape((rows, width), F32),
            shape((rows, 1), F32),
            shape((rows, width), BF),
            shape((rows, 3 * width), BF),
            shape((rows, width), BF),
            shape((rows, width), F32),
            shape((rows, 1), F32),
        ],
        scratch_shapes=[
            pltpu.VMEM((CO_W, width), BF),
            pltpu.VMEM((width, 3 * width), BF),
            pltpu.VMEM((width, width), BF),
            pltpu.SemaphoreType.DMA((3,)),
        ],
        compiler_params=params(),
    )(lengths, context, inputs, proj, out_w, bias, gain)


def ffn_kernel(
    chunk,
    zhat2_ref,
    inv2_ref,
    cot_ref,
    proj_ref,
    out_w_ref,
    up_bias_ref,
    bias_ref,
    gain_ref,
    final_ref,
    low2_ref,
    active_ref,
    third_low_ref,
    hidden_low_ref,
    second_grad_ref,
    sums_ref,
    up_sum_ref,
    wup,
    wdown,
    slope,
    sems,
):
    step = pl.program_id(0)
    width = zhat2_ref.shape[1]
    hidden = wup.shape[1]
    fetch(
        step,
        [
            pltpu.make_async_copy(proj_ref.at[:, pl.ds(3 * width, hidden)], wup, sems.at[0]),
            pltpu.make_async_copy(out_w_ref.at[pl.ds(CO_W + width, hidden)], wdown, sems.at[1]),
        ],
    )

    @pl.when(step == 0)
    def _():
        sums_ref[...] = jnp.zeros_like(sums_ref)
        up_sum_ref[...] = jnp.zeros_like(up_sum_ref)

    second = zhat2_ref[...] * gain_ref[1:2] + bias_ref[5:6]
    second_low = second.astype(BF)
    low2_ref[...] = second_low
    total = second + bias_ref[6:7]
    for start in range(0, hidden, chunk):
        at = slice(start, start + chunk)
        u = dot_nn(second_low, wup[:, at]) + up_bias_ref[:, at]
        phi = 0.5 + 0.5 * lax.erf(u * HALF_ROOT)
        active = (u * phi).astype(BF)
        active_ref[:, at] = active
        slope[:, at] = phi + (u * INV_ROOT) * jnp.exp(-0.5 * u * u)
        total = total + dot_nn(active, wdown[at])
    normed, inverse = norm_rows(total)
    final_ref[...] = normed * gain_ref[2:3] + bias_ref[7:8]
    upstream = cot_ref[...].astype(F32)
    third = norm_back_rows(upstream, gain_ref[2:3], normed, inverse)
    third_low = third.astype(BF)
    third_low_ref[...] = third_low
    sums_ref[0:1] += col_sum(upstream * normed)
    sums_ref[1:2] += col_sum(upstream)
    sums_ref[2:3] += col_sum(third)
    back = third
    for start in range(0, hidden, chunk):
        at = slice(start, start + chunk)
        grad = dot_nt(third_low, wdown[at]) * slope[:, at]
        up_sum_ref[:, at] += col_sum(grad)
        grad_low = grad.astype(BF)
        hidden_low_ref[:, at] = grad_low
        back = back + dot_nt(grad_low, wup[:, at])
    zhat2 = zhat2_ref[...]
    second_grad = norm_back_rows(back, gain_ref[1:2], zhat2, inv2_ref[...])
    second_grad_ref[...] = second_grad
    sums_ref[3:4] += col_sum(back * zhat2)
    sums_ref[4:5] += col_sum(back)
    sums_ref[5:6] += col_sum(second_grad)


def ffn(block, chunk, hidden, zhat2, inv2, cot, proj, out_w, up_bias, bias, gain):
    rows, width = zhat2.shape
    shape = jax.ShapeDtypeStruct
    return pl.pallas_call(
        functools.partial(ffn_kernel, chunk),
        grid=(rows // block,),
        in_specs=[
            row_spec(block, width),
            row_spec(block, 1),
            row_spec(block, width),
            ANY,
            ANY,
            whole_spec(1, hidden),
            whole_spec(8, width),
            whole_spec(3, width),
        ],
        out_specs=[
            row_spec(block, width),
            row_spec(block, width),
            row_spec(block, hidden),
            row_spec(block, width),
            row_spec(block, hidden),
            row_spec(block, width),
            whole_spec(8, width),
            whole_spec(1, hidden),
        ],
        out_shape=[
            shape((rows, width), F32),
            shape((rows, width), BF),
            shape((rows, hidden), BF),
            shape((rows, width), BF),
            shape((rows, hidden), BF),
            shape((rows, width), F32),
            shape((8, width), F32),
            shape((1, hidden), F32),
        ],
        scratch_shapes=[
            pltpu.VMEM((width, hidden), BF),
            pltpu.VMEM((hidden, width), BF),
            pltpu.VMEM((block, hidden), F32),
            pltpu.SemaphoreType.DMA((2,)),
        ],
        compiler_params=params(),
    )(zhat2, inv2, cot, proj, out_w, up_bias, bias, gain)


def attn_backward_kernel(
    is_text,
    len_ref,
    second_grad_ref,
    triple_ref,
    zhat1_ref,
    inv1_ref,
    proj_ref,
    out_w_ref,
    gain_ref,
    second_low_ref,
    triple_low_ref,
    first_grad_ref,
    first_low_ref,
    context_low_ref,
    sums_ref,
    wco,
    wqkv,
    wo,
    upstream,
    sems,
):
    step = pl.program_id(0)
    rows, width = second_grad_ref.shape
    fetch(
        step,
        [
            pltpu.make_async_copy(out_w_ref.at[pl.ds(0, CO_W)], wco, sems.at[0]),
            pltpu.make_async_copy(proj_ref.at[:, pl.ds(0, 3 * width)], wqkv, sems.at[1]),
            pltpu.make_async_copy(out_w_ref.at[pl.ds(CO_W, width)], wo, sems.at[2]),
        ],
    )

    @pl.when(step == 0)
    def _():
        sums_ref[...] = jnp.zeros_like(sums_ref)

    second_low = second_grad_ref[...].astype(BF)
    second_low_ref[...] = second_low
    upstream[...] = dot_nt(second_low, wo[...]).astype(BF)

    def lanes(part, lane):
        return slice(part * width + lane, part * width + lane + 128)

    if is_text:
        places = list(text_units(len_ref, step, rows // CAP))
        factor = (width // HEADS_T) ** -0.5
    else:
        places = image_units(rows)
        factor = (width // HEADS_I) ** -0.5
    units, ups = [], []
    for where, lane, mask in places:
        q, k, v = [triple_ref[where, lanes(part, lane)] for part in range(3)]
        up = upstream[where, lane : lane + 128]
        units.append((halves(q) if is_text else q, k, v, mask))
        ups.append(halves(up) if is_text else up)
    for (where, lane, _), grads in zip(places, attend_back_all(units, ups, factor)):
        dq, dk, dv = grads
        for part, grad in enumerate((unhalve(dq) if is_text else dq, dk, dv)):
            triple_low_ref[where, lanes(part, lane)] = grad.astype(BF)
    back = second_grad_ref[...]
    for part in range(3):
        at = slice(part * width, part * width + width)
        piece = triple_low_ref[:, at]
        back = back + dot_nt(piece, wqkv[:, at])
        if part != 1:
            row = 3 + part // 2
            sums_ref[row : row + 1] += col_sum(piece.astype(F32))
    zhat1 = zhat1_ref[...]
    first_grad = norm_back_rows(back, gain_ref[0:1], zhat1, inv1_ref[...])
    first_grad_ref[...] = first_grad
    sums_ref[0:1] += col_sum(back * zhat1)
    sums_ref[1:2] += col_sum(back)
    sums_ref[2:3] += col_sum(first_grad)
    first_low = first_grad.astype(BF)
    first_low_ref[...] = first_low
    context_low_ref[...] = dot_nt(first_low, wco[...]).astype(BF)


def attn_backward(is_text, block, lengths, second_grad, triple, zhat1, inv1, proj, out_w, gain):
    rows, width = zhat1.shape
    shape = jax.ShapeDtypeStruct
    return pl.pallas_call(
        functools.partial(attn_backward_kernel, is_text),
        grid=(rows // block,),
        in_specs=[
            SMEM,
            row_spec(block, width),
            row_spec(block, 3 * width),
            row_spec(block, width),
            row_spec(block, 1),
            ANY,
            ANY,
            whole_spec(3, width),
        ],
        out_specs=[
            row_spec(block, width),
            row_spec(block, 3 * width),
            row_spec(block, width),
            row_spec(block, width),
            row_spec(block, CO_W),
            whole_spec(8, width),
        ],
        out_shape=[
            shape((rows, width), BF),
            shape((rows, 3 * width), BF),
            shape((rows, width), F32),
            shape((rows, width), BF),
            shape((rows, CO_W), BF),
            shape((8, width), F32),
        ],
        scratch_shapes=[
            pltpu.VMEM((CO_W, width), BF),
            pltpu.VMEM((width, 3 * width), BF),
            pltpu.VMEM((width, width), BF),
            pltpu.VMEM((block, width), BF),
            pltpu.SemaphoreType.DMA((3,)),
        ],
        compiler_params=params(),
    )(lengths, second_grad, triple, zhat1, inv1, proj, out_w, gain)


def weight_grad(inputs, upstream):
    return dot_tn(inputs, upstream).astype(BF)


def co_project(inputs, weight, wide):
    bias = jnp.concatenate([wide[:CO_W], jnp.zeros((CO_W,), F32), wide[CO_W : 2 * CO_W]])
    return (dot_nn(inputs, weight[:, : 3 * CO_W]) + bias).astype(BF)


def pad_pairs(block):
    wide = block.reshape(-1, REGIONS, block.shape[1])
    return jnp.pad(wide, ((0, 0), (0, SLOTS - REGIONS), (0, 0))).reshape(-1, block.shape[1])


def unpad_pairs(block):
    return block.reshape(-1, SLOTS, block.shape[1])[:, :REGIONS].reshape(-1, block.shape[1])


def shards(
    text_in,
    image_in,
    lengths,
    t_proj,
    t_out,
    t_bias_wide,
    t_bias,
    t_gain,
    i_proj,
    i_out,
    i_bias_wide,
    i_bias,
    i_gain,
    text_cot,
    image_cot,
):
    small = (t_bias_wide, t_bias, t_gain, i_bias_wide, i_bias, i_gain)
    flat = jnp.concatenate([piece.reshape(-1) for piece in small])
    t_rows = t_proj.shape[0]
    extra = -(-flat.shape[0] // (t_rows * 128)) * 128
    riders = jnp.pad(flat, (0, extra * t_rows - flat.shape[0])).reshape(t_rows, extra)
    near_image = over_x(image_in)
    near_cot = over_x(image_cot)

    t_co = gather_rows(jnp.concatenate([t_proj[:, : 3 * CO_W], riders], 1), True)
    i_co = gather_rows(i_proj[:, : 3 * CO_W], False)
    t_outw = gather_rows(t_out, True)
    i_outw = gather_rows(i_out, False)
    i_rest = gather_rows(i_proj[:, 3 * CO_W :], True)
    t_rest = gather_rows(t_proj[:, 3 * CO_W :], False)

    shard_count = t_co.shape[0] // t_rows
    table = t_co[:, 3 * CO_W :].reshape(shard_count, -1)[:, : flat.shape[0]].astype(F32)
    taken = []
    offset = 0
    for piece in small:
        block = table[:, offset : offset + piece.size].reshape((shard_count,) + piece.shape)
        offset += piece.size
        if piece.ndim == 1:
            taken.append(block.reshape(1, -1))
        else:
            taken.append(block.transpose(1, 0, 2).reshape(piece.shape[0], -1))
    t_wide, t_rows8, t_gains, i_wide, i_rows8, i_gains = taken

    image_rows = pad_pairs(near_image)
    image_up = pad_pairs(near_cot)
    text_co = co_project(text_in, t_co, t_wide[0])
    image_co = co_project(image_rows, i_co, i_wide[0])
    text_context, image_context = co_forward(lengths, text_co, image_co)

    image_block = image_rows.shape[0]
    streams = (
        (True, 256, 512, text_context, text_in, text_cot, t_rest, t_outw, t_wide, t_rows8, t_gains),
        (
            False,
            image_block,
            512,
            image_context,
            image_rows,
            image_up,
            i_rest,
            i_outw,
            i_wide,
            i_rows8,
            i_gains,
        ),
    )
    finished = []
    for is_text, block, chunk, context, inputs, cot, rest, outw, wide, rows8, gains in streams:
        width = inputs.shape[1]
        hidden = wide.shape[1] - 2 * CO_W
        zhat1, inv1, low1, triple, attended, zhat2, inv2 = attn_forward(
            is_text, block, lengths, context, inputs, rest, outw, rows8, gains
        )
        final, low2, active, third_low, hidden_low, second_grad, sums2, up_sum = ffn(
            block, chunk, hidden, zhat2, inv2, cot, rest, outw, wide[:, 2 * CO_W :], rows8, gains
        )
        up_grad = weight_grad(low2, hidden_low)
        down_grad = weight_grad(active, third_low)
        second_low, triple_low, first_grad, first_low, context_low, sums1 = attn_backward(
            is_text, block, lengths, second_grad, triple, zhat1, inv1, rest, outw, gains
        )
        triple_grad = weight_grad(low1, triple_low)
        out_grad = jnp.concatenate(
            [weight_grad(context, first_low), weight_grad(attended, second_low), down_grad], 0
        )
        finished.append(
            (final, first_grad, context_low, up_grad, triple_grad, out_grad, sums1, sums2, up_sum)
        )
    (
        (t_final, t_first, t_ctx, t_up, t_qkv, t_outg, t_sums1, t_sums2, t_upsum),
        (i_final, i_first, i_ctx, i_up, i_qkv, i_outg, i_sums1, i_sums2, i_upsum),
    ) = finished

    image_final = over_x(unpad_pairs(i_final).astype(BF)).astype(F32)

    t_co_grad, i_co_grad, t_co_sum, i_co_sum = co_backward(
        lengths, text_co, image_co, t_ctx, i_ctx
    )
    text_grad = t_first + dot_nt(t_co_grad, t_co[:, : 3 * CO_W])
    image_grad = i_first + dot_nt(i_co_grad, i_co)
    image_grad = over_x(unpad_pairs(image_grad).astype(BF)).astype(F32)

    def small_grads(sums1, sums2, up_sum, co_sum):
        wide = jnp.concatenate([co_sum[0, :CO_W], co_sum[0, 2 * CO_W :], up_sum[0]])
        rows8 = jnp.stack(
            [sums1[2], sums1[1], sums1[3], sums1[4], sums2[5], sums2[4], sums2[2], sums2[1]]
        )
        return wide, rows8, jnp.stack([sums1[0], sums2[3], sums2[0]])

    pieces = small_grads(t_sums1, t_sums2, t_upsum, t_co_sum) + small_grads(
        i_sums1, i_sums2, i_upsum, i_co_sum
    )
    packed = []
    for piece in pieces:
        if piece.ndim == 1:
            packed.append(piece.reshape(shard_count, -1))
        else:
            packed.append(
                piece.reshape(piece.shape[0], shard_count, -1)
                .transpose(1, 0, 2)
                .reshape(shard_count, -1)
            )
    packed = jnp.concatenate(packed, 1)
    count = packed.shape[1]
    packed = jnp.pad(packed, ((0, 0), (0, extra * t_rows - count))).reshape(-1, extra).astype(BF)

    t_up = scatter_rows(t_up, True)
    i_up = scatter_rows(i_up, False)
    t_qkv = scatter_rows(t_qkv, False)
    i_qkv = scatter_rows(i_qkv, True)
    t_outg = scatter_rows(t_outg, True)
    i_outg = scatter_rows(i_outg, False)
    i_cog = scatter_rows(weight_grad(image_rows, i_co_grad), True)
    t_cog = scatter_rows(
        jnp.concatenate([weight_grad(text_in, t_co_grad), packed], 1), False
    )

    mine = t_cog[:, 3 * CO_W :].reshape(-1)
    outs = []
    offset = 0
    for piece in small:
        outs.append(mine[offset : offset + piece.size].reshape(piece.shape))
        offset += piece.size
    t_wide_g, t_rows_g, t_gain_g, i_wide_g, i_rows_g, i_gain_g = outs
    return (
        t_final,
        image_final,
        text_grad,
        image_grad,
        jnp.concatenate([t_cog[:, : 3 * CO_W], t_qkv, t_up], 1),
        t_outg,
        t_wide_g,
        t_rows_g,
        t_gain_g,
        jnp.concatenate([i_cog, i_qkv, i_up], 1),
        i_outg,
        i_wide_g,
        i_rows_g,
        i_gain_g,
    )


def solution(mesh):
    both = ("stream", "dp")
    rows, cols, flat = P(both, None), P(None, both), P(both)
    weights = (rows, rows, flat, cols, cols)
    return jax.shard_map(
        shards,
        mesh=mesh,
        in_specs=(rows, rows, flat) + weights + weights + (rows, rows),
        out_specs=(rows, rows, rows, rows) + weights + weights,
        check_vma=False,
    )
```

time: 1780 us -> 1020 us (0.57)
  waiting for transfers between devices: 975 us -> 340 us
  matrix products: 362 us -> 80.7 us
  Pallas kernels: 0 us -> 275 us
  blocking collectives: 196 us -> 0 us
  starting transfers between devices: 6.43 us -> 145 us
  local copies, waits for them, and re-layouts: 130 us -> 84.1 us
    reduce_scatter x4 -> x0, waiting for transfers between devices: 862 us -> none  [the longest x1 314 us: shards(): lax.psum_scatter(image_pack[0], ('stream', 'dp'), scatter_dimension=0, ti...]
    ppermute x5 -> x97, waiting for transfers between devices: 13.7 us -> 340 us  [the longest x17 189 us: over_y(): return lax.ppermute(block, 'dp', [(d, d ^ 2) for d in range(total)])]
    dot_general x66 -> x16, matrix products: 362 us -> 80.7 us  [the longest x12 51.3 us: dot_tn(): lax.dot_general(a, b, (((0,), (0,)), ((), ())), preferred_element_type=F32)]
    pallas_call x0 -> x29, Pallas kernels: none -> 275 us  [the longest x21 129 us: place(): pl.pallas_call(place_kernel, grid_spec=pltpu.PrefetchScalarGridSpec(num_s...]
    all_gather x4 -> x0, blocking collectives: 153 us -> none  [the longest x1 39.7 us: shards(): lax.all_gather(t_bias, ('stream', 'dp'), axis=1, tiled=True)]
    ppermute x5 -> x97, starting transfers between devices: 5.64 us -> 145 us  [the longest x42 99.9 us: over_z(): lax.ppermute(block, 'dp', [(d, (d + 4 * shift) % total) for d in range(to...]
    all_gather x4 -> x0, waiting for transfers between devices: 97.3 us -> none  [the longest x1 58.5 us: shards(): lax.all_gather(t_proj, ('stream', 'dp'), axis=0, tiled=True)]
    unnamed x283 -> x158, local copies, waits for them, and re-layouts: 67.3 us -> 8.07 us
  transfers between devices with their start and end apart: 16 -> 97, of which waited for: 7 -> 36; matrix products, arithmetic and copies ran while one was open for 31% -> 23% of each run, Pallas kernels for 0% -> 27%
where the time goes in v1:
time: 1020 us; the launch traced here: 999 us
  waiting for transfers between devices  340 us (33%)
  Pallas kernels  275 us (27%)
  starting transfers between devices  145 us (14%)
  local copies, waits for them, and re-layouts  84.1 us (8%)
  matrix products  80.7 us (8%)
  other arithmetic  71.9 us (7%)
    ppermute x17, waiting for transfers between devices, over_y(): return lax.ppermute(block, 'dp', [(d, d ^ 2) for d in range(total)])  189 us
    pallas_call x21, Pallas kernels, place(): pl.pallas_call(place_kernel, grid_spec=pltpu.PrefetchScalarGridSpec(num_s...  129 us
    ppermute x42, starting transfers between devices, over_z(): lax.ppermute(block, 'dp', [(d, (d + 4 * shift) % total) for d in range(to...  99.9 us
    ppermute x42, waiting for transfers between devices, over_z(): lax.ppermute(block, 'dp', [(d, (d + 4 * shift) % total) for d in range(to...  96 us
    ppermute x18, waiting for transfers between devices, over_x(): return lax.ppermute(block, 'stream', [(d, d ^ 1) for d in range(total)])  55 us
    dot_general x12, matrix products, dot_tn(): lax.dot_general(a, b, (((0,), (0,)), ((), ())), preferred_element_type=F32)  51.3 us
    pallas_call x2, Pallas kernels, ffn(): pl.pallas_call(functools.partial(ffn_kernel, chunk), grid=(rows // block,...  47.9 us
    pallas_call x2, Pallas kernels, attn_backward(): pl.pallas_call(functools.partial(attn_backward_kernel, is_text), grid=(ro...  40.6 us
  transfers between devices with their start and end apart: 97, of which 36 were waited for; matrix products, arithmetic and copies ran while one was open for 23% of the time, Pallas kernels for 27%

profile of v1, /device:TPU:0, one launch (start us, length us, event | category | flops | bytes accessed | tf_op | source)
XLA Modules:
  0.0 998.7 jit_solution(15003205711270730562)
XLA Ops:
  18.8 27.5 %collective-permute-done.1.refs_2_ = bf16[24,3200]{1,0:T(8,128)(2,1)S(1)} collective-permute-done((bf16[24,3200]{1,0:T(8,128)(2,1)S(1)}, bf16[24,3200]{1,0:T(8,128)(2,1)S(1)}, u32[]{:S(2)}, u32[]{:S(2)}) %collective-permute-start.1) | collective-permute-done | bytes 153632 | tf_op jit(solution)/shard_map/ppermute | solution.py:68
  139.4 18.6 %collective-permute-done.3.refs_1_ = bf16[4,24,3200]{2,1,0:T(8,128)(2,1)S(1)} collective-permute-done((bf16[4,24,3200]{2,1,0:T(8,128)(2,1)}, bf16[4,24,3200]{2,1,0:T(8,128)(2,1)S(1)}, u32[]{:S(2)}, u32[]{:S(2)}) %collective-permute-start.3) | collective-permute-done | bytes 614432 | tf_op jit(solution)/shard_map/ppermute | solution.py:58
  176.4 18.5 %collective-permute-done.27.refs_1_ = bf16[4,152,768]{2,1,0:T(8,128)(2,1)} collective-permute-done((bf16[4,152,768]{2,1,0:T(8,128)(2,1)}, bf16[4,152,768]{2,1,0:T(8,128)(2,1)}, u32[]{:S(2)}, u32[]{:S(2)}) %collective-permute-start.27) | collective-permute-done | bytes 933920 | tf_op jit(solution)/shard_map/ppermute | solution.py:58
  195.0 16.2 %collective-permute-done.20.refs_0_ = bf16[4,24,5376]{2,1,0:T(8,128)(2,1)} collective-permute-done((bf16[4,24,5376]{2,1,0:T(8,128)(2,1)}, bf16[4,24,5376]{2,1,0:T(8,128)(2,1)}, u32[]{:S(2)}, u32[]{:S(2)}) %collective-permute-start.20) | collective-permute-done | bytes 1032224 | tf_op jit(solution)/shard_map/ppermute | solution.py:63
  218.6 21.0 %collective-permute-done.34.refs_1_ = bf16[4,32,4096]{2,1,0:T(8,128)(2,1)} collective-permute-done((bf16[4,32,4096]{2,1,0:T(8,128)(2,1)}, bf16[4,32,4096]{2,1,0:T(8,128)(2,1)}, u32[]{:S(2)}, u32[]{:S(2)}) %collective-permute-start.34) | collective-permute-done | bytes 1048608 | tf_op jit(solution)/shard_map/ppermute | solution.py:58
  244.5 11.9 %collective-permute-done.43.refs_1_ = bf16[4,96,1024]{2,1,0:T(8,128)(2,1)} collective-permute-done((bf16[4,96,1024]{2,1,0:T(8,128)(2,1)}, bf16[4,96,1024]{2,1,0:T(8,128)(2,1)}, u32[]{:S(2)}, u32[]{:S(2)}) %collective-permute-start.43) | collective-permute-done | bytes 786464 | tf_op jit(solution)/shard_map/ppermute | solution.py:58
  280.5 13.2 %collective-permute-done.21.refs_1_ = bf16[4,24,5376]{2,1,0:T(8,128)(2,1)} collective-permute-done((bf16[4,24,5376]{2,1,0:T(8,128)(2,1)}, bf16[4,24,5376]{2,1,0:T(8,128)(2,1)}, u32[]{:S(2)}, u32[]{:S(2)}) %collective-permute-start.21) | collective-permute-done | bytes 1032224 | tf_op jit(solution)/shard_map/ppermute | solution.py:58
  308.4 11.9 %shard_map.256 = bf16[2,4,2,2,24,3200]{5,4,3,2,1,0:T(8,128)(2,1)} custom-call(s32[8]{0:T(128)} %stack.44.table_ref, bf16[4,2,24,3200]{3,2,1,0:T(8,128)(2,1)} %shard_map.255.refs_0_, bf16[4,2,24,3200]{3,2,1,0:T(8,128)(2,1)} %copy-done.26, bf16[4,2,24,3200]{3,2,1,0:T(8,128)(2,1)} %copy-done.27, bf16[4,2,24,3200]{3,2,1,0:T(8,128)(2,1)} %collective-permute-done.6.refs_3_), custom_call_target="tpu_custom_call" | custom-call | tf_op jit(solution)/shard_map/pallas_call | solution.py:92
  337.9 12.5 %shard_map.260 = bf16[2,4,2,2,32,3072]{5,4,3,2,1,0:T(8,128)(2,1)} custom-call(s32[8]{0:T(128)} %stack.44.table_ref, bf16[4,2,32,3072]{3,2,1,0:T(8,128)(2,1)} %shard_map.258.refs_0_, bf16[4,2,32,3072]{3,2,1,0:T(8,128)(2,1)} %shard_map.259.refs_1_, bf16[4,2,32,3072]{3,2,1,0:T(8,128)(2,1)} %collective-permute-done.14.refs_2_, ...), custom_call_target="tpu_custom_call" | custom-call | tf_op jit(solution)/shard_map/pallas_call | solution.py:92
  367.0 12.5 %shard_map.277 = bf16[2,4,2,2,96,1024]{5,4,3,2,1,0:T(8,128)(2,1)} custom-call(s32[8]{0:T(128)} %stack.44.table_ref, bf16[4,2,96,1024]{3,2,1,0:T(8,128)(2,1)} %shard_map.275.refs_0_, bf16[4,2,96,1024]{3,2,1,0:T(8,128)(2,1)} %shard_map.276.refs_1_, bf16[4,2,96,1024]{3,2,1,0:T(8,128)(2,1)} %collective-permute-done.44.refs_2_, ...), custom_call_target="tpu_custom_call" | custom-call | tf_op jit(solution)/shard_map/pallas_call | solution.py:92
  380.0 13.8 %shard_map.265 = bf16[2,4,2,2,24,5376]{5,4,3,2,1,0:T(8,128)(2,1)} custom-call(s32[8]{0:T(128)} %stack.44.table_ref, bf16[4,2,24,5376]{3,2,1,0:T(8,128)(2,1)} %shard_map.263.refs_0_, bf16[4,2,24,5376]{3,2,1,0:T(8,128)(2,1)} %shard_map.264.refs_1_, bf16[4,2,24,5376]{3,2,1,0:T(8,128)(2,1)} %collective-permute-done.22.refs_2_, ...), custom_call_target="tpu_custom_call" | custom-call | tf_op jit(solution)/shard_map/pallas_call | solution.py:92
  393.8 13.2 %shard_map.268 = bf16[2,4,2,2,152,768]{5,4,3,2,1,0:T(8,128)(2,1)} custom-call(s32[8]{0:T(128)} %stack.44.table_ref, bf16[4,2,152,768]{3,2,1,0:T(8,128)(2,1)} %shard_map.267.refs_0_, bf16[4,2,152,768]{3,2,1,0:T(8,128)(2,1)} %collective-permute-done.28.refs_1_, bf16[4,2,152,768]{3,2,1,0:T(8,128)(2,1)} %collective-permute-done.29.refs_2_, ...), custom_call_target="tpu_custom_call" | custom-call | tf_op jit(solution)/shard_map/pallas_call | solution.py:92
  407.0 19.5 %shard_map.269 = (f32[1024,768]{1,0:T(8,128)}, f32[1024,1]{1,0:T(8,128)}, bf16[1024,768]{1,0:T(8,128)(2,1)}, bf16[1024,2304]{1,0:T(8,128)(2,1)}, bf16[1024,768]{...) custom-call(s32[8]{0:T(128)} %len_ref.11, bf16[1024,1024]{1,0:T(8,128)(2,1)} %get-tuple-element.62.context_ref, ...), custom_call_target="tpu_custom_call" | custom-call | tf_op jit(solution)/shard_map/pallas_call | solution.py:459
  426.4 37.0 %shard_map.270 = (f32[1024,768]{1,0:T(8,128)}, bf16[1024,768]{1,0:T(8,128)(2,1)}, bf16[1024,3072]{1,0:T(8,128)(2,1)}, bf16[1024,768]{1,0:T(8,128)(2,1)}, bf16[10...) custom-call(f32[1024,768]{1,0:T(8,128)} %get-tuple-element.63.zhat2_ref, ...), custom_call_target="tpu_custom_call" | custom-call | tf_op jit(solution)/shard_map/pallas_call | solution.py:578
  463.5 24.9 %shard_map.280 = (bf16[1024,768]{1,0:T(8,128)(2,1)}, bf16[1024,2304]{1,0:T(8,128)(2,1)}, f32[1024,768]{1,0:T(8,128)}, bf16[1024,768]{1,0:T(8,128)(2,1)}, bf16[1024,1024]{1,0:T(8,128)(2,1)}, /*index=5*/f32[8,768]{1,0:T(8,128)}) custom-call(s32[8]{0:T(128)} %len_ref.11, f32[1024,768]{1,0:T(8,128)} %get-tuple-element.70.second_grad_ref, ...), custom_call_target="tpu_custom_call" | custom-call | tf_op jit(solution)/shard_map/pallas_call | solution.py:703
  538.6 14.2 %shard_map.273 = bf16[2,4,2,2,32,4096]{5,4,3,2,1,0:T(8,128)(2,1)} custom-call(s32[8]{0:T(128)} %stack.44.table_ref, bf16[4,2,32,4096]{3,2,1,0:T(8,128)(2,1)} %shard_map.272.refs_0_, bf16[4,2,32,4096]{3,2,1,0:T(8,128)(2,1)} %collective-permute-done.35.refs_1_, bf16[4,2,32,4096]{3,2,1,0:T(8,128)(2,1)} %collective-permute-done.36.refs_2_, ...), custom_call_target="tpu_custom_call" | custom-call | tf_op jit(solution)/shard_map/pallas_call | solution.py:92
  552.8 12.8 %shard_map.278 = (f32[384,1024]{1,0:T(8,128)}, f32[384,1]{1,0:T(8,128)}, bf16[384,1024]{1,0:T(8,128)(2,1)}, bf16[384,3072]{1,0:T(8,128)(2,1)}, bf16[384,1024]{1,...) custom-call(s32[8]{0:T(128)} %len_ref.11, bf16[384,1024]{1,0:T(8,128)(2,1)} %get-tuple-element.66.context_ref, ...), custom_call_target="tpu_custom_call" | custom-call | tf_op jit(solution)/shard_map/pallas_call | solution.py:459
  576.5 15.6 %shard_map.281 = (bf16[384,1024]{1,0:T(8,128)(2,1)}, bf16[384,3072]{1,0:T(8,128)(2,1)}, f32[384,1024]{1,0:T(8,128)}, bf16[384,1024]{1,0:T(8,128)(2,1)}, bf16[384,1024]{1,0:T(8,128)(2,1)}, /*index=5*/f32[8,1024]{1,0:T(8,128)}) custom-call(s32[8]{0:T(128)} %len_ref.11, f32[384,1024]{1,0:T(8,128)} %get-tuple-element.76.second_grad_ref, ...), custom_call_target="tpu_custom_call" | custom-call | tf_op jit(solution)/shard_map/pallas_call | solution.py:703
  593.0 14.7 %shard_map.282 = (bf16[1024,3072]{1,0:T(8,128)(2,1)}, bf16[384,3072]{1,0:T(8,128)(2,1)}, f32[1,3072]{1,0:T(1,128)}, f32[1,3072]{1,0:T(1,128)}) custom-call(s32[8]{0:T(128)} %len_ref.11, bf16[1024,3072]{1,0:T(8,128)(2,1)} %fusion.1.text_ref, bf16[384,3072]{1,0:T(8,128)(2,1)} %add_convert_fusion.1.image_ref, bf16[1024,1024]{1,0:T(8,128)(2,1)} %get-tuple-element.75.text_up, ...), custom_call_target="tpu_custom_call" | custom-call | tf_op jit(solution)/shard_map/pallas_call | solution.py:305
  670.3 12.0 %pad_maximum_fusion.1 = bf16[3072,1024]{1,0:T(8,128)(2,1)S(1)} fusion(bf16[1024,1024]{1,0:T(8,128)(2,1)S(1)} %convolution_convert_fusion.6, bf16[1024,1024]{1,0:T(8,128)(2,1)S(1)} %convolution_convert_fusion.7, bf16[1024,1024]{1,0:T(8,128)(2,1)S(1)} %copy-done.21), kind=kLoop, calls=%fused_computation.5 | loop fusion | flops 18874368 | bytes 12582912 | tf_op jit(solution)/shard_map/concatenate | solution.py:845
  827.5 12.8 %collective-permute-done.51 = bf16[4,24,3200]{2,1,0:T(8,128)(2,1)S(1)} collective-permute-done((bf16[4,24,3200]{2,1,0:T(8,128)(2,1)S(1)}, bf16[4,24,3200]{2,1,0:T(8,128)(2,1)S(1)}, u32[]{:S(2)}, u32[]{:S(2)}) %collective-permute-start.51) | collective-permute-done | bytes 614432 | tf_op jit(solution)/shard_map/ppermute | solution.py:58
  868.5 22.3 %collective-permute-done.80 = bf16[2,4,32,3072]{3,2,1,0:T(8,128)(2,1)} collective-permute-done((bf16[2,4,32,3072]{3,2,1,0:T(8,128)(2,1)}, bf16[2,4,32,3072]{3,2,1,0:T(8,128)(2,1)}, u32[]{:S(2)}, u32[]{:S(2)}) %collective-permute-start.80) | collective-permute-done | bytes 1572896 | tf_op jit(solution)/shard_map/ppermute | solution.py:58
  893.4 29.8 %collective-permute-done.74 = bf16[2,4,32,3072]{3,2,1,0:T(8,128)(2,1)} collective-permute-done((bf16[2,4,32,3072]{3,2,1,0:T(8,128)(2,1)}, bf16[2,4,32,3072]{3,2,1,0:T(8,128)(2,1)}, u32[]{:S(2)}, u32[]{:S(2)}) %collective-permute-start.74) | collective-permute-done | bytes 1572896 | tf_op jit(solution)/shard_map/ppermute | solution.py:58
  957.1 11.2 %collective-permute-start.96 = (bf16[96,1024]{1,0:T(8,128)(2,1)S(1)}, bf16[96,1024]{1,0:T(8,128)(2,1)S(1)}, u32[]{:S(2)}, u32[]{:S(2)}) collective-permute-start(bf16[96,1024]{1,0:T(8,128)(2,1)S(1)} %get-tuple-element.132), channel_id=1, source_target_pairs={{0,12},{1,13},{2,14},{3,15},{4,0},{5,1},{6,2},{7,3},{8,4},{9,5},{1... | collective-permute-start | bytes 589832 | tf_op jit(solution)/shard_map/ppermute | solution.py:68
  (560 shorter events, 578.7 us)
Async XLA Ops:
  81.1 51.8 %collective-permute-start.7 = (bf16[288,1024]{1,0:T(8,128)(2,1)}, bf16[288,1024]{1,0:T(8,128)(2,1)S(1)}, u32[]{:S(2)}, u32[]{:S(2)}) collective-permute-start(bf16[288,1024]{1,0:T(8,128)(2,1)} %param.16), channel_id=1, source_target_pairs={{0,16},{16,0},{1,17},{17,1},{2,18},{18,2},{3,19},{19,3},{4,20},{20... | collective-permute-start | bytes 1769480 | tf_op jit(solution)/shard_map/ppermute | solution.py:63
  174.9 64.6 %collective-permute-start.34 = (bf16[4,32,4096]{2,1,0:T(8,128)(2,1)}, bf16[4,32,4096]{2,1,0:T(8,128)(2,1)}, u32[]{:S(2)}, u32[]{:S(2)}) collective-permute-start(bf16[4,32,4096]{2,1,0:T(8,128)(2,1)} %shard_map.271.refs_0_), channel_id=1, source_target_pairs={{0,2},{1,3},{2,0},{3,1},{4,6},{5,7},{6,4},{7,5},{8,10},{9,11},{10,... | collective-permute-start | bytes 3145736 | tf_op jit(solution)/shard_map/ppermute | solution.py:58
  195.0 78.3 %collective-permute-start.5 = (bf16[4,2,24,3200]{3,2,1,0:T(8,128)(2,1)S(1)}, bf16[4,2,24,3200]{3,2,1,0:T(8,128)(2,1)S(1)}, u32[]{:S(2)}, u32[]{:S(2)}) collective-permute-start(bf16[4,2,24,3200]{3,2,1,0:T(8,128)(2,1)S(1)} %copy-done.13), channel_id=1, source_target_pairs={{0,1},{1,0},{2,3},{3,2},{4,5},{5,4},{6,7},{7,6},{8,9},{9,8},{10,11... | collective-permute-start | bytes 3686408 | tf_op jit(solution)/shard_map/ppermute | solution.py:53
  211.7 82.0 %collective-permute-start.6 = (bf16[4,2,24,3200]{3,2,1,0:T(8,128)(2,1)S(1)}, bf16[4,2,24,3200]{3,2,1,0:T(8,128)(2,1)}, u32[]{:S(2)}, u32[]{:S(2)}) collective-permute-start(bf16[4,2,24,3200]{3,2,1,0:T(8,128)(2,1)S(1)} %collective-permute-done.4.refs_1_), channel_id=1, source_target_pairs={{0,1},{1,0},{2,3},{3,2},{4,5},{5,4},{6,7},{7,6},{8,9},{9,8},{10,11... | collective-permute-start | bytes 3686408 | tf_op jit(solution)/shard_map/ppermute | solution.py:53
  217.1 56.2 %collective-permute-start.13 = (bf16[4,32,3072]{2,1,0:T(8,128)(2,1)}, bf16[4,32,3072]{2,1,0:T(8,128)(2,1)}, u32[]{:S(2)}, u32[]{:S(2)}) collective-permute-start(bf16[4,32,3072]{2,1,0:T(8,128)(2,1)} %collective-permute-done.12.refs_0_), channel_id=1, source_target_pairs={{0,2},{1,3},{2,0},{3,1},{4,6},{5,7},{6,4},{7,5},{8,10},{9,11},{10,... | collective-permute-start | bytes 2359304 | tf_op jit(solution)/shard_map/ppermute | solution.py:58
  239.6 54.2 %collective-permute-start.21 = (bf16[4,24,5376]{2,1,0:T(8,128)(2,1)}, bf16[4,24,5376]{2,1,0:T(8,128)(2,1)}, u32[]{:S(2)}, u32[]{:S(2)}) collective-permute-start(bf16[4,24,5376]{2,1,0:T(8,128)(2,1)} %collective-permute-done.20.refs_0_), channel_id=1, source_target_pairs={{0,2},{1,3},{2,0},{3,1},{4,6},{5,7},{6,4},{7,5},{8,10},{9,11},{10,... | collective-permute-start | bytes 3096584 | tf_op jit(solution)/shard_map/ppermute | solution.py:58
  256.4 66.7 %collective-permute-start.28 = (bf16[4,2,152,768]{3,2,1,0:T(8,128)(2,1)}, bf16[4,2,152,768]{3,2,1,0:T(8,128)(2,1)}, u32[]{:S(2)}, u32[]{:S(2)}) collective-permute-start(bf16[4,2,152,768]{3,2,1,0:T(8,128)(2,1)} %shard_map.267.refs_0_), channel_id=1, source_target_pairs={{0,16},{16,0},{1,17},{17,1},{2,18},{18,2},{3,19},{19,3},{4,20},{20... | collective-permute-start | bytes 5603336 | tf_op jit(solution)/shard_map/ppermute | solution.py:63
  321.6 57.9 %collective-permute-start.22 = (bf16[4,2,24,5376]{3,2,1,0:T(8,128)(2,1)}, bf16[4,2,24,5376]{3,2,1,0:T(8,128)(2,1)}, u32[]{:S(2)}, u32[]{:S(2)}) collective-permute-start(bf16[4,2,24,5376]{3,2,1,0:T(8,128)(2,1)} %shard_map.263.refs_0_), channel_id=1, source_target_pairs={{0,1},{1,0},{2,3},{3,2},{4,5},{5,4},{6,7},{7,6},{8,9},{9,8},{10,11... | collective-permute-start | bytes 6193160 | tf_op jit(solution)/shard_map/ppermute | solution.py:53
  321.6 58.2 %collective-permute-start.35 = (bf16[4,2,32,4096]{3,2,1,0:T(8,128)(2,1)S(1)}, bf16[4,2,32,4096]{3,2,1,0:T(8,128)(2,1)}, u32[]{:S(2)}, u32[]{:S(2)}) collective-permute-start(bf16[4,2,32,4096]{3,2,1,0:T(8,128)(2,1)S(1)} %copy-done.11), channel_id=1, source_target_pairs={{0,16},{16,0},{1,17},{17,1},{2,18},{18,2},{3,19},{19,3},{4,20},{20... | collective-permute-start | bytes 6291464 | tf_op jit(solution)/shard_map/ppermute | solution.py:63
  323.1 56.9 %collective-permute-start.23 = (bf16[4,2,24,5376]{3,2,1,0:T(8,128)(2,1)}, bf16[4,2,24,5376]{3,2,1,0:T(8,128)(2,1)}, u32[]{:S(2)}, u32[]{:S(2)}) collective-permute-start(bf16[4,2,24,5376]{3,2,1,0:T(8,128)(2,1)} %shard_map.264.refs_1_), channel_id=1, source_target_pairs={{0,1},{1,0},{2,3},{3,2},{4,5},{5,4},{6,7},{7,6},{8,9},{9,8},{10,11... | collective-permute-start | bytes 6193160 | tf_op jit(solution)/shard_map/ppermute | solution.py:53
  328.3 65.5 %collective-permute-start.29 = (bf16[4,2,152,768]{3,2,1,0:T(8,128)(2,1)}, bf16[4,2,152,768]{3,2,1,0:T(8,128)(2,1)}, u32[]{:S(2)}, u32[]{:S(2)}) collective-permute-start(bf16[4,2,152,768]{3,2,1,0:T(8,128)(2,1)} %shard_map.267.refs_0_), channel_id=1, source_target_pairs={{0,1},{1,0},{2,3},{3,2},{4,5},{5,4},{6,7},{7,6},{8,9},{9,8},{10,11... | collective-permute-start | bytes 5603336 | tf_op jit(solution)/shard_map/ppermute | solution.py:53
  328.7 65.1 %collective-permute-start.30 = (bf16[4,2,152,768]{3,2,1,0:T(8,128)(2,1)}, bf16[4,2,152,768]{3,2,1,0:T(8,128)(2,1)}, u32[]{:S(2)}, u32[]{:S(2)}) collective-permute-start(bf16[4,2,152,768]{3,2,1,0:T(8,128)(2,1)} %collective-permute-done.28.refs_1_), channel_id=1, source_target_pairs={{0,1},{1,0},{2,3},{3,2},{4,5},{5,4},{6,7},{7,6},{8,9},{9,8},{10,11... | collective-permute-start | bytes 5603336 | tf_op jit(solution)/shard_map/ppermute | solution.py:53
  379.5 159.1 %collective-permute-start.36 = (bf16[4,2,32,4096]{3,2,1,0:T(8,128)(2,1)S(1)}, bf16[4,2,32,4096]{3,2,1,0:T(8,128)(2,1)}, u32[]{:S(2)}, u32[]{:S(2)}) collective-permute-start(bf16[4,2,32,4096]{3,2,1,0:T(8,128)(2,1)S(1)} %copy-done.11), channel_id=1, source_target_pairs={{0,1},{1,0},{2,3},{3,2},{4,5},{5,4},{6,7},{7,6},{8,9},{9,8},{10,11... | collective-permute-start | bytes 6291464 | tf_op jit(solution)/shard_map/ppermute | solution.py:53
  379.8 158.8 %collective-permute-start.37 = (bf16[4,2,32,4096]{3,2,1,0:T(8,128)(2,1)}, bf16[4,2,32,4096]{3,2,1,0:T(8,128)(2,1)}, u32[]{:S(2)}, u32[]{:S(2)}) collective-permute-start(bf16[4,2,32,4096]{3,2,1,0:T(8,128)(2,1)} %collective-permute-done.35.refs_1_), channel_id=1, source_target_pairs={{0,1},{1,0},{2,3},{3,2},{4,5},{5,4},{6,7},{7,6},{8,9},{9,8},{10,11... | collective-permute-start | bytes 6291464 | tf_op jit(solution)/shard_map/ppermute | solution.py:53
  499.4 210.2 %collective-permute-start.55 = (bf16[2,4,2,24,2304]{4,3,1,2,0:T(8,128)(2,1)}, bf16[2,4,2,24,2304]{4,3,1,2,0:T(8,128)(2,1)}, u32[]{:S(2)}, u32[]{:S(2)}) collective-permute-start(bf16[2,4,2,24,2304]{4,3,1,2,0:T(8,128)(2,1)} %bitcast.290), channel_id=1, source_target_pairs={{0,1},{1,0},{2,3},{3,2},{4,5},{5,4},{6,7},{7,6},{8,9},{9,8},{10,11... | collective-permute-start | bytes 5308424 | tf_op jit(solution)/shard_map/ppermute | solution.py:53
  511.8 213.8 %collective-permute-start.61 = (bf16[2,4,2,24,3072]{4,3,1,0,2:T(8,128)(2,1)}, bf16[2,4,2,24,3072]{4,3,1,0,2:T(8,128)(2,1)}, u32[]{:S(2)}, u32[]{:S(2)}) collective-permute-start(bf16[2,4,2,24,3072]{4,3,1,0,2:T(8,128)(2,1)} %bitcast.289), channel_id=1, source_target_pairs={{0,1},{1,0},{2,3},{3,2},{4,5},{5,4},{6,7},{7,6},{8,9},{9,8},{10,11... | collective-permute-start | bytes 7077896 | tf_op jit(solution)/shard_map/ppermute | solution.py:53
  636.0 66.5 %collective-permute-start.47 = (bf16[288,1024]{1,0:T(8,128)(2,1)}, bf16[288,1024]{1,0:T(8,128)(2,1)}, u32[]{:S(2)}, u32[]{:S(2)}) collective-permute-start(bf16[288,1024]{1,0:T(8,128)(2,1)} %convert_element_type.487), channel_id=1, source_target_pairs={{0,16},{16,0},{1,17},{17,1},{2,18},{18,2},{3,19},{19,3},{4,20},{20... | collective-permute-start | bytes 1769480 | tf_op jit(solution)/shard_map/ppermute | solution.py:63
  644.0 63.2 %collective-permute-start.85 = (bf16[2,4,2,32,1024]{4,3,1,2,0:T(8,128)(2,1)}, bf16[2,4,2,32,1024]{4,3,1,2,0:T(8,128)(2,1)}, u32[]{:S(2)}, u32[]{:S(2)}) collective-permute-start(bf16[2,4,2,32,1024]{4,3,1,2,0:T(8,128)(2,1)} %bitcast.291), channel_id=1, source_target_pairs={{0,1},{1,0},{2,3},{3,2},{4,5},{5,4},{6,7},{7,6},{8,9},{9,8},{10,11... | collective-permute-start | bytes 3145736 | tf_op jit(solution)/shard_map/ppermute | solution.py:53
  702.5 53.3 %collective-permute-start.49 = (bf16[2,4,2,24,3200]{4,3,2,1,0:T(8,128)(2,1)S(1)}, bf16[2,4,2,24,3200]{4,3,2,1,0:T(8,128)(2,1)S(1)}, u32[]{:S(2)}, u32[]{:S(2)}) collective-permute-start(bf16[2,4,2,24,3200]{4,3,2,1,0:T(8,128)(2,1)S(1)} %dynamic-slice_bitcast_fusion), channel_id=1, source_target_pairs={{0,1},{1,0},{2,3},{3,2},{4,5},{5,4},{6,7},{7,6},{8,9},{9,8},{10,11... | collective-permute-start | bytes 7372808 | tf_op jit(solution)/shard_map/ppermute | solution.py:53
  786.3 140.7 %collective-permute-start.68 = (bf16[2,4,152,768]{3,2,1,0:T(8,128)(2,1)}, bf16[2,4,152,768]{3,2,1,0:T(8,128)(2,1)}, u32[]{:S(2)}, u32[]{:S(2)}) collective-permute-start(bf16[2,4,152,768]{3,2,1,0:T(8,128)(2,1)} %dynamic-slice_bitcast_fusion.1), channel_id=1, source_target_pairs={{0,2},{1,3},{2,0},{3,1},{4,6},{5,7},{6,4},{7,5},{8,10},{9,11},{10,... | collective-permute-start | bytes 5603336 | tf_op jit(solution)/shard_map/ppermute | solution.py:58
  793.7 70.4 %collective-permute-start.92 = (bf16[4,2,96,1024]{3,2,0,1:T(8,128)(2,1)}, bf16[4,2,96,1024]{3,2,0,1:T(8,128)(2,1)}, u32[]{:S(2)}, u32[]{:S(2)}) collective-permute-start(bf16[4,2,96,1024]{3,2,0,1:T(8,128)(2,1)} %dynamic-slice_bitcast_fusion.2), channel_id=1, source_target_pairs={{0,16},{16,0},{1,17},{17,1},{2,18},{18,2},{3,19},{19,3},{4,20},{20... | collective-permute-start | bytes 4718600 | tf_op jit(solution)/shard_map/ppermute | solution.py:63
  854.5 68.7 %collective-permute-start.74 = (bf16[2,4,32,3072]{3,2,1,0:T(8,128)(2,1)}, bf16[2,4,32,3072]{3,2,1,0:T(8,128)(2,1)}, u32[]{:S(2)}, u32[]{:S(2)}) collective-permute-start(bf16[2,4,32,3072]{3,2,1,0:T(8,128)(2,1)} %dynamic-slice_bitcast_fusion.4), channel_id=1, source_target_pairs={{0,2},{1,3},{2,0},{3,1},{4,6},{5,7},{6,4},{7,5},{8,10},{9,11},{10,... | collective-permute-start | bytes 4718600 | tf_op jit(solution)/shard_map/ppermute | solution.py:58
  866.9 64.6 %collective-permute-start.93 = (bf16[4,96,1024]{2,1,0:T(8,128)(2,1)S(1)}, bf16[4,96,1024]{2,1,0:T(8,128)(2,1)S(1)}, u32[]{:S(2)}, u32[]{:S(2)}) collective-permute-start(bf16[4,96,1024]{2,1,0:T(8,128)(2,1)S(1)} %dynamic-slice_bitcast_fusion.9), channel_id=1, source_target_pairs={{0,2},{1,3},{2,0},{3,1},{4,6},{5,7},{6,4},{7,5},{8,10},{9,11},{10,... | collective-permute-start | bytes 2359304 | tf_op jit(solution)/shard_map/ppermute | solution.py:58
  931.9 53.3 %collective-permute-start.94 = (bf16[96,1024]{1,0:T(8,128)(2,1)S(1)}, bf16[96,1024]{1,0:T(8,128)(2,1)S(1)}, u32[]{:S(2)}, u32[]{:S(2)}) collective-permute-start(bf16[96,1024]{1,0:T(8,128)(2,1)S(1)} %get-tuple-element.131), channel_id=1, source_target_pairs={{0,4},{1,5},{2,6},{3,7},{4,8},{5,9},{6,10},{7,11},{8,12},{9,13},{1... | collective-permute-start | bytes 589832 | tf_op jit(solution)/shard_map/ppermute | solution.py:68
  (152 other events, 3359.4 us)

commit v2 on v1

--- a/solution.py
+++ b/solution.py
@@ -42,6 +42,26 @@
     return pltpu.CompilerParams(vmem_limit_bytes=VMEM_LIMIT)
 
 
+def call(kernel, deps, operands, in_specs, **kwargs):
+    count = len(operands)
+
+    def body(*refs):
+        kernel(*refs[:count], *refs[count + len(deps) :])
+
+    return pl.pallas_call(
+        body,
+        in_specs=in_specs + [ANY] * len(deps),
+        compiler_params=params(),
+        **kwargs,
+    )(*operands, *deps)
+
+
+def cost(gmacs, mbytes):
+    return pl.CostEstimate(
+        flops=int(2e9 * gmacs), bytes_accessed=int(1e6 * mbytes), transcendentals=0
+    )
+
+
 def dp_parts():
     total = lax.axis_size("dp")
     index = lax.axis_index("dp")
@@ -72,108 +92,282 @@
     return lax.dynamic_index_in_dim(buffer, position, axis, keepdims=False)
 
 
-def place_kernel(table_ref, *refs):
-    pieces, out_ref = refs[:-1], refs[-1]
-    step = pl.program_id(0)
-    for number, piece in enumerate(pieces):
-
-        @pl.when(step == number)
-        def _(piece=piece):
-            out_ref[...] = piece[...]
-
-
-def place(shape, block_in, grid, steps, block_out, spot, pieces, table):
-    def read(number):
-        def index(i, j, table_ref):
-            return steps(jnp.where(i == number, j, jnp.where(i < number, 0, grid - 1)))
-
-        return pl.BlockSpec(block_in, index)
-
+def place_kernel(blocks, table_ref, *refs):
+    count = (len(refs) - 3) // 2
+    pieces, out_ref = refs[:count], refs[count]
+    held, in_sems, out_sems = refs[count + 1 : 2 * count + 1], refs[2 * count + 1], refs[2 * count + 2]
+    loads, stores = [], []
+    for number in range(count * blocks):
+        piece, block = number // blocks, number % blocks
+        x, y, c = [table_ref[3 * number + i] for i in range(3)]
+        loads.append(
+            pltpu.make_async_copy(pieces[piece].at[block], held[piece].at[block], in_sems.at[number])
+        )
+        stores.append(
+            pltpu.make_async_copy(
+                held[piece].at[block], out_ref.at[x, :, y, c], out_sems.at[number]
+            )
+        )
+    for load in loads:
+        load.start()
+    for load, store in zip(loads, stores):
+        load.wait()
+        store.start()
+    for store in stores:
+        store.wait()
+
+
+def place(pieces, table, deps):
+    blocks, nz, rows, cols = pieces[0].shape
+    size = 4 * len(pieces) * pieces[0].size
+    return call(
+        functools.partial(place_kernel, blocks),
+        deps,
+        (table, *pieces),
+        [SMEM] + [ANY] * len(pieces),
+        out_specs=ANY,
+        out_shape=jax.ShapeDtypeStruct((2, nz, 2, 2, rows, cols), pieces[0].dtype),
+        scratch_shapes=[pltpu.VMEM(piece.shape, piece.dtype) for piece in pieces]
+        + [pltpu.SemaphoreType.DMA((len(pieces) * blocks,))] * 2,
+        cost_estimate=pl.CostEstimate(flops=0, bytes_accessed=size, transcendentals=0),
+    )
+
+
+def table_of(rows):
+    return jnp.stack([jnp.asarray(v, jnp.int32) for row in rows for v in row])
+
+
+def z_groups():
+    total = lax.axis_size("dp")
+    return [[first + 4 * k for k in range(total // 4)] for first in range(4)]
+
+
+def after_kernel(*refs):
+    pass
+
+
+def after(block, *earlier):
     return pl.pallas_call(
-        place_kernel,
-        grid_spec=pltpu.PrefetchScalarGridSpec(
-            num_scalar_prefetch=1,
-            grid=(len(pieces), grid),
-            in_specs=[read(number) for number in range(len(pieces))],
-            out_specs=pl.BlockSpec(
-                block_out, lambda i, j, table_ref: spot(table_ref[2 * i], table_ref[2 * i + 1], j)
-            ),
-        ),
-        out_shape=jax.ShapeDtypeStruct(shape, pieces[0].dtype),
+        after_kernel,
+        in_specs=[ANY] * (1 + len(earlier)),
+        out_specs=ANY,
+        out_shape=jax.ShapeDtypeStruct(block.shape, block.dtype),
+        input_output_aliases={0: 0},
         compiler_params=params(),
-    )(table, *pieces)
-
-
-def table_of(pairs):
-    return jnp.stack([jnp.asarray(v, jnp.int32) for pair in pairs for v in pair])
-
-
-def gather_rows(own, y_first):
-    nz, z, y, c = dp_parts()
-    x = lax.axis_index("stream")
-    rows, cols = own.shape
-    column = place(
-        (nz, rows, cols),
-        (rows, cols),
-        1,
-        lambda j: (0, 0),
-        (None, rows, cols),
-        lambda p, q, j: (p, 0, 0),
-        [own] + [over_z(own, shift) for shift in range(1, nz)],
-        table_of([((z - shift) % nz, 0) for shift in range(nz)]),
-    )
-
-    def pair(first, second):
-        return place(
-            (nz, 2, rows, cols),
-            (nz, rows, cols),
-            1,
-            lambda j: (0, 0, 0),
-            (nz, None, rows, cols),
-            lambda p, q, j: (0, p, 0, 0),
-            [first, second],
-            table_of([(y, 0), (1 - y, 0)]),
-        )
-
-    plane = pair(column, over_y(column))
-    if y_first:
-        far = over_x(plane)
-    else:
-        over = over_x(column)
-        far = pair(over, over_y(over))
-    full = place(
-        (2, nz, 2, 2, rows, cols),
-        (None, 2, rows, cols),
-        nz,
-        lambda j: (j, 0, 0, 0),
-        (None, None, 2, None, rows, cols),
-        lambda p, q, j: (p, j, 0, q, 0, 0),
-        [plane, far, over_core(plane), over_core(far)],
-        table_of([(x, c), (1 - x, c), (x, 1 - c), (1 - x, 1 - c)]),
-    )
-    return full.reshape(-1, cols)
+        cost_estimate=pl.CostEstimate(flops=0, bytes_accessed=0, transcendentals=0),
+    )(block, *earlier)
+
+
+def column_by_permutes(own):
+    nz, z, _, _ = dp_parts()
+    came = jnp.stack([own] + [over_z(own, shift) for shift in range(1, nz)])
+    turned = jnp.concatenate([came[::-1]] * 2)
+    return lax.dynamic_slice_in_dim(turned, nz - 1 - z, nz, 0)
+
+
+def column_by_gather(own, rows, cols):
+    full = lax.all_gather(own, "dp", axis_index_groups=z_groups(), axis=0)
+    return full[:, :rows, :cols]
+
+
+class Gather:
+    def __init__(self, column, y_first):
+        self.column = column
+        self.links = (over_y, over_x) if y_first else (over_x, over_y)
+        self.y_first = y_first
+        self.over = self.links[0](column)
+
+    def second(self):
+        self.pair = jnp.stack([self.column, self.over])
+        self.far = self.links[1](self.pair)
+
+    def core(self):
+        self.others = [over_core(self.pair), over_core(self.far)]
+
+    def full(self, deps):
+        _, _, y, c = dp_parts()
+        x = lax.axis_index("stream")
+        table = []
+        for core in (0, 1):
+            for outer in (0, 1):
+                for inner in (0, 1):
+                    dx, dy = (outer, inner) if self.y_first else (inner, outer)
+                    table.append((x ^ dx, y ^ dy, c ^ core))
+        whole = place([self.pair, self.far] + self.others, table_of(table), deps)
+        return whole.reshape(-1, whole.shape[-1])
 
 
 def add_low(kept, came):
     return (kept.astype(F32) + came.astype(F32)).astype(BF)
 
 
-def scatter_rows(grad, y_first):
-    nz, z, y, c = dp_parts()
-    x = lax.axis_index("stream")
-    cols = grad.shape[1]
-    part = grad.reshape(2, nz, 2, 2, -1, cols)
-    part = add_low(pick(part, c, 3), over_core(pick(part, 1 - c, 3)))
-    if y_first:
-        part = add_low(pick(part, y, 2), over_y(pick(part, 1 - y, 2)))
-        part = add_low(pick(part, x, 0), over_x(pick(part, 1 - x, 0)))
+class Scatter:
+    def __init__(self, halves, y_first):
+        self.send, self.keep = halves
+        self.came = over_core(self.send)
+        self.axes = ("y", "x") if y_first else ("x", "y")
+
+    def link(self):
+        axis, self.axes = self.axes[0], self.axes[1:]
+        at = dp_parts()[2] if axis == "y" else lax.axis_index("stream")
+        self.send = add_low(pick(self.keep, 1 - at, 0), pick(self.came, 1 - at, 0))
+        self.keep = add_low(pick(self.keep, at, 0), pick(self.came, at, 0))
+        self.came = over_y(self.send) if axis == "y" else over_x(self.send)
+
+    def column_by_permutes(self):
+        nz, z, _, _ = dp_parts()
+        self.send = add_low(self.keep, self.came)
+        self.sum = pick(self.send, z, 0).astype(F32)
+        for shift in range(1, nz):
+            came = over_z(pick(self.send, (z + shift) % nz, 0), shift)
+            self.sum = self.sum + came.astype(F32)
+
+    def column(self):
+        self.send = add_low(self.keep, self.came)
+        self.sum = lax.psum_scatter(
+            self.send.reshape(-1, self.send.shape[-1]),
+            "dp",
+            axis_index_groups=z_groups(),
+            scatter_dimension=0,
+            tiled=True,
+        )
+
+    def total(self):
+        return self.sum.astype(F32)
+
+
+def store_halves(y_first, core_ref, send_ref, keep_ref, block, at):
+    columns, rows = send_ref.shape[:2]
+    nz = columns // 4
+
+    def store(even_ref, odd_ref):
+        for number in range(columns):
+            x, z, y = number // (2 * nz), number // 2 % nz, number % 2
+            spot = (y * 2 + x if y_first else x * 2 + y) * nz + z
+            start = 2 * number * rows
+            even_ref[spot, :, at] = block[start : start + rows].astype(BF)
+            odd_ref[spot, :, at] = block[start + rows : start + 2 * rows].astype(BF)
+
+    @pl.when(core_ref[0] == 0)
+    def _():
+        store(keep_ref, send_ref)
+
+    @pl.when(core_ref[0] == 1)
+    def _():
+        store(send_ref, keep_ref)
+
+
+def cols_grad_kernel(y_first, counts, tile, has_riders, core_ref, *refs):
+    segments = len(counts)
+    lhs, ups = refs[:segments], refs[segments : 2 * segments]
+    riders = refs[2 * segments] if has_riders else None
+    send_ref, keep_ref = refs[2 * segments + has_riders : 2 * segments + has_riders + 2]
+    turned = refs[2 * segments + has_riders + 2 :]
+    step = pl.program_id(0)
+
+    @pl.when(step == 0)
+    def _():
+        for flat, kept in zip(lhs, turned):
+            kept[...] = flat[...].T
+
+    first = 0
+    for count, kept, up in zip(counts, turned, ups):
+
+        @pl.when((step >= first) & (step < first + count))
+        def _(kept=kept, up=up):
+            at = pl.ds(pl.multiple_of(step * tile, 128), tile) if has_riders else slice(None)
+            store_halves(y_first, core_ref, send_ref, keep_ref, dot_nn(kept[...], up[...]), at)
+
+        first += count
+    if has_riders:
+
+        @pl.when(step == 0)
+        def _():
+            width = riders.shape[1]
+            start = sum(counts) * tile
+            store_halves(y_first, core_ref, send_ref, keep_ref, riders[...], slice(start, start + width))
+
+
+def half_shapes(shards, rows, cols):
+    return [jax.ShapeDtypeStruct((shards // 2, rows, cols), BF)] * 2
+
+
+def cols_grad(shards, y_first, segments, tile, riders=None, deps=()):
+    counts = [up.shape[1] // tile for _, up in segments]
+    width = segments[0][0].shape[1]
+    length = segments[0][0].shape[0]
+    rows = width // shards
+    total = sum(counts) * tile + (0 if riders is None else riders.shape[1])
+    starts = [sum(counts[:i]) for i in range(len(counts))]
+
+    def up_spec(start, count):
+        return pl.BlockSpec((length, tile), lambda j: (0, jnp.clip(j - start, 0, count - 1)))
+
+    whole = [pl.BlockSpec(lhs.shape, lambda j: (0, 0)) for lhs, _ in segments]
+    tiles = [up_spec(start, count) for start, count in zip(starts, counts)]
+    extra = [] if riders is None else [riders]
+    core = jnp.reshape(dp_parts()[3], (1,)).astype(jnp.int32)
+    if riders is None:
+        out = pl.BlockSpec((shards // 2, rows, tile), lambda j: (0, 0, j))
     else:
-        part = add_low(pick(part, x, 0), over_x(pick(part, 1 - x, 0)))
-        part = add_low(pick(part, y, 1), over_y(pick(part, 1 - y, 1)))
-    total = pick(part, z, 0).astype(F32)
-    for shift in range(1, nz):
-        total = total + over_z(pick(part, (z + shift) % nz, 0), shift).astype(F32)
-    return total
+        out = pl.BlockSpec((shards // 2, rows, total), lambda j: (0, 0, 0))
+    halves = call(
+        functools.partial(cols_grad_kernel, y_first, counts, tile, len(extra)),
+        deps,
+        (core,) + tuple(lhs for lhs, _ in segments) + tuple(up for _, up in segments) + tuple(extra),
+        [SMEM] + whole + tiles + [pl.BlockSpec(block.shape, lambda j: (0, 0)) for block in extra],
+        grid=(sum(counts),),
+        out_specs=[out, out],
+        out_shape=half_shapes(shards, rows, total),
+        scratch_shapes=[pltpu.VMEM((width, length), BF) for _ in segments],
+        cost_estimate=cost(1.3e-9 * length * width * total, 20),
+    )
+    return [half.reshape(2, 2, -1, rows, total) for half in halves]
+
+
+def rows_grad_kernel(y_first, segments, tile, core_ref, *refs):
+    lhs, ups = refs[:segments], refs[segments : 2 * segments]
+    send_ref, keep_ref, total = refs[2 * segments : 2 * segments + 3]
+    turned = refs[2 * segments + 3 :]
+
+    @pl.when(pl.program_id(0) == 0)
+    def _():
+        for flat, kept in zip(lhs, turned):
+            kept[...] = flat[...].T
+
+    start = 0
+    for kept, up in zip(turned, ups):
+        for row in range(0, kept.shape[0], 256):
+            total[start + row : start + row + 256] = dot_nn(kept[row : row + 256], up[...])
+        start += kept.shape[0]
+    store_halves(y_first, core_ref, send_ref, keep_ref, total, slice(None))
+
+
+def rows_grad(shards, y_first, segments, tile, deps=()):
+    length = segments[0][0].shape[0]
+    height = sum(lhs.shape[1] for lhs, _ in segments)
+    width = segments[0][1].shape[1]
+    rows = height // shards
+    core = jnp.reshape(dp_parts()[3], (1,)).astype(jnp.int32)
+    out = pl.BlockSpec((shards // 2, rows, tile), lambda j: (0, 0, j))
+    halves = call(
+        functools.partial(rows_grad_kernel, y_first, len(segments), tile),
+        deps,
+        (core,) + tuple(lhs for lhs, _ in segments) + tuple(up for _, up in segments),
+        [SMEM]
+        + [
+            pl.BlockSpec(lhs.shape, lambda j: (0, 0), pipeline_mode=pl.Buffered(1))
+            for lhs, _ in segments
+        ]
+        + [pl.BlockSpec((length, tile), lambda j: (0, j)) for _ in segments],
+        grid=(width // tile,),
+        out_specs=[out, out],
+        out_shape=half_shapes(shards, rows, width),
+        scratch_shapes=[pltpu.VMEM((height, tile), F32)]
+        + [pltpu.VMEM((lhs.shape[1], length), BF) for lhs, _ in segments],
+        cost_estimate=cost(1.3e-9 * length * height * width, 20),
+    )
+    return [half.reshape(2, 2, -1, rows, width) for half in halves]
 
 
 def softmax_rows(scores):
@@ -241,16 +435,18 @@
         out_ref[:, where] = context.astype(BF)
 
 
-def co_forward(lengths, text_co, image_co):
+def co_forward(lengths, text_co, image_co, deps):
     pairs = lengths.shape[0]
-    return pl.pallas_call(
+    return call(
         co_forward_kernel,
-        grid=(pairs,),
-        in_specs=[
+        deps,
+        (lengths, text_co, image_co,),
+        [
             SMEM,
             pl.BlockSpec((CAP, 3 * CO_W), lambda i: (i, 0)),
             pl.BlockSpec((SLOTS, 3 * CO_W), lambda i: (i, 0)),
         ],
+        grid=(pairs,),
         out_specs=[
             pl.BlockSpec((CAP, CO_W), lambda i: (i, 0)),
             pl.BlockSpec((SLOTS, CO_W), lambda i: (i, 0)),
@@ -259,8 +455,8 @@
             jax.ShapeDtypeStruct((pairs * CAP, CO_W), BF),
             jax.ShapeDtypeStruct((pairs * SLOTS, CO_W), BF),
         ],
-        compiler_params=params(),
-    )(lengths, text_co, image_co)
+        cost_estimate=cost(2 * lengths.shape[0] * 0.4, 8),
+    )
 
 
 def co_backward_kernel(
@@ -299,19 +495,21 @@
             store(image_out, image_sum, where, grad)
 
 
-def co_backward(lengths, text_co, image_co, text_up, image_up):
+def co_backward(lengths, text_co, image_co, text_up, image_up, deps):
     pairs = lengths.shape[0]
     wide = 3 * CO_W
-    return pl.pallas_call(
+    return call(
         co_backward_kernel,
-        grid=(pairs,),
-        in_specs=[
+        deps,
+        (lengths, text_co, image_co, text_up, image_up,),
+        [
             SMEM,
             pl.BlockSpec((CAP, wide), lambda i: (i, 0)),
             pl.BlockSpec((SLOTS, wide), lambda i: (i, 0)),
             pl.BlockSpec((CAP, CO_W), lambda i: (i, 0)),
             pl.BlockSpec((SLOTS, CO_W), lambda i: (i, 0)),
         ],
+        grid=(pairs,),
         out_specs=[
             pl.BlockSpec((CAP, wide), lambda i: (i, 0)),
             pl.BlockSpec((SLOTS, wide), lambda i: (i, 0)),
@@ -324,8 +522,8 @@
             jax.ShapeDtypeStruct((1, wide), F32),
             jax.ShapeDtypeStruct((1, wide), F32),
         ],
-        compiler_params=params(),
-    )(lengths, text_co, image_co, text_up, image_up)
+        cost_estimate=cost(2 * lengths.shape[0] * 0.5, 20),
+    )
 
 
 def fetch(step, copies):
@@ -333,8 +531,13 @@
     def _():
         for copy in copies:
             copy.start()
-        for copy in copies:
-            copy.wait()
+
+    def arrived(number):
+        @pl.when(step == 0)
+        def _():
+            copies[number].wait()
+
+    return arrived
 
 
 def text_units(len_ref, step, pair_count):
@@ -399,7 +602,7 @@
     step = pl.program_id(0)
     width = input_ref.shape[1]
     rows = input_ref.shape[0]
-    fetch(
+    arrived = fetch(
         step,
         [
             pltpu.make_async_copy(out_w_ref.at[pl.ds(0, CO_W)], wco, sems.at[0]),
@@ -407,6 +610,7 @@
             pltpu.make_async_copy(out_w_ref.at[pl.ds(CO_W, width)], wo, sems.at[2]),
         ],
     )
+    arrived(0)
     normed, inverse = norm_rows(
         input_ref[...].astype(F32) + dot_nn(context_ref[...], wco[...]) + bias_ref[0:1]
     )
@@ -415,6 +619,7 @@
     first = normed * gain_ref[0:1] + bias_ref[1:2]
     first_low = first.astype(BF)
     low1_ref[...] = first_low
+    arrived(1)
     for part in range(3):
         at = slice(part * width, part * width + width)
         piece = dot_nn(first_low, wqkv[:, at])
@@ -440,6 +645,7 @@
     for (where, lane, _), context in zip(places, attend_all(units, factor)):
         context = unhalve(context) if is_text else context
         attended_ref[where, lane : lane + 128] = context.astype(BF)
+    arrived(2)
     normed, inverse = norm_rows(first + dot_nn(attended_ref[...], wo[...]) + bias_ref[4:5])
     zhat2_ref[...] = normed
     inv2_ref[...] = inverse
@@ -453,13 +659,14 @@
     return pl.BlockSpec((rows, cols), lambda i: (0, 0))
 
 
-def attn_forward(is_text, block, lengths, context, inputs, proj, out_w, bias, gain):
+def attn_forward(is_text, block, lengths, context, inputs, proj, out_w, bias, gain, deps):
     rows, width = inputs.shape
     shape = jax.ShapeDtypeStruct
-    return pl.pallas_call(
+    return call(
         functools.partial(attn_forward_kernel, is_text, CO_W + width),
-        grid=(rows // block,),
-        in_specs=[
+        deps,
+        (lengths, context, inputs, proj, out_w, bias, gain,),
+        [
             SMEM,
             row_spec(block, CO_W),
             row_spec(block, width),
@@ -468,6 +675,7 @@
             whole_spec(8, width),
             whole_spec(3, width),
         ],
+        grid=(rows // block,),
         out_specs=[
             row_spec(block, width),
             row_spec(block, 1),
@@ -492,8 +700,8 @@
             pltpu.VMEM((width, width), BF),
             pltpu.SemaphoreType.DMA((3,)),
         ],
-        compiler_params=params(),
-    )(lengths, context, inputs, proj, out_w, bias, gain)
+        cost_estimate=cost(rows * width * width * 1.6e-8, 40),
+    )
 
 
 def ffn_kernel(
@@ -522,7 +730,7 @@
     step = pl.program_id(0)
     width = zhat2_ref.shape[1]
     hidden = wup.shape[1]
-    fetch(
+    arrived = fetch(
         step,
         [
             pltpu.make_async_copy(proj_ref.at[:, pl.ds(3 * width, hidden)], wup, sems.at[0]),
@@ -535,6 +743,8 @@
         sums_ref[...] = jnp.zeros_like(sums_ref)
         up_sum_ref[...] = jnp.zeros_like(up_sum_ref)
 
+    arrived(0)
+    arrived(1)
     second = zhat2_ref[...] * gain_ref[1:2] + bias_ref[5:6]
     second_low = second.astype(BF)
     low2_ref[...] = second_low
@@ -572,13 +782,14 @@
     sums_ref[5:6] += col_sum(second_grad)
 
 
-def ffn(block, chunk, hidden, zhat2, inv2, cot, proj, out_w, up_bias, bias, gain):
+def ffn(block, chunk, hidden, zhat2, inv2, cot, proj, out_w, up_bias, bias, gain, deps):
     rows, width = zhat2.shape
     shape = jax.ShapeDtypeStruct
-    return pl.pallas_call(
+    return call(
         functools.partial(ffn_kernel, chunk),
-        grid=(rows // block,),
-        in_specs=[
+        deps,
+        (zhat2, inv2, cot, proj, out_w, up_bias, bias, gain,),
+        [
             row_spec(block, width),
             row_spec(block, 1),
             row_spec(block, width),
@@ -588,6 +799,7 @@
             whole_spec(8, width),
             whole_spec(3, width),
         ],
+        grid=(rows // block,),
         out_specs=[
             row_spec(block, width),
             row_spec(block, width),
@@ -614,8 +826,8 @@
             pltpu.VMEM((block, hidden), F32),
             pltpu.SemaphoreType.DMA((2,)),
         ],
-        compiler_params=params(),
-    )(zhat2, inv2, cot, proj, out_w, up_bias, bias, gain)
+        cost_estimate=cost(rows * width * hidden * 6.5e-9, 40),
+    )
 
 
 def attn_backward_kernel(
@@ -642,7 +854,7 @@
 ):
     step = pl.program_id(0)
     rows, width = second_grad_ref.shape
-    fetch(
+    arrived = fetch(
         step,
         [
             pltpu.make_async_copy(out_w_ref.at[pl.ds(0, CO_W)], wco, sems.at[0]),
@@ -657,6 +869,7 @@
 
     second_low = second_grad_ref[...].astype(BF)
     second_low_ref[...] = second_low
+    arrived(2)
     upstream[...] = dot_nt(second_low, wo[...]).astype(BF)
 
     def lanes(part, lane):
@@ -678,6 +891,7 @@
         dq, dk, dv = grads
         for part, grad in enumerate((unhalve(dq) if is_text else dq, dk, dv)):
             triple_low_ref[where, lanes(part, lane)] = grad.astype(BF)
+    arrived(1)
     back = second_grad_ref[...]
     for part in range(3):
         at = slice(part * width, part * width + width)
@@ -694,16 +908,18 @@
     sums_ref[2:3] += col_sum(first_grad)
     first_low = first_grad.astype(BF)
     first_low_ref[...] = first_low
+    arrived(0)
     context_low_ref[...] = dot_nt(first_low, wco[...]).astype(BF)
 
 
-def attn_backward(is_text, block, lengths, second_grad, triple, zhat1, inv1, proj, out_w, gain):
+def attn_backward(is_text, block, lengths, second_grad, triple, zhat1, inv1, proj, out_w, gain, deps):
     rows, width = zhat1.shape
     shape = jax.ShapeDtypeStruct
-    return pl.pallas_call(
+    return call(
         functools.partial(attn_backward_kernel, is_text),
-        grid=(rows // block,),
-        in_specs=[
+        deps,
+        (lengths, second_grad, triple, zhat1, inv1, proj, out_w, gain,),
+        [
             SMEM,
             row_spec(block, width),
             row_spec(block, 3 * width),
@@ -713,6 +929,7 @@
             ANY,
             whole_spec(3, width),
         ],
+        grid=(rows // block,),
         out_specs=[
             row_spec(block, width),
             row_spec(block, 3 * width),
@@ -736,12 +953,8 @@
             pltpu.VMEM((block, width), BF),
             pltpu.SemaphoreType.DMA((3,)),
         ],
-        compiler_params=params(),
-    )(lengths, second_grad, triple, zhat1, inv1, proj, out_w, gain)
-
-
-def weight_grad(inputs, upstream):
-    return dot_tn(inputs, upstream).astype(BF)
+        cost_estimate=cost(rows * width * width * 1.6e-8, 40),
+    )
 
 
 def co_project(inputs, weight, wide):
@@ -783,12 +996,41 @@
     near_image = over_x(image_in)
     near_cot = over_x(image_cot)
 
-    t_co = gather_rows(jnp.concatenate([t_proj[:, : 3 * CO_W], riders], 1), True)
-    i_co = gather_rows(i_proj[:, : 3 * CO_W], False)
-    t_outw = gather_rows(t_out, True)
-    i_outw = gather_rows(i_out, False)
-    i_rest = gather_rows(i_proj[:, 3 * CO_W :], True)
-    t_rest = gather_rows(t_proj[:, 3 * CO_W :], False)
+    def padded(own, rows, cols):
+        return jnp.pad(own, ((0, rows - own.shape[0]), (0, cols - own.shape[1])))
+
+    def z_gather(own):
+        rows, cols = own.shape
+        short = (1 << 20) - 2 * rows * cols * dp_parts()[0]
+        if short > 0:
+            line = 2 * dp_parts()[0]
+            more_rows = -(-short // (line * cols * 8)) * 8
+            more_cols = -(-short // (line * rows * 128)) * 128
+            if more_rows * cols < more_cols * rows:
+                own = padded(own, rows + more_rows, cols)
+            else:
+                own = padded(own, rows, cols + more_cols)
+        return column_by_gather(own, rows, cols)
+
+    t_co_own = jnp.concatenate([t_proj[:, : 3 * CO_W], riders], 1)
+    t_co_column = column_by_permutes(t_co_own)
+    i_co_column = after(column_by_permutes(i_proj[:, : 3 * CO_W]), near_image, near_cot)
+    i_out_column, i_rest_column = z_gather(i_out), z_gather(i_proj[:, 3 * CO_W :])
+    t_out_column, t_rest_column = z_gather(t_out), z_gather(t_proj[:, 3 * CO_W :])
+    first = [Gather(t_co_column, True), Gather(i_co_column, False)]
+    for part in first:
+        part.second()
+    fars = [part.far for part in first]
+    second = [
+        Gather(after(i_out_column, *fars), True),
+        Gather(after(i_rest_column, *fars), False),
+    ]
+    for part in first:
+        part.core()
+    overs = [part.over for part in second]
+    t_co, i_co = [part.full(overs) for part in first]
+    for part in second:
+        part.second()
 
     shard_count = t_co.shape[0] // t_rows
     table = t_co[:, 3 * CO_W :].reshape(shard_count, -1)[:, : flat.shape[0]].astype(F32)
@@ -807,60 +1049,134 @@
     image_up = pad_pairs(near_cot)
     text_co = co_project(text_in, t_co, t_wide[0])
     image_co = co_project(image_rows, i_co, i_wide[0])
-    text_context, image_context = co_forward(lengths, text_co, image_co)
+    text_context, image_context = co_forward(
+        lengths, text_co, image_co, ()
+    )
+    fars = [part.far for part in second] + [image_context]
+    third = [
+        Gather(after(t_out_column, *fars), True),
+        Gather(after(t_rest_column, *fars), False),
+    ]
+    for part in second:
+        part.core()
+    overs = [part.over for part in third]
+    i_outw, i_rest = [part.full(overs) for part in second]
+    for part in third:
+        part.second()
 
     image_block = image_rows.shape[0]
-    streams = (
-        (True, 256, 512, text_context, text_in, text_cot, t_rest, t_outw, t_wide, t_rows8, t_gains),
-        (
-            False,
-            image_block,
-            512,
-            image_context,
-            image_rows,
-            image_up,
-            i_rest,
-            i_outw,
-            i_wide,
-            i_rows8,
-            i_gains,
+    image_hidden = i_wide.shape[1] - 2 * CO_W
+    zhat1, inv1, low1, triple, attended, zhat2, inv2 = attn_forward(
+        False,
+        image_block,
+        lengths,
+        image_context,
+        image_rows,
+        i_rest,
+        i_outw,
+        i_rows8,
+        i_gains,
+        (),
+    )
+    i_final, low2, active, third_low, hidden_low, second_grad, i_sums2, i_upsum = ffn(
+        image_block,
+        512,
+        image_hidden,
+        zhat2,
+        inv2,
+        image_up,
+        i_rest,
+        i_outw,
+        i_wide[:, 2 * CO_W :],
+        i_rows8,
+        i_gains,
+        (),
+    )
+    image_final = over_x(unpad_pairs(i_final).astype(BF))
+    second_low, triple_low, i_first, first_low, i_ctx, i_sums1 = attn_backward(
+        False, image_block, lengths, second_grad, triple, zhat1, inv1, i_rest, i_outw, i_gains, ()
+    )
+    i_rest_sum = Scatter(
+        cols_grad(shard_count, True, [(low1, triple_low), (low2, hidden_low)], 512), True
+    )
+    i_out_sum = Scatter(
+        rows_grad(
+            shard_count, False,
+            [(image_context, first_low), (attended, second_low), (active, third_low)],
+            256,
         ),
-    )
-    finished = []
-    for is_text, block, chunk, context, inputs, cot, rest, outw, wide, rows8, gains in streams:
-        width = inputs.shape[1]
-        hidden = wide.shape[1] - 2 * CO_W
-        zhat1, inv1, low1, triple, attended, zhat2, inv2 = attn_forward(
-            is_text, block, lengths, context, inputs, rest, outw, rows8, gains
-        )
-        final, low2, active, third_low, hidden_low, second_grad, sums2, up_sum = ffn(
-            block, chunk, hidden, zhat2, inv2, cot, rest, outw, wide[:, 2 * CO_W :], rows8, gains
-        )
-        up_grad = weight_grad(low2, hidden_low)
-        down_grad = weight_grad(active, third_low)
-        second_low, triple_low, first_grad, first_low, context_low, sums1 = attn_backward(
-            is_text, block, lengths, second_grad, triple, zhat1, inv1, rest, outw, gains
-        )
-        triple_grad = weight_grad(low1, triple_low)
-        out_grad = jnp.concatenate(
-            [weight_grad(context, first_low), weight_grad(attended, second_low), down_grad], 0
-        )
-        finished.append(
-            (final, first_grad, context_low, up_grad, triple_grad, out_grad, sums1, sums2, up_sum)
-        )
-    (
-        (t_final, t_first, t_ctx, t_up, t_qkv, t_outg, t_sums1, t_sums2, t_upsum),
-        (i_final, i_first, i_ctx, i_up, i_qkv, i_outg, i_sums1, i_sums2, i_upsum),
-    ) = finished
-
-    image_final = over_x(unpad_pairs(i_final).astype(BF)).astype(F32)
-
+        False,
+    )
+
+    for part in third:
+        part.core()
+    t_outw, t_rest = [part.full([i_first]) for part in third]
+
+    text_block = 256
+    text_hidden = t_wide.shape[1] - 2 * CO_W
+    zhat1, inv1, low1, triple, attended, zhat2, inv2 = attn_forward(
+        True,
+        text_block,
+        lengths,
+        text_context,
+        text_in,
+        t_rest,
+        t_outw,
+        t_rows8,
+        t_gains,
+        [i_rest_sum.keep, i_out_sum.keep, image_final],
+    )
+    i_rest_sum.link()
+    i_out_sum.link()
+    t_final, low2, active, third_low, hidden_low, second_grad, t_sums2, t_upsum = ffn(
+        text_block,
+        512,
+        text_hidden,
+        zhat2,
+        inv2,
+        text_cot,
+        t_rest,
+        t_outw,
+        t_wide[:, 2 * CO_W :],
+        t_rows8,
+        t_gains,
+        [i_rest_sum.send, i_out_sum.send],
+    )
+    i_rest_sum.link()
+    i_out_sum.link()
+    second_low, triple_low, t_first, first_low, t_ctx, t_sums1 = attn_backward(
+        True,
+        text_block,
+        lengths,
+        second_grad,
+        triple,
+        zhat1,
+        inv1,
+        t_rest,
+        t_outw,
+        t_gains,
+        [i_rest_sum.send, i_out_sum.send],
+    )
+    t_rest_sum = Scatter(
+        cols_grad(shard_count, False, [(low1, triple_low), (low2, hidden_low)], 768), False
+    )
+    t_out_sum = Scatter(
+        rows_grad(
+            shard_count, True,
+            [(text_context, first_low), (attended, second_low), (active, third_low)],
+            256,
+            [t_rest_sum.keep],
+        ),
+        True,
+    )
+    i_rest_sum.column()
+    i_out_sum.column()
+
+    t_rest_sum.link()
     t_co_grad, i_co_grad, t_co_sum, i_co_sum = co_backward(
-        lengths, text_co, image_co, t_ctx, i_ctx
-    )
-    text_grad = t_first + dot_nt(t_co_grad, t_co[:, : 3 * CO_W])
-    image_grad = i_first + dot_nt(i_co_grad, i_co)
-    image_grad = over_x(unpad_pairs(image_grad).astype(BF)).astype(F32)
+        lengths, text_co, image_co, t_ctx, i_ctx, [t_out_sum.keep, i_rest_sum.send, i_out_sum.send, t_rest_sum.send]
+    )
+    t_out_sum.link()
 
     def small_grads(sums1, sums2, up_sum, co_sum):
         wide = jnp.concatenate([co_sum[0, :CO_W], co_sum[0, 2 * CO_W :], up_sum[0]])
@@ -884,18 +1200,35 @@
             )
     packed = jnp.concatenate(packed, 1)
     count = packed.shape[1]
-    packed = jnp.pad(packed, ((0, 0), (0, extra * t_rows - count))).reshape(-1, extra).astype(BF)
-
-    t_up = scatter_rows(t_up, True)
-    i_up = scatter_rows(i_up, False)
-    t_qkv = scatter_rows(t_qkv, False)
-    i_qkv = scatter_rows(i_qkv, True)
-    t_outg = scatter_rows(t_outg, True)
-    i_outg = scatter_rows(i_outg, False)
-    i_cog = scatter_rows(weight_grad(image_rows, i_co_grad), True)
-    t_cog = scatter_rows(
-        jnp.concatenate([weight_grad(text_in, t_co_grad), packed], 1), False
-    )
+    packed = jnp.pad(packed, ((0, 0), (0, extra * t_rows - count))).reshape(-1, extra)
+
+    i_co_sums = Scatter(
+        cols_grad(
+            shard_count, True,
+            [(image_rows, i_co_grad)],
+            512,
+            deps=[t_rest_sum.send, t_out_sum.send],
+        ),
+        True,
+    )
+    t_co_sums = Scatter(
+        cols_grad(shard_count, False, [(text_in, t_co_grad)], 768, packed, [i_co_sums.keep]), False
+    )
+    i_co_sums.link()
+    t_co_sums.link()
+    image_grad = after(i_first, i_co_sums.send) + dot_nt(i_co_grad, i_co)
+    image_grad = over_x(unpad_pairs(image_grad).astype(BF)).astype(F32)
+    text_grad = after(t_first, t_co_sums.send) + dot_nt(t_co_grad, t_co[:, : 3 * CO_W])
+    t_rest_sum.link()
+    t_out_sum.link()
+    t_rest_sum.column()
+    t_out_sum.column()
+    i_co_sums.link()
+    t_co_sums.link()
+    i_co_sums.column_by_permutes()
+    t_co_sums.column_by_permutes()
+    image_final = image_final.astype(F32)
+    t_cog = t_co_sums.total()
 
     mine = t_cog[:, 3 * CO_W :].reshape(-1)
     outs = []
@@ -909,13 +1242,13 @@
         image_final,
         text_grad,
         image_grad,
-        jnp.concatenate([t_cog[:, : 3 * CO_W], t_qkv, t_up], 1),
-        t_outg,
+        jnp.concatenate([t_cog[:, : 3 * CO_W], t_rest_sum.total()], 1),
+        t_out_sum.total(),
         t_wide_g,
         t_rows_g,
         t_gain_g,
-        jnp.concatenate([i_cog, i_qkv, i_up], 1),
-        i_outg,
+        jnp.concatenate([i_co_sums.total(), i_rest_sum.total()], 1),
+        i_out_sum.total(),
         i_wide_g,
         i_rows_g,
         i_gain_g,

time: 1020 us -> 721 us (0.71); the launches traced: 999 us -> 712 us
  waiting for transfers between devices: 340 us -> 202 us
  starting transfers between devices: 145 us -> 70 us
  matrix products: 80.7 us -> 32.9 us
  local copies, waits for them, and re-layouts: 84.1 us -> 46.8 us
  Pallas kernels: 275 us -> 262 us
  between operations: 2.43 us -> 15.2 us
  other arithmetic: 71.9 us -> 83.7 us
    ppermute x17 -> x12, waiting for transfers between devices: 189 us -> 84.9 us  [over_y(): return lax.ppermute(block, 'dp', [(d, d ^ 2) for d in range(total)])]
    ppermute x42 -> x12, starting transfers between devices: 99.9 us -> 33.8 us  [over_z(): lax.ppermute(block, 'dp', [(d, (d + 4 * shift) % total) for d in range(to...]
    dot_general x12 -> x0, matrix products: 51.3 us -> none  [dot_tn(): lax.dot_general(a, b, (((0,), (0,)), ((), ())), preferred_element_type=F32)]
    ppermute x42 -> x12, waiting for transfers between devices: 96 us -> 49.1 us  [over_z(): lax.ppermute(block, 'dp', [(d, (d + 4 * shift) % total) for d in range(to...]
    dynamic_slice x14 -> x0, local copies, waits for them, and re-layouts: 31.6 us -> none  [pick(): return lax.dynamic_index_in_dim(buffer, position, axis, keepdims=False)]
    convert_element_type x24 -> x18, other arithmetic: 32.3 us -> 56.4 us  [add_low(): return (kept.astype(F32) + came.astype(F32)).astype(BF)]
    concatenate x6 -> x4, other arithmetic: 25.2 us -> 3.36 us  [the longest x2 1.43 us: column_by_permutes(): turned = jnp.concatenate([came[::-1]] * 2)]
    pallas_call x29 -> x27, Pallas kernels: 275 us -> 262 us  [the longest x20 262 us: call(): pl.pallas_call(body, in_specs=in_specs + [ANY] * len(deps), compiler_para...]
  transfers between devices with their start and end apart: 97 -> 66, of which waited for: 36 -> 24; matrix products, arithmetic and copies ran while one was open for 23% -> 21% of each run, Pallas kernels for 27% -> 31%
where the time goes in v2:
time: 721 us; the launch traced here: 712 us
  Pallas kernels  262 us (36%)
  waiting for transfers between devices  202 us (28%)
  other arithmetic  83.7 us (12%)
  starting transfers between devices  70 us (10%)
  local copies, waits for them, and re-layouts  46.8 us (6%)
  matrix products  32.9 us (5%)
  between operations  15.2 us (2%)
    pallas_call x20, Pallas kernels, call(): pl.pallas_call(body, in_specs=in_specs + [ANY] * len(deps), compiler_para...  262 us
    ppermute x12, waiting for transfers between devices, over_y(): return lax.ppermute(block, 'dp', [(d, d ^ 2) for d in range(total)])  84.9 us
    ppermute x16, waiting for transfers between devices, over_x(): return lax.ppermute(block, 'stream', [(d, d ^ 1) for d in range(total)])  63.1 us
    convert_element_type x18, other arithmetic, add_low(): return (kept.astype(F32) + came.astype(F32)).astype(BF)  56.4 us
    ppermute x12, waiting for transfers between devices, over_z(): lax.ppermute(block, 'dp', [(d, (d + 4 * shift) % total) for d in range(to...  49.1 us
    ppermute x12, starting transfers between devices, over_z(): lax.ppermute(block, 'dp', [(d, (d + 4 * shift) % total) for d in range(to...  33.8 us
    ppermute x16, starting transfers between devices, over_x(): return lax.ppermute(block, 'stream', [(d, d ^ 1) for d in range(total)])  19.4 us
    dot_general x2, matrix products, dot_nt(): lax.dot_general(a, b, (((1,), (1,)), ((), ())), preferred_element_type=F32)  16.9 us
  transfers between devices with their start and end apart: 66, of which 24 were waited for; matrix products, arithmetic and copies ran while one was open for 21% of the time, Pallas kernels for 31%

profile of v2, /device:TPU:0, one launch (start us, length us, event | category | flops | bytes accessed | tf_op | source)
XLA Modules:
  0.0 712.1 jit_solution(11666712227261735353)
XLA Ops:
  25.4 11.7 %collective-permute-done.1 = bf16[24,3200]{1,0:T(8,128)(2,1)S(1)} collective-permute-done((bf16[24,3200]{1,0:T(8,128)(2,1)S(1)}, bf16[24,3200]{1,0:T(8,128)(2,1)S(1)}, u32[]{:S(2)}, u32[]{:S(2)}) %collective-permute-start.1) | collective-permute-done | bytes 153632 | tf_op jit(solution)/shard_map/ppermute | solution.py:88
  42.0 20.8 %collective-permute-done.8 = bf16[32,3072]{1,0:T(8,128)(2,1)S(1)} collective-permute-done((bf16[32,3072]{1,0:T(8,128)(2,1)}, bf16[32,3072]{1,0:T(8,128)(2,1)S(1)}, u32[]{:S(2)}, u32[]{:S(2)}) %collective-permute-start.8) | collective-permute-done | bytes 196640 | tf_op jit(solution)/shard_map/ppermute | solution.py:88
  69.7 14.2 %collective-permute-done.12 = bf16[4,32,3072]{2,1,0:T(8,128)(2,1)S(1)} collective-permute-done((bf16[4,32,3072]{2,1,0:T(8,128)(2,1)}, bf16[4,32,3072]{2,1,0:T(8,128)(2,1)S(1)}, u32[]{:S(2)}, u32[]{:S(2)}) %collective-permute-start.12) | collective-permute-done | bytes 786464 | tf_op jit(solution)/shard_map/ppermute | solution.py:83
  89.0 23.6 %collective-permute-done.4.refs_1_.refs_2_ = bf16[2,4,24,3200]{3,2,1,0:T(8,128)(2,1)S(1)} collective-permute-done((bf16[2,4,24,3200]{3,2,1,0:T(8,128)(2,1)}, bf16[2,4,24,3200]{3,2,1,0:T(8,128)(2,1)S(1)}, u32[]{:S(2)}, u32[]{:S(2)}) %collective-permute-start.4) | collective-permute-done | bytes 1228832 | tf_op jit(solution)/shard_map/ppermute | solution.py:83
  151.0 9.4 %fusion.refs_1_ = bf16[1024,3072]{1,0:T(8,128)(2,1)} fusion(f32[3072]{0:T(1024)S(1)} %get-tuple-element.187, bf16[1024,768]{1,0:T(8,128)(2,1)S(1)} %copy-done.34, bf16[768,3200]{1,0:T(8,128)(2,1)} %bitcast.223), kind=kOutput, calls=%fused_computation.1 | convolution fusion | flops 4838129664 | bytes 12595200 | tf_op jit(solution)/shard_map/dot_general | solution.py:30
  173.4 10.1 %shard_map.259 = (bf16[1024,1024]{1,0:T(8,128)(2,1)}, bf16[384,1024]{1,0:T(8,128)(2,1)}) custom-call(s32[8]{0:T(128)} %refs_0_.11, bf16[1024,3072]{1,0:T(8,128)(2,1)} %fusion.refs_1_, bf16[384,3072]{1,0:T(8,128)(2,1)} %add_convert_fusion.1.refs_2_), custom_call_target="tpu_custom_call" | custom-call | flops 12800000000 | bytes 8000000 | tf_op jit(solution)/shard_map/pallas_call | solution.py:51
  183.5 14.7 %collective-permute-done.19.refs_2_ = bf16[2,4,32,4096]{3,2,1,0:T(8,128)(2,1)S(1)} collective-permute-done((bf16[2,4,32,4096]{3,2,1,0:T(8,128)(2,1)}, bf16[2,4,32,4096]{3,2,1,0:T(8,128)(2,1)S(1)}, u32[]{:S(2)}, u32[]{:S(2)}) %collective-permute-start.19) | collective-permute-done | bytes 2097184 | tf_op jit(solution)/shard_map/ppermute | solution.py:78
  204.0 17.0 %collective-permute-done.26.refs_5_ = bf16[4,152,768]{2,1,0:T(8,128)(2,1)S(1)} collective-permute-done((bf16[4,152,768]{2,1,0:T(8,128)(2,1)}, bf16[4,152,768]{2,1,0:T(8,128)(2,1)S(1)}, u32[]{:S(2)}, u32[]{:S(2)}) %collective-permute-start.26) | collective-permute-done | bytes 933920 | tf_op jit(solution)/shard_map/ppermute | solution.py:78
  244.5 11.6 %shard_map.264 = (f32[384,1024]{1,0:T(8,128)}, f32[384,1]{1,0:T(8,128)}, bf16[384,1024]{1,0:T(8,128)(2,1)}, bf16[384,3072]{1,0:T(8,128)(2,1)}, bf16[384,1024]{1,...) custom-call(s32[8]{0:T(128)} %refs_0_.11, bf16[384,1024]{1,0:T(8,128)(2,1)} %get-tuple-element.75.refs_3_.refs_1_, ...), custom_call_target="tpu_custom_call" | custom-call | flops 12884901888 | bytes 40000000 | tf_op jit(solution)/shard_map/pallas_call | solution.py:51
  256.2 11.2 %shard_map.265 = (f32[384,1024]{1,0:T(8,128)}, bf16[384,1024]{1,0:T(8,128)(2,1)}, bf16[384,1024]{1,0:T(8,128)(2,1)}, bf16[384,1024]{1,0:T(8,128)(2,1)}, bf16[384...) custom-call(f32[384,1024]{1,0:T(8,128)} %get-tuple-element.76.refs_0_, ...), custom_call_target="tpu_custom_call" | custom-call | flops 5234491392 | bytes 40000000 | tf_op jit(solution)/shard_map/pallas_call | solution.py:51
  267.4 16.4 %shard_map.266 = (bf16[384,1024]{1,0:T(8,128)(2,1)}, bf16[384,3072]{1,0:T(8,128)(2,1)}, f32[384,1024]{1,0:T(8,128)}, bf16[384,1024]{1,0:T(8,128)(2,1)}, bf16[384,1024]{1,0:T(8,128)(2,1)}, /*index=5*/f32[8,1024]{1,0:T(8,128)}) custom-call(s32[8]{0:T(128)} %refs_0_.11, f32[384,1024]{1,0:T(8,128)} %get-tuple-element.78.refs_1_, ...), custom_call_target="tpu_custom_call" | custom-call | flops 12884901888 | bytes 40000000 | tf_op jit(solution)/shard_map/pallas_call | solution.py:51
  283.9 11.5 %shard_map.269 = (bf16[16,32,4096]{2,1,0:T(8,128)(2,1)}, bf16[16,32,4096]{2,1,0:T(8,128)(2,1)}) custom-call(s32[1]{0:T(128)} %bitcast.2.refs_0_, bf16[384,1024]{1,0:T(8,128)(2,1)} %get-tuple-element.83.refs_1_, bf16[384,1024]{1,0:T(8,128)(2,1)} %get-tuple-element.84.refs_2_, bf16[384,3072]{1,0:T(8,128)(2,1)} %get-tuple-element.85.refs_3_, ...), custom_call_target="tpu_custom_call" | custom-call | flops 4187593216 | bytes 20000000 | tf_op jit(solution)/shard_map/pallas_call | solution.py:51
  327.8 19.5 %shard_map.271 = (f32[1024,768]{1,0:T(8,128)}, f32[1024,1]{1,0:T(8,128)}, bf16[1024,768]{1,0:T(8,128)(2,1)}, bf16[1024,2304]{1,0:T(8,128)(2,1)}, bf16[1024,768]{...) custom-call(s32[8]{0:T(128)} %refs_0_.11, bf16[1024,1024]{1,0:T(8,128)(2,1)} %get-tuple-element.74.refs_1_, ...), custom_call_target="tpu_custom_call" | custom-call | flops 19327352832 | bytes 40000000 | tf_op jit(solution)/shard_map/pallas_call | solution.py:51
  359.6 37.7 %shard_map.272 = (f32[1024,768]{1,0:T(8,128)}, bf16[1024,768]{1,0:T(8,128)(2,1)}, bf16[1024,3072]{1,0:T(8,128)(2,1)}, bf16[1024,768]{1,0:T(8,128)(2,1)}, bf16[10...) custom-call(f32[1024,768]{1,0:T(8,128)} %get-tuple-element.95.refs_0_, ...), custom_call_target="tpu_custom_call" | custom-call | flops 31406948352 | bytes 40000000 | tf_op jit(solution)/shard_map/pallas_call | solution.py:51
  408.0 26.4 %shard_map.273 = (bf16[1024,768]{1,0:T(8,128)(2,1)}, bf16[1024,2304]{1,0:T(8,128)(2,1)}, f32[1024,768]{1,0:T(8,128)}, bf16[1024,768]{1,0:T(8,128)(2,1)}, bf16[1024,1024]{1,0:T(8,128)(2,1)}, /*index=5*/f32[8,768]{1,0:T(8,128)}) custom-call(s32[8]{0:T(128)} %refs_0_.11, f32[1024,768]{1,0:T(8,128)} %get-tuple-element.100.refs_1_, ...), custom_call_target="tpu_custom_call" | custom-call | flops 19327352832 | bytes 40000000 | tf_op jit(solution)/shard_map/pallas_call | solution.py:51
  434.4 16.8 %shard_map.274 = (bf16[16,24,5376]{2,1,0:T(8,128)(2,1)}, bf16[16,24,5376]{2,1,0:T(8,128)(2,1)}) custom-call(s32[1]{0:T(128)} %bitcast.2.refs_0_, bf16[1024,768]{1,0:T(8,128)(2,1)} %get-tuple-element.112.refs_1_, bf16[1024,768]{1,0:T(8,128)(2,1)} %get-tuple-element.113.refs_2_, bf16[1024,2304]{1,0:T(8,128)(2,1)} %get-tuple-element.114.refs_3_, ...), custom_call_target="tpu_custom_call" | custom-call | flops 10992432128 | bytes 20000000 | tf_op jit(solution)/shard_map/pallas_call | solution.py:51
  451.2 18.1 %shard_map.275 = (bf16[16,152,768]{2,1,0:T(8,128)(2,1)}, bf16[16,152,768]{2,1,0:T(8,128)(2,1)}) custom-call(s32[1]{0:T(128)} %bitcast.2.refs_0_, bf16[1024,1024]{1,0:T(8,128)(2,1)} %get-tuple-element.74.refs_1_, bf16[1024,768]{1,0:T(8,128)(2,1)} %get-tuple-element.107.refs_2_, bf16[1024,3072]{1,0:T(8,128)(2,1)} %get-tuple-element.108.refs_3_, ...), custom_call_target="tpu_custom_call" | custom-call | flops 9945533440 | bytes 20000000 | tf_op jit(solution)/shard_map/pallas_call | solution.py:51
  471.9 17.6 %collective-permute-done.38 = bf16[4,96,1024]{2,1,0:T(8,128)(2,1)S(1)} collective-permute-done((bf16[4,96,1024]{2,1,0:T(8,128)(2,1)}, bf16[4,96,1024]{2,1,0:T(8,128)(2,1)S(1)}, u32[]{:S(2)}, u32[]{:S(2)}) %collective-permute-start.38) | collective-permute-done | bytes 786464 | tf_op jit(solution)/shard_map/ppermute | solution.py:78
  512.5 14.6 %shard_map.276 = (bf16[1024,3072]{1,0:T(8,128)(2,1)}, bf16[384,3072]{1,0:T(8,128)(2,1)}, f32[1,3072]{1,0:T(1,128)}, f32[1,3072]{1,0:T(1,128)}) custom-call(s32[8]{0:T(128)} %refs_0_.11, bf16[1024,3072]{1,0:T(8,128)(2,1)} %fusion.refs_1_, bf16[384,3072]{1,0:T(8,128)(2,1)} %add_convert_fusion.1.refs_2_, bf16[1024,1024]{1,0:T(8,128)(2,1)} %get-tuple-element.105.refs_3_, ...), custom_call_target="tpu_custom_call" | custom-call | flops 16000000000 | bytes 20000000 | tf_op jit(solution)/shard_map/pallas_call | solution.py:51
  538.3 10.9 %shard_map.278 = (bf16[16,24,3200]{2,1,0:T(8,128)(2,1)}, bf16[16,24,3200]{2,1,0:T(8,128)(2,1)}) custom-call(s32[1]{0:T(128)} %bitcast.2.refs_0_, bf16[1024,768]{1,0:T(8,128)(2,1)} %refs_1_.1, bf16[1024,3072]{1,0:T(8,128)(2,1)} %get-tuple-element.119.refs_2_, f32[768,128]{1,0:T(8,128)} %reshape.414.refs_3_, bf16[2,2,4,32,3072]{4,3,2,1,0:T(8,128)(2,1)} %bitcast.236), custom_call_target="tpu_custom_call" | custom-call | flops 6543114240 | bytes 20000000 | tf_op jit(solution)/shard_map/pallas_call | solution.py:51
  565.4 11.2 %collective-permute-done.52 = bf16[4,152,768]{2,1,0:T(8,128)(2,1)} collective-permute-done((bf16[4,152,768]{2,1,0:T(8,128)(2,1)S(1)}, bf16[4,152,768]{2,1,0:T(8,128)(2,1)}, u32[]{:S(2)}, u32[]{:S(2)}) %collective-permute-start.52) | collective-permute-done | bytes 933920 | tf_op jit(solution)/shard_map/ppermute | solution.py:83
  585.3 10.4 %fusion.59 = f32[1024,768]{1,0:T(8,128)} fusion(f32[1024,768]{1,0:T(8,128)} %shard_map.279, bf16[1024,3072]{1,0:T(8,128)(2,1)} %get-tuple-element.119.refs_2_, bf16[768,3200]{1,0:T(8,128)(2,1)} %bitcast.224), kind=kOutput, calls=%fused_computation.127 | convolution fusion | flops 4832624640 | bytes 17301504 | tf_op jit(solution)/shard_map/dot_general | solution.py:34
  627.7 19.8 %collective-permute-done.45 = bf16[4,24,3200]{2,1,0:T(8,128)(2,1)S(1)} collective-permute-done((bf16[4,24,3200]{2,1,0:T(8,128)(2,1)}, bf16[4,24,3200]{2,1,0:T(8,128)(2,1)S(1)}, u32[]{:S(2)}, u32[]{:S(2)}) %collective-permute-start.45) | collective-permute-done | bytes 614432 | tf_op jit(solution)/shard_map/ppermute | solution.py:78
  648.8 15.9 %collective-permute-start.46 = (bf16[24,3200]{1,0:T(8,128)(2,1)S(1)}, bf16[24,3200]{1,0:T(8,128)(2,1)S(1)}, u32[]{:S(2)}, u32[]{:S(2)}) collective-permute-start(bf16[24,3200]{1,0:T(8,128)(2,1)S(1)} %get-tuple-element.149), channel_id=1, source_target_pairs={{0,4},{1,5},{2,6},{3,7},{4,8},{5,9},{6,10},{7,11},{8,12},{9,13},{1... | collective-permute-start | bytes 460808 | tf_op jit(solution)/shard_map/ppermute | solution.py:88
  (360 shorter events, 306.0 us)
Async XLA Ops:
  7.2 105.4 %all-gather.11.cloned.1.call-start = ((), (), s32[]{:S(2)}) async-start(), calls=%async_computation.9 | async-start | bytes 1310720 | tf_op jit(solution)/shard_map/all_gather | solution.py:169
  9.0 110.0 %all-gather.9.cloned.1.call-start = ((), (), s32[]{:S(2)}) async-start(), calls=%async_computation.8 | async-start | bytes 1310720 | tf_op jit(solution)/shard_map/all_gather | solution.py:169
  25.4 104.3 %all-gather.15.cloned.1.call-start = ((), (), s32[]{:S(2)}) async-start(), calls=%async_computation.11 | async-start | bytes 1351680 | tf_op jit(solution)/shard_map/all_gather | solution.py:169
  88.9 111.5 %all-gather.13.cloned.1.call-start = ((), (), s32[]{:S(2)}) async-start(), calls=%async_computation.10 | async-start | bytes 1320960 | tf_op jit(solution)/shard_map/all_gather | solution.py:169
  88.9 49.2 %collective-permute-start.5 = (bf16[2,4,24,3200]{3,2,1,0:T(8,128)(2,1)}, bf16[2,4,24,3200]{3,2,1,0:T(8,128)(2,1)}, u32[]{:S(2)}, u32[]{:S(2)}) collective-permute-start(bf16[2,4,24,3200]{3,2,1,0:T(8,128)(2,1)} %pad_maximum_fusion.5.refs_1_), channel_id=1, source_target_pairs={{0,1},{1,0},{2,3},{3,2},{4,5},{5,4},{6,7},{7,6},{8,9},{9,8},{10,11... | collective-permute-start | bytes 3686408 | tf_op jit(solution)/shard_map/ppermute | solution.py:73
  123.3 430.7 %reduce-scatter.11.cloned.1.call-start = ((), (), s32[]{:S(2)}) async-start(), calls=%async_computation.7 | async-start | bytes 983040 | tf_op jit(solution)/shard_map/reduce_scatter | solution.py:227
  138.1 45.4 %collective-permute-start.18 = (bf16[2,4,96,1024]{3,2,1,0:T(8,128)(2,1)}, bf16[2,4,96,1024]{3,2,1,0:T(8,128)(2,1)}, u32[]{:S(2)}, u32[]{:S(2)}) collective-permute-start(bf16[2,4,96,1024]{3,2,1,0:T(8,128)(2,1)} %pad_maximum_fusion.4.refs_1_), channel_id=1, source_target_pairs={{0,16},{16,0},{1,17},{17,1},{2,18},{18,2},{3,19},{19,3},{4,20},{20... | collective-permute-start | bytes 4718600 | tf_op jit(solution)/shard_map/ppermute | solution.py:83
  150.9 47.3 %collective-permute-start.19 = (bf16[2,4,32,4096]{3,2,1,0:T(8,128)(2,1)}, bf16[2,4,32,4096]{3,2,1,0:T(8,128)(2,1)S(1)}, u32[]{:S(2)}, u32[]{:S(2)}) collective-permute-start(bf16[2,4,32,4096]{3,2,1,0:T(8,128)(2,1)} %pad_maximum_fusion.refs_1_), channel_id=1, source_target_pairs={{0,2},{1,3},{2,0},{3,1},{4,6},{5,7},{6,4},{7,5},{8,10},{9,11},{10,... | collective-permute-start | bytes 6291464 | tf_op jit(solution)/shard_map/ppermute | solution.py:78
  227.5 78.0 %collective-permute-start.30 = (bf16[2,4,152,768]{3,2,1,0:T(8,128)(2,1)}, bf16[2,4,152,768]{3,2,1,0:T(8,128)(2,1)}, u32[]{:S(2)}, u32[]{:S(2)}) collective-permute-start(bf16[2,4,152,768]{3,2,1,0:T(8,128)(2,1)} %pad_maximum_fusion.2.refs_1_), channel_id=1, source_target_pairs={{0,1},{1,0},{2,3},{3,2},{4,5},{5,4},{6,7},{7,6},{8,9},{9,8},{10,11... | collective-permute-start | bytes 5603336 | tf_op jit(solution)/shard_map/ppermute | solution.py:73
  229.1 54.7 %collective-permute-start.29 = (bf16[2,4,152,768]{3,2,1,0:T(8,128)(2,1)}, bf16[2,4,152,768]{3,2,1,0:T(8,128)(2,1)}, u32[]{:S(2)}, u32[]{:S(2)}) collective-permute-start(bf16[2,4,152,768]{3,2,1,0:T(8,128)(2,1)} %pad_maximum_fusion.2.refs_1_), channel_id=1, source_target_pairs={{0,16},{16,0},{1,17},{17,1},{2,18},{18,2},{3,19},{19,3},{4,20},{20... | collective-permute-start | bytes 5603336 | tf_op jit(solution)/shard_map/ppermute | solution.py:83
  230.6 65.3 %collective-permute-start.21 = (bf16[2,4,24,5376]{3,2,1,0:T(8,128)(2,1)}, bf16[2,4,24,5376]{3,2,1,0:T(8,128)(2,1)S(1)}, u32[]{:S(2)}, u32[]{:S(2)}) collective-permute-start(bf16[2,4,24,5376]{3,2,1,0:T(8,128)(2,1)} %pad_maximum_fusion.1.refs_1_), channel_id=1, source_target_pairs={{0,2},{1,3},{2,0},{3,1},{4,6},{5,7},{6,4},{7,5},{8,10},{9,11},{10,... | collective-permute-start | bytes 6193160 | tf_op jit(solution)/shard_map/ppermute | solution.py:78
  295.4 57.6 %collective-permute-start.33 = (bf16[2,2,4,32,4096]{4,3,2,1,0:T(8,128)(2,1)}, bf16[2,2,4,32,4096]{4,3,2,1,0:T(8,128)(2,1)}, u32[]{:S(2)}, u32[]{:S(2)}) collective-permute-start(bf16[2,2,4,32,4096]{4,3,2,1,0:T(8,128)(2,1)} %bitcast.274), channel_id=1, source_target_pairs={{0,1},{1,0},{2,3},{3,2},{4,5},{5,4},{6,7},{7,6},{8,9},{9,8},{10,11... | collective-permute-start | bytes 12582920 | tf_op jit(solution)/shard_map/ppermute | solution.py:73
  305.5 41.8 %collective-permute-start.34 = (bf16[2,2,4,96,1024]{4,3,2,1,0:T(8,128)(2,1)}, bf16[2,2,4,96,1024]{4,3,2,1,0:T(8,128)(2,1)}, u32[]{:S(2)}, u32[]{:S(2)}) collective-permute-start(bf16[2,2,4,96,1024]{4,3,2,1,0:T(8,128)(2,1)} %bitcast.278), channel_id=1, source_target_pairs={{0,1},{1,0},{2,3},{3,2},{4,5},{5,4},{6,7},{7,6},{8,9},{9,8},{10,11... | collective-permute-start | bytes 9437192 | tf_op jit(solution)/shard_map/ppermute | solution.py:73
  352.7 44.6 %collective-permute-start.36 = (bf16[2,4,96,1024]{3,2,1,0:T(8,128)(2,1)}, bf16[2,4,96,1024]{3,2,1,0:T(8,128)(2,1)}, u32[]{:S(2)}, u32[]{:S(2)}) collective-permute-start(bf16[2,4,96,1024]{3,2,1,0:T(8,128)(2,1)} %get-tuple-element.143.refs_9_), channel_id=1, source_target_pairs={{0,16},{16,0},{1,17},{17,1},{2,18},{18,2},{3,19},{19,3},{4,20},{20... | collective-permute-start | bytes 4718600 | tf_op jit(solution)/shard_map/ppermute | solution.py:83
  358.2 47.3 %collective-permute-start.35 = (bf16[2,4,32,4096]{3,2,1,0:T(8,128)(2,1)}, bf16[2,4,32,4096]{3,2,1,0:T(8,128)(2,1)}, u32[]{:S(2)}, u32[]{:S(2)}) collective-permute-start(bf16[2,4,32,4096]{3,2,1,0:T(8,128)(2,1)} %get-tuple-element.135.refs_8_), channel_id=1, source_target_pairs={{0,2},{1,3},{2,0},{3,1},{4,6},{5,7},{6,4},{7,5},{8,10},{9,11},{10,... | collective-permute-start | bytes 6291464 | tf_op jit(solution)/shard_map/ppermute | solution.py:78
  451.2 55.1 %collective-permute-start.39 = (bf16[2,2,4,24,5376]{4,3,2,1,0:T(8,128)(2,1)}, bf16[2,2,4,24,5376]{4,3,2,1,0:T(8,128)(2,1)}, u32[]{:S(2)}, u32[]{:S(2)}) collective-permute-start(bf16[2,2,4,24,5376]{4,3,2,1,0:T(8,128)(2,1)} %bitcast.275), channel_id=1, source_target_pairs={{0,1},{1,0},{2,3},{3,2},{4,5},{5,4},{6,7},{7,6},{8,9},{9,8},{10,11... | collective-permute-start | bytes 12386312 | tf_op jit(solution)/shard_map/ppermute | solution.py:73
  492.2 67.4 %reduce-scatter.9.cloned.1.call-start = ((), (), s32[]{:S(2)}) async-start(), calls=%async_computation.6 | async-start | bytes 1310720 | tf_op jit(solution)/shard_map/reduce_scatter | solution.py:227
  499.0 126.8 %reduce-scatter.7.cloned.1.call-start = ((), (), s32[]{:S(2)}) async-start(), calls=%async_computation.5 | async-start | bytes 1167360 | tf_op jit(solution)/shard_map/reduce_scatter | solution.py:227
  505.7 44.0 %collective-permute-start.51 = (bf16[2,4,152,768]{3,2,1,0:T(8,128)(2,1)}, bf16[2,4,152,768]{3,2,1,0:T(8,128)(2,1)}, u32[]{:S(2)}, u32[]{:S(2)}) collective-permute-start(bf16[2,4,152,768]{3,2,1,0:T(8,128)(2,1)} %get-tuple-element.139.refs_4_), channel_id=1, source_target_pairs={{0,2},{1,3},{2,0},{3,1},{4,6},{5,7},{6,4},{7,5},{8,10},{9,11},{10,... | collective-permute-start | bytes 5603336 | tf_op jit(solution)/shard_map/ppermute | solution.py:78
  510.8 50.7 %collective-permute-start.49 = (bf16[2,4,24,5376]{3,2,1,0:T(8,128)(2,1)}, bf16[2,4,24,5376]{3,2,1,0:T(8,128)(2,1)}, u32[]{:S(2)}, u32[]{:S(2)}) collective-permute-start(bf16[2,4,24,5376]{3,2,1,0:T(8,128)(2,1)} %get-tuple-element.137.refs_8_.refs_3_), channel_id=1, source_target_pairs={{0,16},{16,0},{1,17},{17,1},{2,18},{18,2},{3,19},{19,3},{4,20},{20... | collective-permute-start | bytes 6193160 | tf_op jit(solution)/shard_map/ppermute | solution.py:83
  549.2 46.5 %collective-permute-start.42 = (bf16[2,2,4,32,3072]{4,3,2,1,0:T(8,128)(2,1)}, bf16[2,2,4,32,3072]{4,3,2,1,0:T(8,128)(2,1)}, u32[]{:S(2)}, u32[]{:S(2)}) collective-permute-start(bf16[2,2,4,32,3072]{4,3,2,1,0:T(8,128)(2,1)} %bitcast.277), channel_id=1, source_target_pairs={{0,1},{1,0},{2,3},{3,2},{4,5},{5,4},{6,7},{7,6},{8,9},{9,8},{10,11... | collective-permute-start | bytes 9437192 | tf_op jit(solution)/shard_map/ppermute | solution.py:73
  563.9 51.2 %collective-permute-start.50 = (bf16[4,24,5376]{2,1,0:T(8,128)(2,1)}, bf16[4,24,5376]{2,1,0:T(8,128)(2,1)}, u32[]{:S(2)}, u32[]{:S(2)}) collective-permute-start(bf16[4,24,5376]{2,1,0:T(8,128)(2,1)} %fusion.31), channel_id=1, source_target_pairs={{0,2},{1,3},{2,0},{3,1},{4,6},{5,7},{6,4},{7,5},{8,10},{9,11},{10,... | collective-permute-start | bytes 3096584 | tf_op jit(solution)/shard_map/ppermute | solution.py:78
  579.4 100.8 %reduce-scatter.5.cloned.1.call-start = ((), (), s32[]{:S(2)}) async-start(), calls=%async_computation.4 | async-start | bytes 1290240 | tf_op jit(solution)/shard_map/reduce_scatter | solution.py:227
  600.4 68.4 %collective-permute-start.53 = (bf16[2,4,32,3072]{3,2,1,0:T(8,128)(2,1)}, bf16[2,4,32,3072]{3,2,1,0:T(8,128)(2,1)}, u32[]{:S(2)}, u32[]{:S(2)}) collective-permute-start(bf16[2,4,32,3072]{3,2,1,0:T(8,128)(2,1)} %get-tuple-element.141.refs_1_), channel_id=1, source_target_pairs={{0,2},{1,3},{2,0},{3,1},{4,6},{5,7},{6,4},{7,5},{8,10},{9,11},{10,... | collective-permute-start | bytes 4718600 | tf_op jit(solution)/shard_map/ppermute | solution.py:78
  (78 other events, 1366.5 us)
Sparse Core Ops, SparseCore 0:
  10.2 50.8 all-gather.10
  63.2 28.2 all-gather.8
  93.7 35.9 all-gather.14
  131.6 33.2 all-gather.12
  492.3 38.0 reduce-scatter.10
  533.2 26.3 reduce-scatter.8
  579.5 40.2 reduce-scatter.6
  622.1 40.0 reduce-scatter.4

commit v3 on v2

--- a/solution.py
+++ b/solution.py
@@ -1027,8 +1027,7 @@
     ]
     for part in first:
         part.core()
-    overs = [part.over for part in second]
-    t_co, i_co = [part.full(overs) for part in first]
+    t_co, i_co = [part.full(()) for part in first]
     for part in second:
         part.second()
 
@@ -1059,8 +1058,7 @@
     ]
     for part in second:
         part.core()
-    overs = [part.over for part in third]
-    i_outw, i_rest = [part.full(overs) for part in second]
+    i_outw, i_rest = [part.full(()) for part in second]
     for part in third:
         part.second()
 
@@ -1142,6 +1140,8 @@
         t_gains,
         [i_rest_sum.send, i_out_sum.send],
     )
+    i_rest_sum.came = after(i_rest_sum.came, second_grad)
+    i_out_sum.came = after(i_out_sum.came, second_grad)
     i_rest_sum.link()
     i_out_sum.link()
     second_low, triple_low, t_first, first_low, t_ctx, t_sums1 = attn_backward(
@@ -1157,8 +1157,12 @@
         t_gains,
         [i_rest_sum.send, i_out_sum.send],
     )
+    i_rest_sum.came = after(i_rest_sum.came, t_ctx)
+    i_out_sum.came = after(i_out_sum.came, t_ctx)
+    i_rest_sum.column()
+    i_out_sum.column()
     t_rest_sum = Scatter(
-        cols_grad(shard_count, False, [(low1, triple_low), (low2, hidden_low)], 768), False
+        cols_grad(shard_count, False, [(low1, triple_low), (low2, hidden_low)], 768, None, [i_rest_sum.send, i_out_sum.send]), False
     )
     t_out_sum = Scatter(
         rows_grad(
@@ -1169,13 +1173,12 @@
         ),
         True,
     )
-    i_rest_sum.column()
-    i_out_sum.column()
 
     t_rest_sum.link()
     t_co_grad, i_co_grad, t_co_sum, i_co_sum = co_backward(
-        lengths, text_co, image_co, t_ctx, i_ctx, [t_out_sum.keep, i_rest_sum.send, i_out_sum.send, t_rest_sum.send]
-    )
+        lengths, text_co, image_co, t_ctx, i_ctx, [t_out_sum.keep, t_rest_sum.send]
+    )
+    t_out_sum.came = after(t_out_sum.came, t_rest_sum.send)
     t_out_sum.link()
 
     def small_grads(sums1, sums2, up_sum, co_sum):
@@ -1215,12 +1218,14 @@
         cols_grad(shard_count, False, [(text_in, t_co_grad)], 768, packed, [i_co_sums.keep]), False
     )
     i_co_sums.link()
+    t_co_sums.came = after(t_co_sums.came, i_co_sums.send)
     t_co_sums.link()
     image_grad = after(i_first, i_co_sums.send) + dot_nt(i_co_grad, i_co)
     image_grad = over_x(unpad_pairs(image_grad).astype(BF)).astype(F32)
     text_grad = after(t_first, t_co_sums.send) + dot_nt(t_co_grad, t_co[:, : 3 * CO_W])
     t_rest_sum.link()
     t_out_sum.link()
+    t_out_sum.came = after(t_out_sum.came, t_co_sums.send)
     t_rest_sum.column()
     t_out_sum.column()
     i_co_sums.link()

time: 721 us -> 700 us (0.971)
  waiting for transfers between devices: 202 us -> 177 us
    ppermute x12, waiting for transfers between devices: 84.9 us -> 63.4 us  [over_y(): return lax.ppermute(block, 'dp', [(d, d ^ 2) for d in range(total)])]
    ppermute x12, waiting for transfers between devices: 49.1 us -> 37.3 us  [over_z(): lax.ppermute(block, 'dp', [(d, (d + 4 * shift) % total) for d in range(to...]
    ppermute x16, waiting for transfers between devices: 63.1 us -> 74.5 us  [over_x(): return lax.ppermute(block, 'stream', [(d, d ^ 1) for d in range(total)])]
  transfers between devices with their start and end apart: 66 -> 66, of which waited for: 24 -> 22; matrix products, arithmetic and copies ran while one was open for 21% -> 22% of each run, Pallas kernels for 31% -> 35%
where the time goes in v3:
time: 700 us; the launch traced here: 690 us
  Pallas kernels  261 us (37%)
  waiting for transfers between devices  177 us (25%)
  other arithmetic  90.1 us (13%)
  starting transfers between devices  69.4 us (10%)
  local copies, waits for them, and re-layouts  46.4 us (7%)
  matrix products  30.4 us (4%)
  between operations  15.5 us (2%)
    pallas_call x20, Pallas kernels, call(): pl.pallas_call(body, in_specs=in_specs + [ANY] * len(deps), compiler_para...  261 us
    ppermute x16, waiting for transfers between devices, over_x(): return lax.ppermute(block, 'stream', [(d, d ^ 1) for d in range(total)])  74.5 us
    ppermute x12, waiting for transfers between devices, over_y(): return lax.ppermute(block, 'dp', [(d, d ^ 2) for d in range(total)])  63.4 us
    convert_element_type x18, other arithmetic, add_low(): return (kept.astype(F32) + came.astype(F32)).astype(BF)  60 us
    ppermute x12, waiting for transfers between devices, over_z(): lax.ppermute(block, 'dp', [(d, (d + 4 * shift) % total) for d in range(to...  37.3 us
    ppermute x12, starting transfers between devices, over_z(): lax.ppermute(block, 'dp', [(d, (d + 4 * shift) % total) for d in range(to...  30.4 us
    ppermute x16, starting transfers between devices, over_x(): return lax.ppermute(block, 'stream', [(d, d ^ 1) for d in range(total)])  19.7 us
    dot_general x2, matrix products, dot_nt(): lax.dot_general(a, b, (((1,), (1,)), ((), ())), preferred_element_type=F32)  16.8 us
  transfers between devices with their start and end apart: 66, of which 22 were waited for; matrix products, arithmetic and copies ran while one was open for 22% of the time, Pallas kernels for 35%

profile of v3, /device:TPU:0, one launch (start us, length us, event | category | flops | bytes accessed | tf_op | source)
XLA Modules:
  0.0 690.2 jit_solution(12791912085112804820)
XLA Ops:
  34.8 16.8 %collective-permute-done.1 = bf16[24,3200]{1,0:T(8,128)(2,1)S(1)} collective-permute-done((bf16[24,3200]{1,0:T(8,128)(2,1)S(1)}, bf16[24,3200]{1,0:T(8,128)(2,1)S(1)}, u32[]{:S(2)}, u32[]{:S(2)}) %collective-permute-start.1) | collective-permute-done | bytes 153632 | tf_op jit(solution)/shard_map/ppermute | solution.py:88
  69.0 17.1 %collective-permute-done.12 = bf16[4,32,3072]{2,1,0:T(8,128)(2,1)S(1)} collective-permute-done((bf16[4,32,3072]{2,1,0:T(8,128)(2,1)}, bf16[4,32,3072]{2,1,0:T(8,128)(2,1)S(1)}, u32[]{:S(2)}, u32[]{:S(2)}) %collective-permute-start.12) | collective-permute-done | bytes 786464 | tf_op jit(solution)/shard_map/ppermute | solution.py:83
  89.8 17.2 %collective-permute-done.4.refs_2_.refs_1_ = bf16[2,4,24,3200]{3,2,1,0:T(8,128)(2,1)S(1)} collective-permute-done((bf16[2,4,24,3200]{3,2,1,0:T(8,128)(2,1)S(1)}, bf16[2,4,24,3200]{3,2,1,0:T(8,128)(2,1)S(1)}, u32[]{:S(2)}, u32[]{:S(2)}) %collective-permute-start.4) | collective-permute-done | bytes 1228832 | tf_op jit(solution)/shard_map/ppermute | solution.py:83
  137.4 8.6 %collective-permute-done.16 = bf16[4,96,1024]{2,1,0:T(8,128)(2,1)} collective-permute-done((bf16[4,96,1024]{2,1,0:T(8,128)(2,1)}, bf16[4,96,1024]{2,1,0:T(8,128)(2,1)}, u32[]{:S(2)}, u32[]{:S(2)}) %collective-permute-start.16) | collective-permute-done | bytes 786464 | tf_op jit(solution)/shard_map/ppermute | solution.py:78
  170.3 12.2 %collective-permute-done.17.refs_1_.refs_2_ = bf16[2,4,96,1024]{3,2,1,0:T(8,128)(2,1)} collective-permute-done((bf16[2,4,96,1024]{3,2,1,0:T(8,128)(2,1)}, bf16[2,4,96,1024]{3,2,1,0:T(8,128)(2,1)}, u32[]{:S(2)}, u32[]{:S(2)}) %collective-permute-start.17) | collective-permute-done | bytes 1572896 | tf_op jit(solution)/shard_map/ppermute | solution.py:83
  189.5 10.8 %shard_map.257 = (bf16[1024,1024]{1,0:T(8,128)(2,1)}, bf16[384,1024]{1,0:T(8,128)(2,1)}) custom-call(s32[8]{0:T(128)} %refs_0_.11, bf16[1024,3072]{1,0:T(8,128)(2,1)} %fusion.refs_1_, bf16[384,3072]{1,0:T(8,128)(2,1)} %add_convert_fusion.1.refs_2_), custom_call_target="tpu_custom_call" | custom-call | flops 12800000000 | bytes 8000000 | tf_op jit(solution)/shard_map/pallas_call | solution.py:51
  239.8 11.6 %shard_map.263 = (f32[384,1024]{1,0:T(8,128)}, f32[384,1]{1,0:T(8,128)}, bf16[384,1024]{1,0:T(8,128)(2,1)}, bf16[384,3072]{1,0:T(8,128)(2,1)}, bf16[384,1024]{1,...) custom-call(s32[8]{0:T(128)} %refs_0_.11, bf16[384,1024]{1,0:T(8,128)(2,1)} %get-tuple-element.75.refs_3_.refs_1_, ...), custom_call_target="tpu_custom_call" | custom-call | flops 12884901888 | bytes 40000000 | tf_op jit(solution)/shard_map/pallas_call | solution.py:51
  251.4 10.8 %shard_map.264 = (f32[384,1024]{1,0:T(8,128)}, bf16[384,1024]{1,0:T(8,128)(2,1)}, bf16[384,1024]{1,0:T(8,128)(2,1)}, bf16[384,1024]{1,0:T(8,128)(2,1)}, bf16[384...) custom-call(f32[384,1024]{1,0:T(8,128)} %get-tuple-element.76.refs_0_, ...), custom_call_target="tpu_custom_call" | custom-call | flops 5234491392 | bytes 40000000 | tf_op jit(solution)/shard_map/pallas_call | solution.py:51
  262.2 16.4 %shard_map.265 = (bf16[384,1024]{1,0:T(8,128)(2,1)}, bf16[384,3072]{1,0:T(8,128)(2,1)}, f32[384,1024]{1,0:T(8,128)}, bf16[384,1024]{1,0:T(8,128)(2,1)}, bf16[384,1024]{1,0:T(8,128)(2,1)}, /*index=5*/f32[8,1024]{1,0:T(8,128)}) custom-call(s32[8]{0:T(128)} %refs_0_.11, f32[384,1024]{1,0:T(8,128)} %get-tuple-element.78.refs_1_, ...), custom_call_target="tpu_custom_call" | custom-call | flops 12884901888 | bytes 40000000 | tf_op jit(solution)/shard_map/pallas_call | solution.py:51
  278.7 11.4 %shard_map.269 = (bf16[16,32,4096]{2,1,0:T(8,128)(2,1)}, bf16[16,32,4096]{2,1,0:T(8,128)(2,1)}) custom-call(s32[1]{0:T(128)} %bitcast.2.refs_0_, bf16[384,1024]{1,0:T(8,128)(2,1)} %get-tuple-element.83.refs_1_, bf16[384,1024]{1,0:T(8,128)(2,1)} %get-tuple-element.84.refs_2_, bf16[384,3072]{1,0:T(8,128)(2,1)} %get-tuple-element.85.refs_3_, ...), custom_call_target="tpu_custom_call" | custom-call | flops 4187593216 | bytes 20000000 | tf_op jit(solution)/shard_map/pallas_call | solution.py:51
  291.0 8.9 %shard_map.270 = (bf16[16,96,1024]{2,1,0:T(8,128)(2,1)}, bf16[16,96,1024]{2,1,0:T(8,128)(2,1)}) custom-call(s32[1]{0:T(128)} %bitcast.2.refs_0_, bf16[384,1024]{1,0:T(8,128)(2,1)} %get-tuple-element.75.refs_3_.refs_1_, bf16[384,1024]{1,0:T(8,128)(2,1)} %get-tuple-element.88.refs_2_, bf16[384,1024]{1,0:T(8,128)(2,1)} %get-tuple-element.89.refs_3_, ...), custom_call_target="tpu_custom_call" | custom-call | flops 3140694784 | bytes 20000000 | tf_op jit(solution)/shard_map/pallas_call | solution.py:51
  322.8 19.3 %shard_map.271 = (f32[1024,768]{1,0:T(8,128)}, f32[1024,1]{1,0:T(8,128)}, bf16[1024,768]{1,0:T(8,128)(2,1)}, bf16[1024,2304]{1,0:T(8,128)(2,1)}, bf16[1024,768]{...) custom-call(s32[8]{0:T(128)} %refs_0_.11, bf16[1024,1024]{1,0:T(8,128)(2,1)} %get-tuple-element.74.refs_1_, ...), custom_call_target="tpu_custom_call" | custom-call | flops 19327352832 | bytes 40000000 | tf_op jit(solution)/shard_map/pallas_call | solution.py:51
  355.9 37.7 %shard_map.272 = (f32[1024,768]{1,0:T(8,128)}, bf16[1024,768]{1,0:T(8,128)(2,1)}, bf16[1024,3072]{1,0:T(8,128)(2,1)}, bf16[1024,768]{1,0:T(8,128)(2,1)}, bf16[10...) custom-call(f32[1024,768]{1,0:T(8,128)} %get-tuple-element.95.refs_0_, ...), custom_call_target="tpu_custom_call" | custom-call | flops 31406948352 | bytes 40000000 | tf_op jit(solution)/shard_map/pallas_call | solution.py:51
  406.6 26.8 %shard_map.275 = (bf16[1024,768]{1,0:T(8,128)(2,1)}, bf16[1024,2304]{1,0:T(8,128)(2,1)}, f32[1024,768]{1,0:T(8,128)}, bf16[1024,768]{1,0:T(8,128)(2,1)}, bf16[1024,1024]{1,0:T(8,128)(2,1)}, /*index=5*/f32[8,768]{1,0:T(8,128)}) custom-call(s32[8]{0:T(128)} %refs_0_.11, f32[1024,768]{1,0:T(8,128)} %get-tuple-element.100.refs_1_, ...), custom_call_target="tpu_custom_call" | custom-call | flops 19327352832 | bytes 40000000 | tf_op jit(solution)/shard_map/pallas_call | solution.py:51
  439.1 16.5 %shard_map.278 = (bf16[16,24,5376]{2,1,0:T(8,128)(2,1)}, bf16[16,24,5376]{2,1,0:T(8,128)(2,1)}) custom-call(s32[1]{0:T(128)} %bitcast.2.refs_0_, bf16[1024,768]{1,0:T(8,128)(2,1)} %get-tuple-element.112.refs_1_, bf16[1024,768]{1,0:T(8,128)(2,1)} %get-tuple-element.113.refs_2_, bf16[1024,2304]{1,0:T(8,128)(2,1)} %get-tuple-element.114.refs_3_, ...), custom_call_target="tpu_custom_call" | custom-call | flops 10992432128 | bytes 20000000 | tf_op jit(solution)/shard_map/pallas_call | solution.py:51
  455.7 18.0 %shard_map.279 = (bf16[16,152,768]{2,1,0:T(8,128)(2,1)}, bf16[16,152,768]{2,1,0:T(8,128)(2,1)}) custom-call(s32[1]{0:T(128)} %bitcast.2.refs_0_, bf16[1024,1024]{1,0:T(8,128)(2,1)} %get-tuple-element.74.refs_1_, bf16[1024,768]{1,0:T(8,128)(2,1)} %get-tuple-element.107.refs_2_, bf16[1024,3072]{1,0:T(8,128)(2,1)} %get-tuple-element.108.refs_3_, ...), custom_call_target="tpu_custom_call" | custom-call | flops 9945533440 | bytes 20000000 | tf_op jit(solution)/shard_map/pallas_call | solution.py:51
  489.8 14.7 %shard_map.280 = (bf16[1024,3072]{1,0:T(8,128)(2,1)}, bf16[384,3072]{1,0:T(8,128)(2,1)}, f32[1,3072]{1,0:T(1,128)}, f32[1,3072]{1,0:T(1,128)}) custom-call(s32[8]{0:T(128)} %refs_0_.11, bf16[1024,3072]{1,0:T(8,128)(2,1)} %fusion.refs_1_, bf16[384,3072]{1,0:T(8,128)(2,1)} %add_convert_fusion.1.refs_2_, bf16[1024,1024]{1,0:T(8,128)(2,1)} %get-tuple-element.105.refs_1_.refs_3_, ...), custom_call_target="tpu_custom_call" | custom-call | flops 16000000000 | bytes 20000000 | tf_op jit(solution)/shard_map/pallas_call | solution.py:51
  506.6 8.7 %shard_map.282 = (bf16[16,32,3072]{2,1,0:T(8,128)(2,1)}, bf16[16,32,3072]{2,1,0:T(8,128)(2,1)}) custom-call(s32[1]{0:T(128)} %bitcast.2.refs_0_, bf16[384,1024]{1,0:T(8,128)(2,1)} %bitcast.242, bf16[384,3072]{1,0:T(8,128)(2,1)} %get-tuple-element.128.refs_2_, bf16[2,4,24,5376]{3,2,1,0:T(8,128)(2,1)} %get-tuple-element.137.refs_6_.refs_1_.refs_3_, ...), custom_call_target="tpu_custom_call" | custom-call | flops 3140694784 | bytes 20000000 | tf_op jit(solution)/shard_map/pallas_call | solution.py:51
  516.5 10.8 %shard_map.283 = (bf16[16,24,3200]{2,1,0:T(8,128)(2,1)}, bf16[16,24,3200]{2,1,0:T(8,128)(2,1)}) custom-call(s32[1]{0:T(128)} %bitcast.2.refs_0_, bf16[1024,768]{1,0:T(8,128)(2,1)} %refs_1_.1, bf16[1024,3072]{1,0:T(8,128)(2,1)} %get-tuple-element.119.refs_2_, f32[768,128]{1,0:T(8,128)} %reshape.414.refs_3_, bf16[2,2,4,32,3072]{4,3,2,1,0:T(8,128)(2,1)} %bitcast.234), custom_call_target="tpu_custom_call" | custom-call | flops 6543114240 | bytes 20000000 | tf_op jit(solution)/shard_map/pallas_call | solution.py:51
  527.8 19.6 %collective-permute-done.51 = bf16[2,4,152,768]{3,2,1,0:T(8,128)(2,1)} collective-permute-done((bf16[2,4,152,768]{3,2,1,0:T(8,128)(2,1)}, bf16[2,4,152,768]{3,2,1,0:T(8,128)(2,1)}, u32[]{:S(2)}, u32[]{:S(2)}) %collective-permute-start.51) | collective-permute-done | bytes 1867808 | tf_op jit(solution)/shard_map/ppermute | solution.py:78
  595.1 15.8 %collective-permute-done.44 = bf16[2,4,24,3200]{3,2,1,0:T(8,128)(2,1)} collective-permute-done((bf16[2,4,24,3200]{3,2,1,0:T(8,128)(2,1)S(1)}, bf16[2,4,24,3200]{3,2,1,0:T(8,128)(2,1)}, u32[]{:S(2)}, u32[]{:S(2)}) %collective-permute-start.44) | collective-permute-done | bytes 1228832 | tf_op jit(solution)/shard_map/ppermute | solution.py:83
  613.8 10.2 %fusion.59 = f32[1024,768]{1,0:T(8,128)} fusion(f32[1024,768]{1,0:T(8,128)} %shard_map.285, bf16[1024,3072]{1,0:T(8,128)(2,1)} %get-tuple-element.119.refs_2_, bf16[768,3200]{1,0:T(8,128)(2,1)} %bitcast.219), kind=kOutput, calls=%fused_computation.127 | convolution fusion | flops 4832624640 | bytes 17301504 | tf_op jit(solution)/shard_map/dot_general | solution.py:34
  625.2 7.8 %collective-permute-done.45 = bf16[4,24,3200]{2,1,0:T(8,128)(2,1)S(1)} collective-permute-done((bf16[4,24,3200]{2,1,0:T(8,128)(2,1)S(1)}, bf16[4,24,3200]{2,1,0:T(8,128)(2,1)S(1)}, u32[]{:S(2)}, u32[]{:S(2)}) %collective-permute-start.45) | collective-permute-done | bytes 614432 | tf_op jit(solution)/shard_map/ppermute | solution.py:78
  635.2 10.0 %collective-permute-start.46 = (bf16[24,3200]{1,0:T(8,128)(2,1)}, bf16[24,3200]{1,0:T(8,128)(2,1)}, u32[]{:S(2)}, u32[]{:S(2)}) collective-permute-start(bf16[24,3200]{1,0:T(8,128)(2,1)} %get-tuple-element.149), channel_id=1, source_target_pairs={{0,4},{1,5},{2,6},{3,7},{4,8},{5,9},{6,10},{7,11},{8,12},{9,13},{1... | collective-permute-start | bytes 460808 | tf_op jit(solution)/shard_map/ppermute | solution.py:88
  (387 shorter events, 316.9 us)
Async XLA Ops:
  7.2 99.8 %all-gather.13.cloned.1.call-start = ((), (), s32[]{:S(2)}) async-start(), calls=%async_computation.10 | async-start | bytes 1310720 | tf_op jit(solution)/shard_map/all_gather | solution.py:169
  9.0 110.0 %all-gather.11.cloned.1.call-start = ((), (), s32[]{:S(2)}) async-start(), calls=%async_computation.9 | async-start | bytes 1310720 | tf_op jit(solution)/shard_map/all_gather | solution.py:169
  26.4 96.7 %all-gather.15.cloned.1.call-start = ((), (), s32[]{:S(2)}) async-start(), calls=%async_computation.11 | async-start | bytes 1351680 | tf_op jit(solution)/shard_map/all_gather | solution.py:169
  68.4 38.6 %collective-permute-start.4 = (bf16[2,4,24,3200]{3,2,1,0:T(8,128)(2,1)S(1)}, bf16[2,4,24,3200]{3,2,1,0:T(8,128)(2,1)S(1)}, u32[]{:S(2)}, u32[]{:S(2)}) collective-permute-start(bf16[2,4,24,3200]{3,2,1,0:T(8,128)(2,1)S(1)} %pad_maximum_fusion.5.refs_1_), channel_id=1, source_target_pairs={{0,16},{16,0},{1,17},{17,1},{2,18},{18,2},{3,19},{19,3},{4,20},{20... | collective-permute-start | bytes 3686408 | tf_op jit(solution)/shard_map/ppermute | solution.py:83
  89.7 112.2 %all-gather.9.cloned.1.call-start = ((), (), s32[]{:S(2)}) async-start(), calls=%async_computation.8 | async-start | bytes 1320960 | tf_op jit(solution)/shard_map/all_gather | solution.py:169
  115.5 461.9 %reduce-scatter.11.cloned.1.call-start = ((), (), s32[]{:S(2)}) async-start(), calls=%async_computation.7 | async-start | bytes 983040 | tf_op jit(solution)/shard_map/reduce_scatter | solution.py:227
  136.6 52.9 %collective-permute-start.19 = (bf16[2,4,32,4096]{3,2,1,0:T(8,128)(2,1)}, bf16[2,4,32,4096]{3,2,1,0:T(8,128)(2,1)S(1)}, u32[]{:S(2)}, u32[]{:S(2)}) collective-permute-start(bf16[2,4,32,4096]{3,2,1,0:T(8,128)(2,1)} %pad_maximum_fusion.refs_1_), channel_id=1, source_target_pairs={{0,2},{1,3},{2,0},{3,1},{4,6},{5,7},{6,4},{7,5},{8,10},{9,11},{10,... | collective-permute-start | bytes 6291464 | tf_op jit(solution)/shard_map/ppermute | solution.py:78
  156.9 47.2 %collective-permute-start.26 = (bf16[2,4,96,1024]{3,2,1,0:T(8,128)(2,1)}, bf16[2,4,96,1024]{3,2,1,0:T(8,128)(2,1)}, u32[]{:S(2)}, u32[]{:S(2)}) collective-permute-start(bf16[2,4,96,1024]{3,2,1,0:T(8,128)(2,1)} %pad_maximum_fusion.4.refs_1_), channel_id=1, source_target_pairs={{0,1},{1,0},{2,3},{3,2},{4,5},{5,4},{6,7},{7,6},{8,9},{9,8},{10,11... | collective-permute-start | bytes 4718600 | tf_op jit(solution)/shard_map/ppermute | solution.py:73
  156.9 75.7 %collective-permute-start.24 = (bf16[2,4,32,4096]{3,2,1,0:T(8,128)(2,1)}, bf16[2,4,32,4096]{3,2,1,0:T(8,128)(2,1)}, u32[]{:S(2)}, u32[]{:S(2)}) collective-permute-start(bf16[2,4,32,4096]{3,2,1,0:T(8,128)(2,1)} %pad_maximum_fusion.refs_1_), channel_id=1, source_target_pairs={{0,1},{1,0},{2,3},{3,2},{4,5},{5,4},{6,7},{7,6},{8,9},{9,8},{10,11... | collective-permute-start | bytes 6291464 | tf_op jit(solution)/shard_map/ppermute | solution.py:73
  189.5 43.1 %collective-permute-start.25 = (bf16[2,4,32,4096]{3,2,1,0:T(8,128)(2,1)S(1)}, bf16[2,4,32,4096]{3,2,1,0:T(8,128)(2,1)}, u32[]{:S(2)}, u32[]{:S(2)}) collective-permute-start(bf16[2,4,32,4096]{3,2,1,0:T(8,128)(2,1)S(1)} %collective-permute-done.19.refs_2_), channel_id=1, source_target_pairs={{0,1},{1,0},{2,3},{3,2},{4,5},{5,4},{6,7},{7,6},{8,9},{9,8},{10,11... | collective-permute-start | bytes 6291464 | tf_op jit(solution)/shard_map/ppermute | solution.py:73
  225.7 53.0 %collective-permute-start.29 = (bf16[2,4,152,768]{3,2,1,0:T(8,128)(2,1)}, bf16[2,4,152,768]{3,2,1,0:T(8,128)(2,1)}, u32[]{:S(2)}, u32[]{:S(2)}) collective-permute-start(bf16[2,4,152,768]{3,2,1,0:T(8,128)(2,1)} %pad_maximum_fusion.2.refs_1_), channel_id=1, source_target_pairs={{0,16},{16,0},{1,17},{17,1},{2,18},{18,2},{3,19},{19,3},{4,20},{20... | collective-permute-start | bytes 5603336 | tf_op jit(solution)/shard_map/ppermute | solution.py:83
  227.1 72.8 %collective-permute-start.30 = (bf16[2,4,152,768]{3,2,1,0:T(8,128)(2,1)}, bf16[2,4,152,768]{3,2,1,0:T(8,128)(2,1)}, u32[]{:S(2)}, u32[]{:S(2)}) collective-permute-start(bf16[2,4,152,768]{3,2,1,0:T(8,128)(2,1)} %pad_maximum_fusion.2.refs_1_), channel_id=1, source_target_pairs={{0,1},{1,0},{2,3},{3,2},{4,5},{5,4},{6,7},{7,6},{8,9},{9,8},{10,11... | collective-permute-start | bytes 5603336 | tf_op jit(solution)/shard_map/ppermute | solution.py:73
  232.6 58.1 %collective-permute-start.21 = (bf16[2,4,24,5376]{3,2,1,0:T(8,128)(2,1)}, bf16[2,4,24,5376]{3,2,1,0:T(8,128)(2,1)}, u32[]{:S(2)}, u32[]{:S(2)}) collective-permute-start(bf16[2,4,24,5376]{3,2,1,0:T(8,128)(2,1)} %pad_maximum_fusion.1.refs_1_), channel_id=1, source_target_pairs={{0,2},{1,3},{2,0},{3,1},{4,6},{5,7},{6,4},{7,5},{8,10},{9,11},{10,... | collective-permute-start | bytes 6193160 | tf_op jit(solution)/shard_map/ppermute | solution.py:78
  290.1 58.4 %collective-permute-start.33 = (bf16[2,2,4,32,4096]{4,3,2,1,0:T(8,128)(2,1)}, bf16[2,2,4,32,4096]{4,3,2,1,0:T(8,128)(2,1)}, u32[]{:S(2)}, u32[]{:S(2)}) collective-permute-start(bf16[2,2,4,32,4096]{4,3,2,1,0:T(8,128)(2,1)} %bitcast.269), channel_id=1, source_target_pairs={{0,1},{1,0},{2,3},{3,2},{4,5},{5,4},{6,7},{7,6},{8,9},{9,8},{10,11... | collective-permute-start | bytes 12582920 | tf_op jit(solution)/shard_map/ppermute | solution.py:73
  299.9 42.2 %collective-permute-start.34 = (bf16[2,2,4,96,1024]{4,3,2,1,0:T(8,128)(2,1)}, bf16[2,2,4,96,1024]{4,3,2,1,0:T(8,128)(2,1)}, u32[]{:S(2)}, u32[]{:S(2)}) collective-permute-start(bf16[2,2,4,96,1024]{4,3,2,1,0:T(8,128)(2,1)} %bitcast.272), channel_id=1, source_target_pairs={{0,1},{1,0},{2,3},{3,2},{4,5},{5,4},{6,7},{7,6},{8,9},{9,8},{10,11... | collective-permute-start | bytes 9437192 | tf_op jit(solution)/shard_map/ppermute | solution.py:73
  347.9 45.8 %collective-permute-start.36 = (bf16[2,4,96,1024]{3,2,1,0:T(8,128)(2,1)}, bf16[2,4,96,1024]{3,2,1,0:T(8,128)(2,1)}, u32[]{:S(2)}, u32[]{:S(2)}) collective-permute-start(bf16[2,4,96,1024]{3,2,1,0:T(8,128)(2,1)} %get-tuple-element.143.refs_9_), channel_id=1, source_target_pairs={{0,16},{16,0},{1,17},{17,1},{2,18},{18,2},{3,19},{19,3},{4,20},{20... | collective-permute-start | bytes 4718600 | tf_op jit(solution)/shard_map/ppermute | solution.py:83
  353.9 48.9 %collective-permute-start.35 = (bf16[2,4,32,4096]{3,2,1,0:T(8,128)(2,1)}, bf16[2,4,32,4096]{3,2,1,0:T(8,128)(2,1)}, u32[]{:S(2)}, u32[]{:S(2)}) collective-permute-start(bf16[2,4,32,4096]{3,2,1,0:T(8,128)(2,1)} %get-tuple-element.135.refs_8_), channel_id=1, source_target_pairs={{0,2},{1,3},{2,0},{3,1},{4,6},{5,7},{6,4},{7,5},{8,10},{9,11},{10,... | collective-permute-start | bytes 6291464 | tf_op jit(solution)/shard_map/ppermute | solution.py:78
  475.6 103.4 %reduce-scatter.9.cloned.1.call-start = ((), (), s32[]{:S(2)}) async-start(), calls=%async_computation.6 | async-start | bytes 1310720 | tf_op jit(solution)/shard_map/reduce_scatter | solution.py:227
  482.2 69.4 %collective-permute-start.49 = (bf16[2,4,24,5376]{3,2,1,0:T(8,128)(2,1)}, bf16[2,4,24,5376]{3,2,1,0:T(8,128)(2,1)}, u32[]{:S(2)}, u32[]{:S(2)}) collective-permute-start(bf16[2,4,24,5376]{3,2,1,0:T(8,128)(2,1)} %get-tuple-element.137.refs_6_.refs_1_.refs_3_), channel_id=1, source_target_pairs={{0,16},{16,0},{1,17},{17,1},{2,18},{18,2},{3,19},{19,3},{4,20},{20... | collective-permute-start | bytes 6193160 | tf_op jit(solution)/shard_map/ppermute | solution.py:83
  504.5 42.9 %collective-permute-start.51 = (bf16[2,4,152,768]{3,2,1,0:T(8,128)(2,1)}, bf16[2,4,152,768]{3,2,1,0:T(8,128)(2,1)}, u32[]{:S(2)}, u32[]{:S(2)}) collective-permute-start(bf16[2,4,152,768]{3,2,1,0:T(8,128)(2,1)} %get-tuple-element.139.refs_4_), channel_id=1, source_target_pairs={{0,2},{1,3},{2,0},{3,1},{4,6},{5,7},{6,4},{7,5},{8,10},{9,11},{10,... | collective-permute-start | bytes 5603336 | tf_op jit(solution)/shard_map/ppermute | solution.py:78
  515.3 40.6 %collective-permute-start.42 = (bf16[2,2,4,32,3072]{4,3,2,1,0:T(8,128)(2,1)}, bf16[2,2,4,32,3072]{4,3,2,1,0:T(8,128)(2,1)}, u32[]{:S(2)}, u32[]{:S(2)}) collective-permute-start(bf16[2,2,4,32,3072]{4,3,2,1,0:T(8,128)(2,1)} %bitcast.273), channel_id=1, source_target_pairs={{0,1},{1,0},{2,3},{3,2},{4,5},{5,4},{6,7},{7,6},{8,9},{9,8},{10,11... | collective-permute-start | bytes 9437192 | tf_op jit(solution)/shard_map/ppermute | solution.py:73
  527.7 123.3 %reduce-scatter.7.cloned.1.call-start = ((), (), s32[]{:S(2)}) async-start(), calls=%async_computation.5 | async-start | bytes 1167360 | tf_op jit(solution)/shard_map/reduce_scatter | solution.py:227
  575.9 85.3 %reduce-scatter.5.cloned.1.call-start = ((), (), s32[]{:S(2)}) async-start(), calls=%async_computation.4 | async-start | bytes 1290240 | tf_op jit(solution)/shard_map/reduce_scatter | solution.py:227
  585.5 62.1 %collective-permute-start.53 = (bf16[2,4,32,3072]{3,2,1,0:T(8,128)(2,1)S(1)}, bf16[2,4,32,3072]{3,2,1,0:T(8,128)(2,1)}, u32[]{:S(2)}, u32[]{:S(2)}) collective-permute-start(bf16[2,4,32,3072]{3,2,1,0:T(8,128)(2,1)S(1)} %copy-done.1), channel_id=1, source_target_pairs={{0,2},{1,3},{2,0},{3,1},{4,6},{5,7},{6,4},{7,5},{8,10},{9,11},{10,... | collective-permute-start | bytes 4718600 | tf_op jit(solution)/shard_map/ppermute | solution.py:78
  (88 other events, 1454.2 us)
Sparse Core Ops, SparseCore 0:
  10.2 54.3 all-gather.12
  66.7 26.1 all-gather.10
  95.0 27.9 all-gather.14
  125.0 28.5 all-gather.8
  475.8 32.4 reduce-scatter.10
  527.9 34.9 reduce-scatter.8
  576.0 34.4 reduce-scatter.6
  612.7 25.8 reduce-scatter.4

commit v4 on v3

--- a/solution.py
+++ b/solution.py
@@ -1078,7 +1078,7 @@
     )
     i_final, low2, active, third_low, hidden_low, second_grad, i_sums2, i_upsum = ffn(
         image_block,
-        512,
+        1024,
         image_hidden,
         zhat2,
         inv2,
@@ -1114,7 +1114,7 @@
     text_hidden = t_wide.shape[1] - 2 * CO_W
     zhat1, inv1, low1, triple, attended, zhat2, inv2 = attn_forward(
         True,
-        text_block,
+        2 * text_block,
         lengths,
         text_context,
         text_in,
@@ -1128,7 +1128,7 @@
     i_out_sum.link()
     t_final, low2, active, third_low, hidden_low, second_grad, t_sums2, t_upsum = ffn(
         text_block,
-        512,
+        768,
         text_hidden,
         zhat2,
         inv2,
@@ -1140,9 +1140,7 @@
         t_gains,
         [i_rest_sum.send, i_out_sum.send],
     )
-    i_rest_sum.came = after(i_rest_sum.came, second_grad)
     i_out_sum.came = after(i_out_sum.came, second_grad)
-    i_rest_sum.link()
     i_out_sum.link()
     second_low, triple_low, t_first, first_low, t_ctx, t_sums1 = attn_backward(
         True,
@@ -1155,11 +1153,11 @@
         t_rest,
         t_outw,
         t_gains,
-        [i_rest_sum.send, i_out_sum.send],
+        [i_out_sum.send],
     )
     i_rest_sum.came = after(i_rest_sum.came, t_ctx)
     i_out_sum.came = after(i_out_sum.came, t_ctx)
-    i_rest_sum.column()
+    i_rest_sum.link()
     i_out_sum.column()
     t_rest_sum = Scatter(
         cols_grad(shard_count, False, [(low1, triple_low), (low2, hidden_low)], 768, None, [i_rest_sum.send, i_out_sum.send]), False
@@ -1175,6 +1173,9 @@
     )
 
     t_rest_sum.link()
+    i_rest_sum.came = after(i_rest_sum.came, t_out_sum.keep)
+    i_rest_sum.column()
+
     t_co_grad, i_co_grad, t_co_sum, i_co_sum = co_backward(
         lengths, text_co, image_co, t_ctx, i_ctx, [t_out_sum.keep, t_rest_sum.send]
     )

time: 700 us -> 682 us (0.974)
  waiting for transfers between devices: 177 us -> 165 us
    ppermute x12, waiting for transfers between devices: 63.4 us -> 52.4 us  [over_y(): return lax.ppermute(block, 'dp', [(d, d ^ 2) for d in range(total)])]
  transfers between devices with their start and end apart: 66 -> 66, of which waited for: 22 -> 21; matrix products, arithmetic and copies ran while one was open for 22% -> 23% of each run, Pallas kernels for 35% -> 36%
where the time goes in v4:
time: 682 us; the launch traced here: 673 us
  Pallas kernels  256 us (38%)
  waiting for transfers between devices  165 us (24%)
  other arithmetic  90.3 us (13%)
  starting transfers between devices  69 us (10%)
  local copies, waits for them, and re-layouts  46.4 us (7%)
  matrix products  30.6 us (4%)
  between operations  15.7 us (2%)
    pallas_call x20, Pallas kernels, call(): pl.pallas_call(body, in_specs=in_specs + [ANY] * len(deps), compiler_para...  256 us
    ppermute x16, waiting for transfers between devices, over_x(): return lax.ppermute(block, 'stream', [(d, d ^ 1) for d in range(total)])  73.4 us
    convert_element_type x18, other arithmetic, add_low(): return (kept.astype(F32) + came.astype(F32)).astype(BF)  60.2 us
    ppermute x12, waiting for transfers between devices, over_y(): return lax.ppermute(block, 'dp', [(d, d ^ 2) for d in range(total)])  52.4 us
    ppermute x12, waiting for transfers between devices, over_z(): lax.ppermute(block, 'dp', [(d, (d + 4 * shift) % total) for d in range(to...  37.3 us
    ppermute x12, starting transfers between devices, over_z(): lax.ppermute(block, 'dp', [(d, (d + 4 * shift) % total) for d in range(to...  29.9 us
    ppermute x16, starting transfers between devices, over_x(): return lax.ppermute(block, 'stream', [(d, d ^ 1) for d in range(total)])  19.8 us
    dot_general x2, matrix products, dot_nt(): lax.dot_general(a, b, (((1,), (1,)), ((), ())), preferred_element_type=F32)  17 us
  transfers between devices with their start and end apart: 66, of which 21 were waited for; matrix products, arithmetic and copies ran while one was open for 23% of the time, Pallas kernels for 36%

profile of v4, /device:TPU:0, one launch (start us, length us, event | category | flops | bytes accessed | tf_op | source)
XLA Modules:
  0.0 673.2 jit_solution(10383737469788347272)
XLA Ops:
  34.8 16.8 %collective-permute-done.1 = bf16[24,3200]{1,0:T(8,128)(2,1)S(1)} collective-permute-done((bf16[24,3200]{1,0:T(8,128)(2,1)S(1)}, bf16[24,3200]{1,0:T(8,128)(2,1)S(1)}, u32[]{:S(2)}, u32[]{:S(2)}) %collective-permute-start.1) | collective-permute-done | bytes 153632 | tf_op jit(solution)/shard_map/ppermute | solution.py:88
  69.0 17.1 %collective-permute-done.12 = bf16[4,32,3072]{2,1,0:T(8,128)(2,1)S(1)} collective-permute-done((bf16[4,32,3072]{2,1,0:T(8,128)(2,1)}, bf16[4,32,3072]{2,1,0:T(8,128)(2,1)S(1)}, u32[]{:S(2)}, u32[]{:S(2)}) %collective-permute-start.12) | collective-permute-done | bytes 786464 | tf_op jit(solution)/shard_map/ppermute | solution.py:83
  89.8 17.2 %collective-permute-done.4.refs_2_.refs_1_ = bf16[2,4,24,3200]{3,2,1,0:T(8,128)(2,1)S(1)} collective-permute-done((bf16[2,4,24,3200]{3,2,1,0:T(8,128)(2,1)S(1)}, bf16[2,4,24,3200]{3,2,1,0:T(8,128)(2,1)S(1)}, u32[]{:S(2)}, u32[]{:S(2)}) %collective-permute-start.4) | collective-permute-done | bytes 1228832 | tf_op jit(solution)/shard_map/ppermute | solution.py:83
  137.4 8.6 %collective-permute-done.16 = bf16[4,96,1024]{2,1,0:T(8,128)(2,1)} collective-permute-done((bf16[4,96,1024]{2,1,0:T(8,128)(2,1)}, bf16[4,96,1024]{2,1,0:T(8,128)(2,1)}, u32[]{:S(2)}, u32[]{:S(2)}) %collective-permute-start.16) | collective-permute-done | bytes 786464 | tf_op jit(solution)/shard_map/ppermute | solution.py:78
  170.3 12.2 %collective-permute-done.17.refs_1_.refs_2_ = bf16[2,4,96,1024]{3,2,1,0:T(8,128)(2,1)} collective-permute-done((bf16[2,4,96,1024]{3,2,1,0:T(8,128)(2,1)}, bf16[2,4,96,1024]{3,2,1,0:T(8,128)(2,1)}, u32[]{:S(2)}, u32[]{:S(2)}) %collective-permute-start.17) | collective-permute-done | bytes 1572896 | tf_op jit(solution)/shard_map/ppermute | solution.py:83
  189.5 11.1 %shard_map.257 = (bf16[1024,1024]{1,0:T(8,128)(2,1)}, bf16[384,1024]{1,0:T(8,128)(2,1)}) custom-call(s32[8]{0:T(128)} %refs_0_.11, bf16[1024,3072]{1,0:T(8,128)(2,1)} %fusion.refs_1_, bf16[384,3072]{1,0:T(8,128)(2,1)} %add_convert_fusion.1.refs_2_), custom_call_target="tpu_custom_call" | custom-call | flops 12800000000 | bytes 8000000 | tf_op jit(solution)/shard_map/pallas_call | solution.py:51
  215.8 7.6 %collective-permute-done.28 = bf16[4,152,768]{2,1,0:T(8,128)(2,1)} collective-permute-done((bf16[4,152,768]{2,1,0:T(8,128)(2,1)}, bf16[4,152,768]{2,1,0:T(8,128)(2,1)}, u32[]{:S(2)}, u32[]{:S(2)}) %collective-permute-start.28) | collective-permute-done | bytes 933920 | tf_op jit(solution)/shard_map/ppermute | solution.py:78
  240.0 11.6 %shard_map.263 = (f32[384,1024]{1,0:T(8,128)}, f32[384,1]{1,0:T(8,128)}, bf16[384,1024]{1,0:T(8,128)(2,1)}, bf16[384,3072]{1,0:T(8,128)(2,1)}, bf16[384,1024]{1,...) custom-call(s32[8]{0:T(128)} %refs_0_.11, bf16[384,1024]{1,0:T(8,128)(2,1)} %get-tuple-element.75.refs_3_.refs_1_, ...), custom_call_target="tpu_custom_call" | custom-call | flops 12884901888 | bytes 40000000 | tf_op jit(solution)/shard_map/pallas_call | solution.py:51
  251.7 10.8 %shard_map.264 = (f32[384,1024]{1,0:T(8,128)}, bf16[384,1024]{1,0:T(8,128)(2,1)}, bf16[384,1024]{1,0:T(8,128)(2,1)}, bf16[384,1024]{1,0:T(8,128)(2,1)}, bf16[384...) custom-call(f32[384,1024]{1,0:T(8,128)} %get-tuple-element.76.refs_0_, ...), custom_call_target="tpu_custom_call" | custom-call | flops 5234491392 | bytes 40000000 | tf_op jit(solution)/shard_map/pallas_call | solution.py:51
  262.4 16.4 %shard_map.265 = (bf16[384,1024]{1,0:T(8,128)(2,1)}, bf16[384,3072]{1,0:T(8,128)(2,1)}, f32[384,1024]{1,0:T(8,128)}, bf16[384,1024]{1,0:T(8,128)(2,1)}, bf16[384,1024]{1,0:T(8,128)(2,1)}, /*index=5*/f32[8,1024]{1,0:T(8,128)}) custom-call(s32[8]{0:T(128)} %refs_0_.11, f32[384,1024]{1,0:T(8,128)} %get-tuple-element.78.refs_1_, ...), custom_call_target="tpu_custom_call" | custom-call | flops 12884901888 | bytes 40000000 | tf_op jit(solution)/shard_map/pallas_call | solution.py:51
  278.9 11.4 %shard_map.269 = (bf16[16,32,4096]{2,1,0:T(8,128)(2,1)}, bf16[16,32,4096]{2,1,0:T(8,128)(2,1)}) custom-call(s32[1]{0:T(128)} %bitcast.2.refs_0_, bf16[384,1024]{1,0:T(8,128)(2,1)} %get-tuple-element.83.refs_1_, bf16[384,1024]{1,0:T(8,128)(2,1)} %get-tuple-element.84.refs_2_, bf16[384,3072]{1,0:T(8,128)(2,1)} %get-tuple-element.85.refs_3_, ...), custom_call_target="tpu_custom_call" | custom-call | flops 4187593216 | bytes 20000000 | tf_op jit(solution)/shard_map/pallas_call | solution.py:51
  291.3 8.9 %shard_map.270 = (bf16[16,96,1024]{2,1,0:T(8,128)(2,1)}, bf16[16,96,1024]{2,1,0:T(8,128)(2,1)}) custom-call(s32[1]{0:T(128)} %bitcast.2.refs_0_, bf16[384,1024]{1,0:T(8,128)(2,1)} %get-tuple-element.75.refs_3_.refs_1_, bf16[384,1024]{1,0:T(8,128)(2,1)} %get-tuple-element.88.refs_2_, bf16[384,1024]{1,0:T(8,128)(2,1)} %get-tuple-element.89.refs_3_, ...), custom_call_target="tpu_custom_call" | custom-call | flops 3140694784 | bytes 20000000 | tf_op jit(solution)/shard_map/pallas_call | solution.py:51
  323.0 18.2 %shard_map.271 = (f32[1024,768]{1,0:T(8,128)}, f32[1024,1]{1,0:T(8,128)}, bf16[1024,768]{1,0:T(8,128)(2,1)}, bf16[1024,2304]{1,0:T(8,128)(2,1)}, bf16[1024,768]{...) custom-call(s32[8]{0:T(128)} %refs_0_.11, bf16[1024,1024]{1,0:T(8,128)(2,1)} %get-tuple-element.74.refs_1_, ...), custom_call_target="tpu_custom_call" | custom-call | flops 19327352832 | bytes 40000000 | tf_op jit(solution)/shard_map/pallas_call | solution.py:51
  355.0 33.6 %shard_map.272 = (f32[1024,768]{1,0:T(8,128)}, bf16[1024,768]{1,0:T(8,128)(2,1)}, bf16[1024,3072]{1,0:T(8,128)(2,1)}, bf16[1024,768]{1,0:T(8,128)(2,1)}, bf16[10...) custom-call(f32[1024,768]{1,0:T(8,128)} %get-tuple-element.95.refs_0_, ...), custom_call_target="tpu_custom_call" | custom-call | flops 31406948352 | bytes 40000000 | tf_op jit(solution)/shard_map/pallas_call | solution.py:51
  391.3 26.4 %shard_map.274 = (bf16[1024,768]{1,0:T(8,128)(2,1)}, bf16[1024,2304]{1,0:T(8,128)(2,1)}, f32[1024,768]{1,0:T(8,128)}, bf16[1024,768]{1,0:T(8,128)(2,1)}, bf16[1024,1024]{1,0:T(8,128)(2,1)}, /*index=5*/f32[8,768]{1,0:T(8,128)}) custom-call(s32[8]{0:T(128)} %refs_0_.11, f32[1024,768]{1,0:T(8,128)} %get-tuple-element.100.refs_1_, ...), custom_call_target="tpu_custom_call" | custom-call | flops 19327352832 | bytes 40000000 | tf_op jit(solution)/shard_map/pallas_call | solution.py:51
  422.9 16.6 %shard_map.277 = (bf16[16,24,5376]{2,1,0:T(8,128)(2,1)}, bf16[16,24,5376]{2,1,0:T(8,128)(2,1)}) custom-call(s32[1]{0:T(128)} %bitcast.2.refs_0_, bf16[1024,768]{1,0:T(8,128)(2,1)} %get-tuple-element.112.refs_1_, bf16[1024,768]{1,0:T(8,128)(2,1)} %get-tuple-element.113.refs_2_, bf16[1024,2304]{1,0:T(8,128)(2,1)} %get-tuple-element.114.refs_3_, ...), custom_call_target="tpu_custom_call" | custom-call | flops 10992432128 | bytes 20000000 | tf_op jit(solution)/shard_map/pallas_call | solution.py:51
  439.6 18.1 %shard_map.278 = (bf16[16,152,768]{2,1,0:T(8,128)(2,1)}, bf16[16,152,768]{2,1,0:T(8,128)(2,1)}) custom-call(s32[1]{0:T(128)} %bitcast.2.refs_0_, bf16[1024,1024]{1,0:T(8,128)(2,1)} %get-tuple-element.74.refs_1_, bf16[1024,768]{1,0:T(8,128)(2,1)} %get-tuple-element.107.refs_2_, bf16[1024,3072]{1,0:T(8,128)(2,1)} %get-tuple-element.108.refs_3_, ...), custom_call_target="tpu_custom_call" | custom-call | flops 9945533440 | bytes 20000000 | tf_op jit(solution)/shard_map/pallas_call | solution.py:51
  475.0 14.8 %shard_map.279 = (bf16[1024,3072]{1,0:T(8,128)(2,1)}, bf16[384,3072]{1,0:T(8,128)(2,1)}, f32[1,3072]{1,0:T(1,128)}, f32[1,3072]{1,0:T(1,128)}) custom-call(s32[8]{0:T(128)} %refs_0_.11, bf16[1024,3072]{1,0:T(8,128)(2,1)} %fusion.refs_1_, bf16[384,3072]{1,0:T(8,128)(2,1)} %add_convert_fusion.1.refs_2_, bf16[1024,1024]{1,0:T(8,128)(2,1)} %get-tuple-element.105.refs_1_.refs_3_, ...), custom_call_target="tpu_custom_call" | custom-call | flops 16000000000 | bytes 20000000 | tf_op jit(solution)/shard_map/pallas_call | solution.py:51
  491.6 8.6 %shard_map.281 = (bf16[16,32,3072]{2,1,0:T(8,128)(2,1)}, bf16[16,32,3072]{2,1,0:T(8,128)(2,1)}) custom-call(s32[1]{0:T(128)} %bitcast.2.refs_0_, bf16[384,1024]{1,0:T(8,128)(2,1)} %bitcast.243, bf16[384,3072]{1,0:T(8,128)(2,1)} %get-tuple-element.128.refs_2_, bf16[2,4,24,5376]{3,2,1,0:T(8,128)(2,1)} %get-tuple-element.137.refs_6_.refs_1_.refs_3_, ...), custom_call_target="tpu_custom_call" | custom-call | flops 3140694784 | bytes 20000000 | tf_op jit(solution)/shard_map/pallas_call | solution.py:51
  501.4 10.8 %shard_map.282 = (bf16[16,24,3200]{2,1,0:T(8,128)(2,1)}, bf16[16,24,3200]{2,1,0:T(8,128)(2,1)}) custom-call(s32[1]{0:T(128)} %bitcast.2.refs_0_, bf16[1024,768]{1,0:T(8,128)(2,1)} %refs_1_.1, bf16[1024,3072]{1,0:T(8,128)(2,1)} %get-tuple-element.119.refs_2_, f32[768,128]{1,0:T(8,128)} %reshape.414.refs_3_, bf16[2,2,4,32,3072]{4,3,2,1,0:T(8,128)(2,1)} %bitcast.235), custom_call_target="tpu_custom_call" | custom-call | flops 6543114240 | bytes 20000000 | tf_op jit(solution)/shard_map/pallas_call | solution.py:51
  516.1 16.2 %collective-permute-done.50 = bf16[2,4,152,768]{3,2,1,0:T(8,128)(2,1)} collective-permute-done((bf16[2,4,152,768]{3,2,1,0:T(8,128)(2,1)}, bf16[2,4,152,768]{3,2,1,0:T(8,128)(2,1)}, u32[]{:S(2)}, u32[]{:S(2)}) %collective-permute-start.50) | collective-permute-done | bytes 1867808 | tf_op jit(solution)/shard_map/ppermute | solution.py:78
  579.5 15.5 %collective-permute-done.43 = bf16[2,4,24,3200]{3,2,1,0:T(8,128)(2,1)} collective-permute-done((bf16[2,4,24,3200]{3,2,1,0:T(8,128)(2,1)S(1)}, bf16[2,4,24,3200]{3,2,1,0:T(8,128)(2,1)}, u32[]{:S(2)}, u32[]{:S(2)}) %collective-permute-start.43) | collective-permute-done | bytes 1228832 | tf_op jit(solution)/shard_map/ppermute | solution.py:83
  598.2 10.5 %fusion.59 = f32[1024,768]{1,0:T(8,128)} fusion(f32[1024,768]{1,0:T(8,128)} %shard_map.284, bf16[1024,3072]{1,0:T(8,128)(2,1)} %get-tuple-element.119.refs_2_, bf16[768,3200]{1,0:T(8,128)(2,1)} %bitcast.222), kind=kOutput, calls=%fused_computation.127 | convolution fusion | flops 4832624640 | bytes 17301504 | tf_op jit(solution)/shard_map/dot_general | solution.py:34
  618.9 9.7 %collective-permute-start.45 = (bf16[24,3200]{1,0:T(8,128)(2,1)}, bf16[24,3200]{1,0:T(8,128)(2,1)}, u32[]{:S(2)}, u32[]{:S(2)}) collective-permute-start(bf16[24,3200]{1,0:T(8,128)(2,1)} %get-tuple-element.149), channel_id=1, source_target_pairs={{0,4},{1,5},{2,6},{3,7},{4,8},{5,9},{6,10},{7,11},{8,12},{9,13},{1... | collective-permute-start | bytes 460808 | tf_op jit(solution)/shard_map/ppermute | solution.py:88
  (389 shorter events, 308.9 us)
Async XLA Ops:
  7.2 99.8 %all-gather.13.cloned.1.call-start = ((), (), s32[]{:S(2)}) async-start(), calls=%async_computation.10 | async-start | bytes 1310720 | tf_op jit(solution)/shard_map/all_gather | solution.py:169
  9.0 110.1 %all-gather.11.cloned.1.call-start = ((), (), s32[]{:S(2)}) async-start(), calls=%async_computation.9 | async-start | bytes 1310720 | tf_op jit(solution)/shard_map/all_gather | solution.py:169
  26.4 96.7 %all-gather.15.cloned.1.call-start = ((), (), s32[]{:S(2)}) async-start(), calls=%async_computation.11 | async-start | bytes 1351680 | tf_op jit(solution)/shard_map/all_gather | solution.py:169
  89.6 112.5 %all-gather.9.cloned.1.call-start = ((), (), s32[]{:S(2)}) async-start(), calls=%async_computation.8 | async-start | bytes 1320960 | tf_op jit(solution)/shard_map/all_gather | solution.py:169
  115.5 446.0 %reduce-scatter.11.cloned.1.call-start = ((), (), s32[]{:S(2)}) async-start(), calls=%async_computation.7 | async-start | bytes 983040 | tf_op jit(solution)/shard_map/reduce_scatter | solution.py:227
  136.6 52.9 %collective-permute-start.19 = (bf16[2,4,32,4096]{3,2,1,0:T(8,128)(2,1)}, bf16[2,4,32,4096]{3,2,1,0:T(8,128)(2,1)S(1)}, u32[]{:S(2)}, u32[]{:S(2)}) collective-permute-start(bf16[2,4,32,4096]{3,2,1,0:T(8,128)(2,1)} %pad_maximum_fusion.refs_1_), channel_id=1, source_target_pairs={{0,2},{1,3},{2,0},{3,1},{4,6},{5,7},{6,4},{7,5},{8,10},{9,11},{10,... | collective-permute-start | bytes 6291464 | tf_op jit(solution)/shard_map/ppermute | solution.py:78
  156.9 47.5 %collective-permute-start.26 = (bf16[2,4,96,1024]{3,2,1,0:T(8,128)(2,1)}, bf16[2,4,96,1024]{3,2,1,0:T(8,128)(2,1)}, u32[]{:S(2)}, u32[]{:S(2)}) collective-permute-start(bf16[2,4,96,1024]{3,2,1,0:T(8,128)(2,1)} %pad_maximum_fusion.4.refs_1_), channel_id=1, source_target_pairs={{0,1},{1,0},{2,3},{3,2},{4,5},{5,4},{6,7},{7,6},{8,9},{9,8},{10,11... | collective-permute-start | bytes 4718600 | tf_op jit(solution)/shard_map/ppermute | solution.py:73
  156.9 75.9 %collective-permute-start.24 = (bf16[2,4,32,4096]{3,2,1,0:T(8,128)(2,1)}, bf16[2,4,32,4096]{3,2,1,0:T(8,128)(2,1)}, u32[]{:S(2)}, u32[]{:S(2)}) collective-permute-start(bf16[2,4,32,4096]{3,2,1,0:T(8,128)(2,1)} %pad_maximum_fusion.refs_1_), channel_id=1, source_target_pairs={{0,1},{1,0},{2,3},{3,2},{4,5},{5,4},{6,7},{7,6},{8,9},{9,8},{10,11... | collective-permute-start | bytes 6291464 | tf_op jit(solution)/shard_map/ppermute | solution.py:73
  189.5 43.4 %collective-permute-start.25 = (bf16[2,4,32,4096]{3,2,1,0:T(8,128)(2,1)S(1)}, bf16[2,4,32,4096]{3,2,1,0:T(8,128)(2,1)}, u32[]{:S(2)}, u32[]{:S(2)}) collective-permute-start(bf16[2,4,32,4096]{3,2,1,0:T(8,128)(2,1)S(1)} %collective-permute-done.19.refs_2_), channel_id=1, source_target_pairs={{0,1},{1,0},{2,3},{3,2},{4,5},{5,4},{6,7},{7,6},{8,9},{9,8},{10,11... | collective-permute-start | bytes 6291464 | tf_op jit(solution)/shard_map/ppermute | solution.py:73
  225.9 52.9 %collective-permute-start.29 = (bf16[2,4,152,768]{3,2,1,0:T(8,128)(2,1)}, bf16[2,4,152,768]{3,2,1,0:T(8,128)(2,1)}, u32[]{:S(2)}, u32[]{:S(2)}) collective-permute-start(bf16[2,4,152,768]{3,2,1,0:T(8,128)(2,1)} %pad_maximum_fusion.2.refs_1_), channel_id=1, source_target_pairs={{0,16},{16,0},{1,17},{17,1},{2,18},{18,2},{3,19},{19,3},{4,20},{20... | collective-permute-start | bytes 5603336 | tf_op jit(solution)/shard_map/ppermute | solution.py:83
  227.4 72.7 %collective-permute-start.30 = (bf16[2,4,152,768]{3,2,1,0:T(8,128)(2,1)}, bf16[2,4,152,768]{3,2,1,0:T(8,128)(2,1)}, u32[]{:S(2)}, u32[]{:S(2)}) collective-permute-start(bf16[2,4,152,768]{3,2,1,0:T(8,128)(2,1)} %pad_maximum_fusion.2.refs_1_), channel_id=1, source_target_pairs={{0,1},{1,0},{2,3},{3,2},{4,5},{5,4},{6,7},{7,6},{8,9},{9,8},{10,11... | collective-permute-start | bytes 5603336 | tf_op jit(solution)/shard_map/ppermute | solution.py:73
  232.9 58.0 %collective-permute-start.21 = (bf16[2,4,24,5376]{3,2,1,0:T(8,128)(2,1)}, bf16[2,4,24,5376]{3,2,1,0:T(8,128)(2,1)}, u32[]{:S(2)}, u32[]{:S(2)}) collective-permute-start(bf16[2,4,24,5376]{3,2,1,0:T(8,128)(2,1)} %pad_maximum_fusion.1.refs_1_), channel_id=1, source_target_pairs={{0,2},{1,3},{2,0},{3,1},{4,6},{5,7},{6,4},{7,5},{8,10},{9,11},{10,... | collective-permute-start | bytes 6193160 | tf_op jit(solution)/shard_map/ppermute | solution.py:78
  290.3 57.3 %collective-permute-start.33 = (bf16[2,2,4,32,4096]{4,3,2,1,0:T(8,128)(2,1)}, bf16[2,2,4,32,4096]{4,3,2,1,0:T(8,128)(2,1)}, u32[]{:S(2)}, u32[]{:S(2)}) collective-permute-start(bf16[2,2,4,32,4096]{4,3,2,1,0:T(8,128)(2,1)} %bitcast.270), channel_id=1, source_target_pairs={{0,1},{1,0},{2,3},{3,2},{4,5},{5,4},{6,7},{7,6},{8,9},{9,8},{10,11... | collective-permute-start | bytes 12582920 | tf_op jit(solution)/shard_map/ppermute | solution.py:73
  300.2 41.1 %collective-permute-start.34 = (bf16[2,2,4,96,1024]{4,3,2,1,0:T(8,128)(2,1)}, bf16[2,2,4,96,1024]{4,3,2,1,0:T(8,128)(2,1)}, u32[]{:S(2)}, u32[]{:S(2)}) collective-permute-start(bf16[2,2,4,96,1024]{4,3,2,1,0:T(8,128)(2,1)} %bitcast.273), channel_id=1, source_target_pairs={{0,1},{1,0},{2,3},{3,2},{4,5},{5,4},{6,7},{7,6},{8,9},{9,8},{10,11... | collective-permute-start | bytes 9437192 | tf_op jit(solution)/shard_map/ppermute | solution.py:73
  347.0 41.6 %collective-permute-start.35 = (bf16[2,4,96,1024]{3,2,1,0:T(8,128)(2,1)}, bf16[2,4,96,1024]{3,2,1,0:T(8,128)(2,1)}, u32[]{:S(2)}, u32[]{:S(2)}) collective-permute-start(bf16[2,4,96,1024]{3,2,1,0:T(8,128)(2,1)} %get-tuple-element.143.refs_9_), channel_id=1, source_target_pairs={{0,16},{16,0},{1,17},{17,1},{2,18},{18,2},{3,19},{19,3},{4,20},{20... | collective-permute-start | bytes 4718600 | tf_op jit(solution)/shard_map/ppermute | solution.py:83
  353.0 67.5 %collective-permute-start.36 = (bf16[2,4,32,4096]{3,2,1,0:T(8,128)(2,1)}, bf16[2,4,32,4096]{3,2,1,0:T(8,128)(2,1)}, u32[]{:S(2)}, u32[]{:S(2)}) collective-permute-start(bf16[2,4,32,4096]{3,2,1,0:T(8,128)(2,1)} %get-tuple-element.135.refs_8_), channel_id=1, source_target_pairs={{0,2},{1,3},{2,0},{3,1},{4,6},{5,7},{6,4},{7,5},{8,10},{9,11},{10,... | collective-permute-start | bytes 6291464 | tf_op jit(solution)/shard_map/ppermute | solution.py:78
  459.6 103.6 %reduce-scatter.9.cloned.1.call-start = ((), (), s32[]{:S(2)}) async-start(), calls=%async_computation.6 | async-start | bytes 1310720 | tf_op jit(solution)/shard_map/reduce_scatter | solution.py:227
  459.6 53.1 %collective-permute-start.57 = (bf16[4,32,4096]{2,1,0:T(8,128)(2,1)}, bf16[4,32,4096]{2,1,0:T(8,128)(2,1)}, u32[]{:S(2)}, u32[]{:S(2)}) collective-permute-start(bf16[4,32,4096]{2,1,0:T(8,128)(2,1)} %fusion.28.refs_5_), channel_id=1, source_target_pairs={{0,16},{16,0},{1,17},{17,1},{2,18},{18,2},{3,19},{19,3},{4,20},{20... | collective-permute-start | bytes 3145736 | tf_op jit(solution)/shard_map/ppermute | solution.py:83
  467.5 69.1 %collective-permute-start.48 = (bf16[2,4,24,5376]{3,2,1,0:T(8,128)(2,1)}, bf16[2,4,24,5376]{3,2,1,0:T(8,128)(2,1)}, u32[]{:S(2)}, u32[]{:S(2)}) collective-permute-start(bf16[2,4,24,5376]{3,2,1,0:T(8,128)(2,1)} %get-tuple-element.137.refs_6_.refs_1_.refs_3_), channel_id=1, source_target_pairs={{0,16},{16,0},{1,17},{17,1},{2,18},{18,2},{3,19},{19,3},{4,20},{20... | collective-permute-start | bytes 6193160 | tf_op jit(solution)/shard_map/ppermute | solution.py:83
  489.8 42.4 %collective-permute-start.50 = (bf16[2,4,152,768]{3,2,1,0:T(8,128)(2,1)}, bf16[2,4,152,768]{3,2,1,0:T(8,128)(2,1)}, u32[]{:S(2)}, u32[]{:S(2)}) collective-permute-start(bf16[2,4,152,768]{3,2,1,0:T(8,128)(2,1)} %get-tuple-element.139.refs_4_), channel_id=1, source_target_pairs={{0,2},{1,3},{2,0},{3,1},{4,6},{5,7},{6,4},{7,5},{8,10},{9,11},{10,... | collective-permute-start | bytes 5603336 | tf_op jit(solution)/shard_map/ppermute | solution.py:78
  500.2 40.4 %collective-permute-start.41 = (bf16[2,2,4,32,3072]{4,3,2,1,0:T(8,128)(2,1)}, bf16[2,2,4,32,3072]{4,3,2,1,0:T(8,128)(2,1)}, u32[]{:S(2)}, u32[]{:S(2)}) collective-permute-start(bf16[2,2,4,32,3072]{4,3,2,1,0:T(8,128)(2,1)} %bitcast.274), channel_id=1, source_target_pairs={{0,1},{1,0},{2,3},{3,2},{4,5},{5,4},{6,7},{7,6},{8,9},{9,8},{10,11... | collective-permute-start | bytes 9437192 | tf_op jit(solution)/shard_map/ppermute | solution.py:73
  516.0 118.4 %reduce-scatter.7.cloned.1.call-start = ((), (), s32[]{:S(2)}) async-start(), calls=%async_computation.5 | async-start | bytes 1167360 | tf_op jit(solution)/shard_map/reduce_scatter | solution.py:227
  560.1 84.2 %reduce-scatter.5.cloned.1.call-start = ((), (), s32[]{:S(2)}) async-start(), calls=%async_computation.4 | async-start | bytes 1290240 | tf_op jit(solution)/shard_map/reduce_scatter | solution.py:227
  569.7 61.5 %collective-permute-start.52 = (bf16[2,4,32,3072]{3,2,1,0:T(8,128)(2,1)S(1)}, bf16[2,4,32,3072]{3,2,1,0:T(8,128)(2,1)}, u32[]{:S(2)}, u32[]{:S(2)}) collective-permute-start(bf16[2,4,32,3072]{3,2,1,0:T(8,128)(2,1)S(1)} %copy-done.2), channel_id=1, source_target_pairs={{0,2},{1,3},{2,0},{3,1},{4,6},{5,7},{6,4},{7,5},{8,10},{9,11},{10,... | collective-permute-start | bytes 4718600 | tf_op jit(solution)/shard_map/ppermute | solution.py:78
  (89 other events, 1511.5 us)
Sparse Core Ops, SparseCore 0:
  10.2 54.3 all-gather.12
  66.7 26.1 all-gather.10
  95.0 27.9 all-gather.14
  125.0 28.5 all-gather.8
  459.7 32.4 reduce-scatter.10
  516.1 35.1 reduce-scatter.8
  560.3 34.6 reduce-scatter.6
  597.3 25.8 reduce-scatter.4

commit v5 on v4

--- a/solution.py
+++ b/solution.py
@@ -1226,7 +1226,6 @@
     text_grad = after(t_first, t_co_sums.send) + dot_nt(t_co_grad, t_co[:, : 3 * CO_W])
     t_rest_sum.link()
     t_out_sum.link()
-    t_out_sum.came = after(t_out_sum.came, t_co_sums.send)
     t_rest_sum.column()
     t_out_sum.column()
     i_co_sums.link()

time: 682 us -> 711 us (1.043)
  waiting for transfers between devices: 165 us -> 195 us
    ppermute x16, waiting for transfers between devices: 73.4 us -> 101 us  [over_x(): return lax.ppermute(block, 'stream', [(d, d ^ 1) for d in range(total)])]
  transfers between devices with their start and end apart: 66 -> 66, of which waited for: 21 -> 23; matrix products, arithmetic and copies ran while one was open for 23% -> 21% of each run, Pallas kernels for 36% -> 34%
where the time goes in v5:
time: 711 us; the launch traced here: 703 us
  Pallas kernels  256 us (36%)
  waiting for transfers between devices  195 us (27%)
  other arithmetic  90 us (13%)
  starting transfers between devices  69.4 us (10%)
  local copies, waits for them, and re-layouts  46.6 us (7%)
  matrix products  30.4 us (4%)
  between operations  15.6 us (2%)
    pallas_call x20, Pallas kernels, call(): pl.pallas_call(body, in_specs=in_specs + [ANY] * len(deps), compiler_para...  256 us
    ppermute x16, waiting for transfers between devices, over_x(): return lax.ppermute(block, 'stream', [(d, d ^ 1) for d in range(total)])  101 us
    convert_element_type x18, other arithmetic, add_low(): return (kept.astype(F32) + came.astype(F32)).astype(BF)  59.7 us
    ppermute x12, waiting for transfers between devices, over_y(): return lax.ppermute(block, 'dp', [(d, d ^ 2) for d in range(total)])  52.2 us
    ppermute x12, waiting for transfers between devices, over_z(): lax.ppermute(block, 'dp', [(d, (d + 4 * shift) % total) for d in range(to...  39.2 us
    ppermute x12, starting transfers between devices, over_z(): lax.ppermute(block, 'dp', [(d, (d + 4 * shift) % total) for d in range(to...  30.5 us
    ppermute x16, starting transfers between devices, over_x(): return lax.ppermute(block, 'stream', [(d, d ^ 1) for d in range(total)])  19.4 us
    dot_general x2, matrix products, dot_nt(): lax.dot_general(a, b, (((1,), (1,)), ((), ())), preferred_element_type=F32)  16.8 us
  transfers between devices with their start and end apart: 66, of which 23 were waited for; matrix products, arithmetic and copies ran while one was open for 21% of the time, Pallas kernels for 34%

profile of v5, /device:TPU:0, one launch (start us, length us, event | category | flops | bytes accessed | tf_op | source)
XLA Modules:
  0.0 703.0 jit_solution(15657585647689212725)
XLA Ops:
  34.8 16.8 %collective-permute-done.1 = bf16[24,3200]{1,0:T(8,128)(2,1)S(1)} collective-permute-done((bf16[24,3200]{1,0:T(8,128)(2,1)S(1)}, bf16[24,3200]{1,0:T(8,128)(2,1)S(1)}, u32[]{:S(2)}, u32[]{:S(2)}) %collective-permute-start.1) | collective-permute-done | bytes 153632 | tf_op jit(solution)/shard_map/ppermute | solution.py:88
  69.0 17.1 %collective-permute-done.12 = bf16[4,32,3072]{2,1,0:T(8,128)(2,1)S(1)} collective-permute-done((bf16[4,32,3072]{2,1,0:T(8,128)(2,1)}, bf16[4,32,3072]{2,1,0:T(8,128)(2,1)S(1)}, u32[]{:S(2)}, u32[]{:S(2)}) %collective-permute-start.12) | collective-permute-done | bytes 786464 | tf_op jit(solution)/shard_map/ppermute | solution.py:83
  89.8 17.2 %collective-permute-done.4.refs_2_.refs_1_ = bf16[2,4,24,3200]{3,2,1,0:T(8,128)(2,1)S(1)} collective-permute-done((bf16[2,4,24,3200]{3,2,1,0:T(8,128)(2,1)S(1)}, bf16[2,4,24,3200]{3,2,1,0:T(8,128)(2,1)S(1)}, u32[]{:S(2)}, u32[]{:S(2)}) %collective-permute-start.4) | collective-permute-done | bytes 1228832 | tf_op jit(solution)/shard_map/ppermute | solution.py:83
  170.3 12.2 %collective-permute-done.17.refs_1_.refs_2_ = bf16[2,4,96,1024]{3,2,1,0:T(8,128)(2,1)} collective-permute-done((bf16[2,4,96,1024]{3,2,1,0:T(8,128)(2,1)}, bf16[2,4,96,1024]{3,2,1,0:T(8,128)(2,1)}, u32[]{:S(2)}, u32[]{:S(2)}) %collective-permute-start.17) | collective-permute-done | bytes 1572896 | tf_op jit(solution)/shard_map/ppermute | solution.py:83
  189.5 11.1 %shard_map.257 = (bf16[1024,1024]{1,0:T(8,128)(2,1)}, bf16[384,1024]{1,0:T(8,128)(2,1)}) custom-call(s32[8]{0:T(128)} %refs_0_.11, bf16[1024,3072]{1,0:T(8,128)(2,1)} %fusion.refs_1_, bf16[384,3072]{1,0:T(8,128)(2,1)} %add_convert_fusion.1.refs_2_), custom_call_target="tpu_custom_call" | custom-call | flops 12800000000 | bytes 8000000 | tf_op jit(solution)/shard_map/pallas_call | solution.py:51
  240.0 11.6 %shard_map.263 = (f32[384,1024]{1,0:T(8,128)}, f32[384,1]{1,0:T(8,128)}, bf16[384,1024]{1,0:T(8,128)(2,1)}, bf16[384,3072]{1,0:T(8,128)(2,1)}, bf16[384,1024]{1,...) custom-call(s32[8]{0:T(128)} %refs_0_.11, bf16[384,1024]{1,0:T(8,128)(2,1)} %get-tuple-element.75.refs_3_.refs_1_, ...), custom_call_target="tpu_custom_call" | custom-call | flops 12884901888 | bytes 40000000 | tf_op jit(solution)/shard_map/pallas_call | solution.py:51
  251.6 10.8 %shard_map.264 = (f32[384,1024]{1,0:T(8,128)}, bf16[384,1024]{1,0:T(8,128)(2,1)}, bf16[384,1024]{1,0:T(8,128)(2,1)}, bf16[384,1024]{1,0:T(8,128)(2,1)}, bf16[384...) custom-call(f32[384,1024]{1,0:T(8,128)} %get-tuple-element.76.refs_0_, ...), custom_call_target="tpu_custom_call" | custom-call | flops 5234491392 | bytes 40000000 | tf_op jit(solution)/shard_map/pallas_call | solution.py:51
  262.4 16.4 %shard_map.265 = (bf16[384,1024]{1,0:T(8,128)(2,1)}, bf16[384,3072]{1,0:T(8,128)(2,1)}, f32[384,1024]{1,0:T(8,128)}, bf16[384,1024]{1,0:T(8,128)(2,1)}, bf16[384,1024]{1,0:T(8,128)(2,1)}, /*index=5*/f32[8,1024]{1,0:T(8,128)}) custom-call(s32[8]{0:T(128)} %refs_0_.11, f32[384,1024]{1,0:T(8,128)} %get-tuple-element.78.refs_1_, ...), custom_call_target="tpu_custom_call" | custom-call | flops 12884901888 | bytes 40000000 | tf_op jit(solution)/shard_map/pallas_call | solution.py:51
  278.9 11.5 %shard_map.269 = (bf16[16,32,4096]{2,1,0:T(8,128)(2,1)}, bf16[16,32,4096]{2,1,0:T(8,128)(2,1)}) custom-call(s32[1]{0:T(128)} %bitcast.2.refs_0_, bf16[384,1024]{1,0:T(8,128)(2,1)} %get-tuple-element.83.refs_1_, bf16[384,1024]{1,0:T(8,128)(2,1)} %get-tuple-element.84.refs_2_, bf16[384,3072]{1,0:T(8,128)(2,1)} %get-tuple-element.85.refs_3_, ...), custom_call_target="tpu_custom_call" | custom-call | flops 4187593216 | bytes 20000000 | tf_op jit(solution)/shard_map/pallas_call | solution.py:51
  291.3 8.9 %shard_map.270 = (bf16[16,96,1024]{2,1,0:T(8,128)(2,1)}, bf16[16,96,1024]{2,1,0:T(8,128)(2,1)}) custom-call(s32[1]{0:T(128)} %bitcast.2.refs_0_, bf16[384,1024]{1,0:T(8,128)(2,1)} %get-tuple-element.75.refs_3_.refs_1_, bf16[384,1024]{1,0:T(8,128)(2,1)} %get-tuple-element.88.refs_2_, bf16[384,1024]{1,0:T(8,128)(2,1)} %get-tuple-element.89.refs_3_, ...), custom_call_target="tpu_custom_call" | custom-call | flops 3140694784 | bytes 20000000 | tf_op jit(solution)/shard_map/pallas_call | solution.py:51
  323.1 18.5 %shard_map.271 = (f32[1024,768]{1,0:T(8,128)}, f32[1024,1]{1,0:T(8,128)}, bf16[1024,768]{1,0:T(8,128)(2,1)}, bf16[1024,2304]{1,0:T(8,128)(2,1)}, bf16[1024,768]{...) custom-call(s32[8]{0:T(128)} %refs_0_.11, bf16[1024,1024]{1,0:T(8,128)(2,1)} %get-tuple-element.74.refs_1_, ...), custom_call_target="tpu_custom_call" | custom-call | flops 19327352832 | bytes 40000000 | tf_op jit(solution)/shard_map/pallas_call | solution.py:51
  354.9 33.6 %shard_map.272 = (f32[1024,768]{1,0:T(8,128)}, bf16[1024,768]{1,0:T(8,128)(2,1)}, bf16[1024,3072]{1,0:T(8,128)(2,1)}, bf16[1024,768]{1,0:T(8,128)(2,1)}, bf16[10...) custom-call(f32[1024,768]{1,0:T(8,128)} %get-tuple-element.95.refs_0_, ...), custom_call_target="tpu_custom_call" | custom-call | flops 31406948352 | bytes 40000000 | tf_op jit(solution)/shard_map/pallas_call | solution.py:51
  391.1 26.4 %shard_map.274 = (bf16[1024,768]{1,0:T(8,128)(2,1)}, bf16[1024,2304]{1,0:T(8,128)(2,1)}, f32[1024,768]{1,0:T(8,128)}, bf16[1024,768]{1,0:T(8,128)(2,1)}, bf16[1024,1024]{1,0:T(8,128)(2,1)}, /*index=5*/f32[8,768]{1,0:T(8,128)}) custom-call(s32[8]{0:T(128)} %refs_0_.11, f32[1024,768]{1,0:T(8,128)} %get-tuple-element.100.refs_1_, ...), custom_call_target="tpu_custom_call" | custom-call | flops 19327352832 | bytes 40000000 | tf_op jit(solution)/shard_map/pallas_call | solution.py:51
  423.8 16.6 %shard_map.277 = (bf16[16,24,5376]{2,1,0:T(8,128)(2,1)}, bf16[16,24,5376]{2,1,0:T(8,128)(2,1)}) custom-call(s32[1]{0:T(128)} %bitcast.2.refs_0_, bf16[1024,768]{1,0:T(8,128)(2,1)} %get-tuple-element.112.refs_1_, bf16[1024,768]{1,0:T(8,128)(2,1)} %get-tuple-element.113.refs_2_, bf16[1024,2304]{1,0:T(8,128)(2,1)} %get-tuple-element.114.refs_3_, ...), custom_call_target="tpu_custom_call" | custom-call | flops 10992432128 | bytes 20000000 | tf_op jit(solution)/shard_map/pallas_call | solution.py:51
  440.5 18.0 %shard_map.278 = (bf16[16,152,768]{2,1,0:T(8,128)(2,1)}, bf16[16,152,768]{2,1,0:T(8,128)(2,1)}) custom-call(s32[1]{0:T(128)} %bitcast.2.refs_0_, bf16[1024,1024]{1,0:T(8,128)(2,1)} %get-tuple-element.74.refs_1_, bf16[1024,768]{1,0:T(8,128)(2,1)} %get-tuple-element.107.refs_2_, bf16[1024,3072]{1,0:T(8,128)(2,1)} %get-tuple-element.108.refs_3_, ...), custom_call_target="tpu_custom_call" | custom-call | flops 9945533440 | bytes 20000000 | tf_op jit(solution)/shard_map/pallas_call | solution.py:51
  461.9 22.4 %collective-permute-done.57.refs_0_ = bf16[4,32,4096]{2,1,0:T(8,128)(2,1)S(1)} collective-permute-done((bf16[4,32,4096]{2,1,0:T(8,128)(2,1)}, bf16[4,32,4096]{2,1,0:T(8,128)(2,1)S(1)}, u32[]{:S(2)}, u32[]{:S(2)}) %collective-permute-start.57) | collective-permute-done | bytes 1048608 | tf_op jit(solution)/shard_map/ppermute | solution.py:83
  503.3 14.7 %shard_map.279 = (bf16[1024,3072]{1,0:T(8,128)(2,1)}, bf16[384,3072]{1,0:T(8,128)(2,1)}, f32[1,3072]{1,0:T(1,128)}, f32[1,3072]{1,0:T(1,128)}) custom-call(s32[8]{0:T(128)} %refs_0_.11, bf16[1024,3072]{1,0:T(8,128)(2,1)} %fusion.refs_1_, bf16[384,3072]{1,0:T(8,128)(2,1)} %add_convert_fusion.1.refs_2_, bf16[1024,1024]{1,0:T(8,128)(2,1)} %get-tuple-element.105.refs_1_.refs_3_, ...), custom_call_target="tpu_custom_call" | custom-call | flops 16000000000 | bytes 20000000 | tf_op jit(solution)/shard_map/pallas_call | solution.py:51
  520.0 8.7 %shard_map.281 = (bf16[16,32,3072]{2,1,0:T(8,128)(2,1)}, bf16[16,32,3072]{2,1,0:T(8,128)(2,1)}) custom-call(s32[1]{0:T(128)} %bitcast.2.refs_0_, bf16[384,1024]{1,0:T(8,128)(2,1)} %bitcast.243, bf16[384,3072]{1,0:T(8,128)(2,1)} %get-tuple-element.128.refs_2_, bf16[2,4,24,5376]{3,2,1,0:T(8,128)(2,1)} %get-tuple-element.137.refs_6_.refs_1_.refs_3_, ...), custom_call_target="tpu_custom_call" | custom-call | flops 3140694784 | bytes 20000000 | tf_op jit(solution)/shard_map/pallas_call | solution.py:51
  529.8 10.8 %shard_map.282 = (bf16[16,24,3200]{2,1,0:T(8,128)(2,1)}, bf16[16,24,3200]{2,1,0:T(8,128)(2,1)}) custom-call(s32[1]{0:T(128)} %bitcast.2.refs_0_, bf16[1024,768]{1,0:T(8,128)(2,1)} %refs_1_.1, bf16[1024,3072]{1,0:T(8,128)(2,1)} %get-tuple-element.119.refs_2_, f32[768,128]{1,0:T(8,128)} %reshape.414.refs_3_, bf16[2,2,4,32,3072]{4,3,2,1,0:T(8,128)(2,1)} %bitcast.233), custom_call_target="tpu_custom_call" | custom-call | flops 6543114240 | bytes 20000000 | tf_op jit(solution)/shard_map/pallas_call | solution.py:51
  541.0 19.1 %collective-permute-done.50 = bf16[2,4,152,768]{3,2,1,0:T(8,128)(2,1)} collective-permute-done((bf16[2,4,152,768]{3,2,1,0:T(8,128)(2,1)}, bf16[2,4,152,768]{3,2,1,0:T(8,128)(2,1)}, u32[]{:S(2)}, u32[]{:S(2)}) %collective-permute-start.50) | collective-permute-done | bytes 1867808 | tf_op jit(solution)/shard_map/ppermute | solution.py:78
  572.7 10.1 %collective-permute-done.51 = bf16[4,152,768]{2,1,0:T(8,128)(2,1)} collective-permute-done((bf16[4,152,768]{2,1,0:T(8,128)(2,1)S(1)}, bf16[4,152,768]{2,1,0:T(8,128)(2,1)}, u32[]{:S(2)}, u32[]{:S(2)}) %collective-permute-start.51) | collective-permute-done | bytes 933920 | tf_op jit(solution)/shard_map/ppermute | solution.py:83
  611.3 16.0 %collective-permute-done.43 = bf16[2,4,24,3200]{3,2,1,0:T(8,128)(2,1)} collective-permute-done((bf16[2,4,24,3200]{3,2,1,0:T(8,128)(2,1)S(1)}, bf16[2,4,24,3200]{3,2,1,0:T(8,128)(2,1)}, u32[]{:S(2)}, u32[]{:S(2)}) %collective-permute-start.43) | collective-permute-done | bytes 1228832 | tf_op jit(solution)/shard_map/ppermute | solution.py:83
  631.0 10.2 %fusion.59 = f32[1024,768]{1,0:T(8,128)} fusion(f32[1024,768]{1,0:T(8,128)} %shard_map.284, bf16[1024,3072]{1,0:T(8,128)(2,1)} %get-tuple-element.119.refs_2_, bf16[768,3200]{1,0:T(8,128)(2,1)} %bitcast.222), kind=kOutput, calls=%fused_computation.127 | convolution fusion | flops 4832624640 | bytes 17301504 | tf_op jit(solution)/shard_map/dot_general | solution.py:34
  649.8 10.0 %collective-permute-start.45 = (bf16[24,3200]{1,0:T(8,128)(2,1)S(1)}, bf16[24,3200]{1,0:T(8,128)(2,1)S(1)}, u32[]{:S(2)}, u32[]{:S(2)}) collective-permute-start(bf16[24,3200]{1,0:T(8,128)(2,1)S(1)} %get-tuple-element.149), channel_id=1, source_target_pairs={{0,4},{1,5},{2,6},{3,7},{4,8},{5,9},{6,10},{7,11},{8,12},{9,13},{1... | collective-permute-start | bytes 460808 | tf_op jit(solution)/shard_map/ppermute | solution.py:88
  (382 shorter events, 318.7 us)
Async XLA Ops:
  7.2 99.8 %all-gather.13.cloned.1.call-start = ((), (), s32[]{:S(2)}) async-start(), calls=%async_computation.10 | async-start | bytes 1310720 | tf_op jit(solution)/shard_map/all_gather | solution.py:169
  9.0 110.1 %all-gather.11.cloned.1.call-start = ((), (), s32[]{:S(2)}) async-start(), calls=%async_computation.9 | async-start | bytes 1310720 | tf_op jit(solution)/shard_map/all_gather | solution.py:169
  26.4 96.7 %all-gather.15.cloned.1.call-start = ((), (), s32[]{:S(2)}) async-start(), calls=%async_computation.11 | async-start | bytes 1351680 | tf_op jit(solution)/shard_map/all_gather | solution.py:169
  89.6 112.5 %all-gather.9.cloned.1.call-start = ((), (), s32[]{:S(2)}) async-start(), calls=%async_computation.8 | async-start | bytes 1320960 | tf_op jit(solution)/shard_map/all_gather | solution.py:169
  115.5 449.2 %reduce-scatter.11.cloned.1.call-start = ((), (), s32[]{:S(2)}) async-start(), calls=%async_computation.7 | async-start | bytes 983040 | tf_op jit(solution)/shard_map/reduce_scatter | solution.py:227
  136.6 52.9 %collective-permute-start.19 = (bf16[2,4,32,4096]{3,2,1,0:T(8,128)(2,1)}, bf16[2,4,32,4096]{3,2,1,0:T(8,128)(2,1)S(1)}, u32[]{:S(2)}, u32[]{:S(2)}) collective-permute-start(bf16[2,4,32,4096]{3,2,1,0:T(8,128)(2,1)} %pad_maximum_fusion.refs_1_), channel_id=1, source_target_pairs={{0,2},{1,3},{2,0},{3,1},{4,6},{5,7},{6,4},{7,5},{8,10},{9,11},{10,... | collective-permute-start | bytes 6291464 | tf_op jit(solution)/shard_map/ppermute | solution.py:78
  156.9 47.5 %collective-permute-start.26 = (bf16[2,4,96,1024]{3,2,1,0:T(8,128)(2,1)}, bf16[2,4,96,1024]{3,2,1,0:T(8,128)(2,1)}, u32[]{:S(2)}, u32[]{:S(2)}) collective-permute-start(bf16[2,4,96,1024]{3,2,1,0:T(8,128)(2,1)} %pad_maximum_fusion.4.refs_1_), channel_id=1, source_target_pairs={{0,1},{1,0},{2,3},{3,2},{4,5},{5,4},{6,7},{7,6},{8,9},{9,8},{10,11... | collective-permute-start | bytes 4718600 | tf_op jit(solution)/shard_map/ppermute | solution.py:73
  156.9 75.9 %collective-permute-start.24 = (bf16[2,4,32,4096]{3,2,1,0:T(8,128)(2,1)}, bf16[2,4,32,4096]{3,2,1,0:T(8,128)(2,1)}, u32[]{:S(2)}, u32[]{:S(2)}) collective-permute-start(bf16[2,4,32,4096]{3,2,1,0:T(8,128)(2,1)} %pad_maximum_fusion.refs_1_), channel_id=1, source_target_pairs={{0,1},{1,0},{2,3},{3,2},{4,5},{5,4},{6,7},{7,6},{8,9},{9,8},{10,11... | collective-permute-start | bytes 6291464 | tf_op jit(solution)/shard_map/ppermute | solution.py:73
  189.5 43.4 %collective-permute-start.25 = (bf16[2,4,32,4096]{3,2,1,0:T(8,128)(2,1)S(1)}, bf16[2,4,32,4096]{3,2,1,0:T(8,128)(2,1)}, u32[]{:S(2)}, u32[]{:S(2)}) collective-permute-start(bf16[2,4,32,4096]{3,2,1,0:T(8,128)(2,1)S(1)} %collective-permute-done.19.refs_2_), channel_id=1, source_target_pairs={{0,1},{1,0},{2,3},{3,2},{4,5},{5,4},{6,7},{7,6},{8,9},{9,8},{10,11... | collective-permute-start | bytes 6291464 | tf_op jit(solution)/shard_map/ppermute | solution.py:73
  226.0 52.9 %collective-permute-start.29 = (bf16[2,4,152,768]{3,2,1,0:T(8,128)(2,1)}, bf16[2,4,152,768]{3,2,1,0:T(8,128)(2,1)}, u32[]{:S(2)}, u32[]{:S(2)}) collective-permute-start(bf16[2,4,152,768]{3,2,1,0:T(8,128)(2,1)} %pad_maximum_fusion.2.refs_1_), channel_id=1, source_target_pairs={{0,16},{16,0},{1,17},{17,1},{2,18},{18,2},{3,19},{19,3},{4,20},{20... | collective-permute-start | bytes 5603336 | tf_op jit(solution)/shard_map/ppermute | solution.py:83
  227.4 72.8 %collective-permute-start.30 = (bf16[2,4,152,768]{3,2,1,0:T(8,128)(2,1)}, bf16[2,4,152,768]{3,2,1,0:T(8,128)(2,1)}, u32[]{:S(2)}, u32[]{:S(2)}) collective-permute-start(bf16[2,4,152,768]{3,2,1,0:T(8,128)(2,1)} %pad_maximum_fusion.2.refs_1_), channel_id=1, source_target_pairs={{0,1},{1,0},{2,3},{3,2},{4,5},{5,4},{6,7},{7,6},{8,9},{9,8},{10,11... | collective-permute-start | bytes 5603336 | tf_op jit(solution)/shard_map/ppermute | solution.py:73
  232.8 58.1 %collective-permute-start.21 = (bf16[2,4,24,5376]{3,2,1,0:T(8,128)(2,1)}, bf16[2,4,24,5376]{3,2,1,0:T(8,128)(2,1)}, u32[]{:S(2)}, u32[]{:S(2)}) collective-permute-start(bf16[2,4,24,5376]{3,2,1,0:T(8,128)(2,1)} %pad_maximum_fusion.1.refs_1_), channel_id=1, source_target_pairs={{0,2},{1,3},{2,0},{3,1},{4,6},{5,7},{6,4},{7,5},{8,10},{9,11},{10,... | collective-permute-start | bytes 6193160 | tf_op jit(solution)/shard_map/ppermute | solution.py:78
  290.4 57.1 %collective-permute-start.33 = (bf16[2,2,4,32,4096]{4,3,2,1,0:T(8,128)(2,1)}, bf16[2,2,4,32,4096]{4,3,2,1,0:T(8,128)(2,1)}, u32[]{:S(2)}, u32[]{:S(2)}) collective-permute-start(bf16[2,2,4,32,4096]{4,3,2,1,0:T(8,128)(2,1)} %bitcast.270), channel_id=1, source_target_pairs={{0,1},{1,0},{2,3},{3,2},{4,5},{5,4},{6,7},{7,6},{8,9},{9,8},{10,11... | collective-permute-start | bytes 12582920 | tf_op jit(solution)/shard_map/ppermute | solution.py:73
  346.9 41.5 %collective-permute-start.35 = (bf16[2,4,96,1024]{3,2,1,0:T(8,128)(2,1)}, bf16[2,4,96,1024]{3,2,1,0:T(8,128)(2,1)}, u32[]{:S(2)}, u32[]{:S(2)}) collective-permute-start(bf16[2,4,96,1024]{3,2,1,0:T(8,128)(2,1)} %get-tuple-element.143.refs_9_), channel_id=1, source_target_pairs={{0,16},{16,0},{1,17},{17,1},{2,18},{18,2},{3,19},{19,3},{4,20},{20... | collective-permute-start | bytes 4718600 | tf_op jit(solution)/shard_map/ppermute | solution.py:83
  352.8 68.6 %collective-permute-start.36 = (bf16[2,4,32,4096]{3,2,1,0:T(8,128)(2,1)}, bf16[2,4,32,4096]{3,2,1,0:T(8,128)(2,1)}, u32[]{:S(2)}, u32[]{:S(2)}) collective-permute-start(bf16[2,4,32,4096]{3,2,1,0:T(8,128)(2,1)} %get-tuple-element.135.refs_8_), channel_id=1, source_target_pairs={{0,2},{1,3},{2,0},{3,1},{4,6},{5,7},{6,4},{7,5},{8,10},{9,11},{10,... | collective-permute-start | bytes 6291464 | tf_op jit(solution)/shard_map/ppermute | solution.py:78
  440.4 48.2 %collective-permute-start.38 = (bf16[2,2,4,24,5376]{4,3,2,1,0:T(8,128)(2,1)}, bf16[2,2,4,24,5376]{4,3,2,1,0:T(8,128)(2,1)}, u32[]{:S(2)}, u32[]{:S(2)}) collective-permute-start(bf16[2,2,4,24,5376]{4,3,2,1,0:T(8,128)(2,1)} %bitcast.271), channel_id=1, source_target_pairs={{0,1},{1,0},{2,3},{3,2},{4,5},{5,4},{6,7},{7,6},{8,9},{9,8},{10,11... | collective-permute-start | bytes 12386312 | tf_op jit(solution)/shard_map/ppermute | solution.py:73
  460.6 105.8 %reduce-scatter.9.cloned.1.call-start = ((), (), s32[]{:S(2)}) async-start(), calls=%async_computation.6 | async-start | bytes 1310720 | tf_op jit(solution)/shard_map/reduce_scatter | solution.py:227
  488.4 154.1 %reduce-scatter.7.cloned.1.call-start = ((), (), s32[]{:S(2)}) async-start(), calls=%async_computation.5 | async-start | bytes 1167360 | tf_op jit(solution)/shard_map/reduce_scatter | solution.py:227
  495.0 73.3 %collective-permute-start.48 = (bf16[2,4,24,5376]{3,2,1,0:T(8,128)(2,1)}, bf16[2,4,24,5376]{3,2,1,0:T(8,128)(2,1)}, u32[]{:S(2)}, u32[]{:S(2)}) collective-permute-start(bf16[2,4,24,5376]{3,2,1,0:T(8,128)(2,1)} %get-tuple-element.137.refs_6_.refs_1_.refs_3_), channel_id=1, source_target_pairs={{0,16},{16,0},{1,17},{17,1},{2,18},{18,2},{3,19},{19,3},{4,20},{20... | collective-permute-start | bytes 6193160 | tf_op jit(solution)/shard_map/ppermute | solution.py:83
  518.0 42.1 %collective-permute-start.50 = (bf16[2,4,152,768]{3,2,1,0:T(8,128)(2,1)}, bf16[2,4,152,768]{3,2,1,0:T(8,128)(2,1)}, u32[]{:S(2)}, u32[]{:S(2)}) collective-permute-start(bf16[2,4,152,768]{3,2,1,0:T(8,128)(2,1)} %get-tuple-element.139.refs_4_), channel_id=1, source_target_pairs={{0,2},{1,3},{2,0},{3,1},{4,6},{5,7},{6,4},{7,5},{8,10},{9,11},{10,... | collective-permute-start | bytes 5603336 | tf_op jit(solution)/shard_map/ppermute | solution.py:78
  528.6 57.3 %collective-permute-start.41 = (bf16[2,2,4,32,3072]{4,3,2,1,0:T(8,128)(2,1)}, bf16[2,2,4,32,3072]{4,3,2,1,0:T(8,128)(2,1)}, u32[]{:S(2)}, u32[]{:S(2)}) collective-permute-start(bf16[2,2,4,32,3072]{4,3,2,1,0:T(8,128)(2,1)} %bitcast.273), channel_id=1, source_target_pairs={{0,1},{1,0},{2,3},{3,2},{4,5},{5,4},{6,7},{7,6},{8,9},{9,8},{10,11... | collective-permute-start | bytes 9437192 | tf_op jit(solution)/shard_map/ppermute | solution.py:73
  540.6 51.1 %collective-permute-start.40 = (bf16[2,2,4,24,3200]{4,3,2,1,0:T(8,128)(2,1)}, bf16[2,2,4,24,3200]{4,3,2,1,0:T(8,128)(2,1)S(1)}, u32[]{:S(2)}, u32[]{:S(2)}) collective-permute-start(bf16[2,2,4,24,3200]{4,3,2,1,0:T(8,128)(2,1)} %bitcast.275), channel_id=1, source_target_pairs={{0,1},{1,0},{2,3},{3,2},{4,5},{5,4},{6,7},{7,6},{8,9},{9,8},{10,11... | collective-permute-start | bytes 7372808 | tf_op jit(solution)/shard_map/ppermute | solution.py:73
  585.7 88.6 %reduce-scatter.5.cloned.1.call-start = ((), (), s32[]{:S(2)}) async-start(), calls=%async_computation.4 | async-start | bytes 1290240 | tf_op jit(solution)/shard_map/reduce_scatter | solution.py:227
  601.1 61.2 %collective-permute-start.52 = (bf16[2,4,32,3072]{3,2,1,0:T(8,128)(2,1)S(1)}, bf16[2,4,32,3072]{3,2,1,0:T(8,128)(2,1)}, u32[]{:S(2)}, u32[]{:S(2)}) collective-permute-start(bf16[2,4,32,3072]{3,2,1,0:T(8,128)(2,1)S(1)} %copy-done.2), channel_id=1, source_target_pairs={{0,2},{1,3},{2,0},{3,1},{4,6},{5,7},{6,4},{7,5},{8,10},{9,11},{10,... | collective-permute-start | bytes 4718600 | tf_op jit(solution)/shard_map/ppermute | solution.py:78
  (86 other events, 1458.4 us)
Sparse Core Ops, SparseCore 0:
  10.2 54.3 all-gather.12
  66.7 26.1 all-gather.10
  95.0 27.9 all-gather.14
  125.0 28.5 all-gather.8
  460.7 32.5 reduce-scatter.10
  496.0 29.0 reduce-scatter.8
  585.8 34.2 reduce-scatter.6
  622.4 25.8 reduce-scatter.4
